TPU v7x, 256 devices: a whole 4x4x8 slice. The times are simulated.
256 devices in a mesh: seq: 8 (over z), ctx: 32 (over y, x, core).
Axes of the slice: x: 4, y: 4, z: 8, core: 2. Of those that a mesh axis runs over, the one named last changes fastest.
Arguments:
- inputs: bfloat16 [65536, 2048], P(('seq', 'ctx')), parts along dimension 0, may hold values from -0.19921875 to 0.19921875
- write_keys: bfloat16 [65536, 128], P(('seq', 'ctx')), parts along dimension 0, may hold values from -0.5 to 0.5
- read_queries: bfloat16 [65536, 128], P(('seq', 'ctx')), parts along dimension 0, may hold values from -6 to 6
- decay_log: float32 [32, 65536], P(None, ('seq', 'ctx')), parts along dimension 1, may hold values from -1 to 0
- level_mix: float32 [6, 32, 65536], P(None, None, ('seq', 'ctx')), parts along dimension 2, may hold values from 0.25 to 1.5
Outputs:
- outputs: bfloat16 [65536, 2048], P(('seq', 'ctx')), parts along dimension 0
There are 8 independent parts, one for each index of `seq`. A program takes and returns all parts, laid end to end along the dimension named above; each array names one. Nothing has to cross between parts.
All inputs are finite; a program needn't handle non-finite values.
Results may differ from a plain program's by a relative error of at most 0.0062.
Values may be sent and summed in bfloat16 or wider, within the bound.
No kernel may reach another device: no remote copies, remote signals or barrier semaphores. Data moves between devices by JAX's collectives and lax.ppermute only.
A program may use at most 128 MiB of HBM per device.

v0:
```python
import jax
import jax.numpy as jnp
from jax import lax
from jax.sharding import PartitionSpec as P

HEAD = 64
SUB = 256
LEVELS = 5


def level_mask(reader, source, level):
    reader_bit = reader >> level & 1
    source_bit = source >> level & 1
    same_high = reader >> level + 1 == source >> level + 1
    return (reader_bit == 1) & (source_bit == 0) & same_high


def local_block(x_block, key_block, query_block, decay_block):
    length = x_block.shape[0]
    head_count = x_block.shape[1]
    pieces = length // SUB
    cum_all = jnp.cumsum(decay_block.reshape(head_count, pieces, SUB), axis=2).reshape(
        head_count, length
    )
    causal = jnp.arange(SUB)[:, None] >= jnp.arange(SUB)[None, :]
    state = jnp.zeros((head_count, key_block.shape[1], HEAD), jnp.float32)
    scores = jnp.dot(query_block, key_block.T, preferred_element_type=jnp.float32)
    gap = cum_all[:, :, None] - cum_all[:, None, :]
    mixing = jnp.where(causal[None], scores[None] * jnp.exp(jnp.where(causal[None], gap, 0.0)), 0.0)
    mixing = mixing.astype(jnp.bfloat16)
    diagonal = jnp.einsum("hts,shp->thp", mixing, x_block, preferred_element_type=jnp.float32)
    rounded = state.astype(jnp.bfloat16)
    carried = jnp.einsum("tn,hnp->thp", query_block, rounded, preferred_element_type=jnp.float32)
    local_list = diagonal + jnp.exp(cum_all).T[:, :, None] * carried
    factor = jnp.exp(cum_all[:, -1:] - cum_all)
    decayed = (x_block * factor.T[:, :, None]).astype(jnp.bfloat16)
    update = jnp.einsum("sn,shp->hnp", key_block, decayed, preferred_element_type=jnp.float32)
    state = jnp.exp(cum_all[:, -1])[:, None, None] * state + update
    offset = cum_all[:, -1]
    return (local_list, state, offset, cum_all)


def body(inputs, write_keys, read_queries, decay_log, level_mix):
    length = inputs.shape[0]
    head_count = decay_log.shape[0]
    x_block = inputs.reshape(length, head_count, HEAD)
    local, state, offset, within = local_block(x_block, write_keys, read_queries, decay_log)
    state_rows = state.shape[1]
    ends_rounded = state.astype(jnp.bfloat16)
    device_index = lax.axis_index("ctx")
    totals_all = lax.all_gather(offset[None], "ctx", axis=0, tiled=True)
    inclusive = jnp.cumsum(totals_all, axis=0)
    exclusive = inclusive - totals_all
    gap_row = lax.dynamic_index_in_dim(exclusive, device_index, 0, keepdims=False)
    level_numbers = jnp.arange(LEVELS, dtype=jnp.int32)[:, None]
    flat_ends = ends_rounded.reshape(1, head_count, state_rows * HEAD)
    piece = lax.all_gather(flat_ends, "ctx", axis=0, tiled=True)
    width = piece.shape[0]
    sources = jnp.arange(width, dtype=jnp.int32)
    chosen = level_mask(device_index, sources[None, :], level_numbers)[:, :, None]
    gap = gap_row[None, :] - inclusive
    weights = jnp.where(chosen, jnp.exp(jnp.where(chosen, gap[None], 0.0)), 0.0)
    shaped = piece.reshape(width, head_count, state_rows, HEAD).astype(jnp.float32)
    levels = jnp.einsum("lkh,khnp->lhnp", weights, shaped, precision=lax.Precision.HIGHEST)
    total = level_mix[0].T[:, :, None] * local
    scale = jnp.exp(within).T
    for level in range(LEVELS):
        rounded = levels[level].astype(jnp.bfloat16)
        weight = level_mix[level + 1].T * scale

        def add_level(running, rounded=rounded, weight=weight):
            product = jnp.einsum(
                "tn,hnp->thp", read_queries, rounded, preferred_element_type=jnp.float32
            )
            return running + weight[:, :, None] * product

        total = lax.cond(device_index >> level & 1 == 1, add_level, lambda running: running, total)
    return total.astype(jnp.bfloat16).reshape(length, head_count * HEAD)


def solution(mesh):
    placed = (
        P(("seq", "ctx"), None),
        P(("seq", "ctx"), None),
        P(("seq", "ctx"), None),
        P(None, ("seq", "ctx")),
        P(None, None, ("seq", "ctx")),
    )
    return jax.shard_map(
        body, mesh=mesh, in_specs=placed, out_specs=P(("seq", "ctx"), None), check_vma=False
    )
```

profile of v0, /device:TPU:31, one launch (start us, length us, event | category | flops | bytes accessed | tf_op | source)
XLA Modules:
  0.0 214.9 jit_solution(6692103116416637831)
XLA Ops:
  6.5 0.8 reshape.193
  7.4 0.6 reduce-window.6
  8.7 1.5 copy.35
  10.2 0.4 fusion.9
  10.7 0.5 copy.36
  11.2 1.6 reshape.199
  12.8 0.6 dynamic-slice
  14.3 63.0 %all-reduce = f32[1024]{0:T(1024)S(1)} all-reduce(f32[1024]{0:T(1024)S(1)} %dynamic-update-slice), channel_id=2, replica_groups=mesh['seq'=8,'ctx'=32] {'ctx'}, use_global_device_ids=true, to_apply=%add | all-reduce | flops 1024 | bytes 8192
  77.9 0.4 fusion.11
  78.4 2.3 %fusion.7 = f32[256,32,64]{0,2,1:T(8,128)S(1)} fusion(f32[32,64,256]{2,1,0:T(8,128)S(1)} %fusion.11, bf16[256,32,64]{0,2,1:T(8,128)(2,1)S(1)} %bitcast.127, f32[32,256]{1,0:T(8,128)S(1)} %get-tuple-element.185, f32[256,256]{1,0:T(8,128)S(1)} %fusion.33, pred[256,256]{1,0:T(8,128)(4,1)S(1)} %iota_compare_fusion, f32[256,32]{0,1:T(8,128)S(1)} %get-tuple-element.184, ...), kind=kOutput, calls=%fused_computation.15 | convolution fusion | flops 280494080 | bytes 5668864 | tf_op jit(solution)/shard_map/hts,shp->thp/dot_general | solution.py:31
  80.6 11.0 %all-gather.3.cloned.1.call-done = bf16[32,32,8192]{2,1,0:T(8,128)(2,1)} async-done(((bf16[1,32,8192]{2,1,0:T(8,128)(2,1)}), bf16[32,32,8192]{2,1,0:T(8,128)(2,1)}) %all-gather.3.cloned.1.call-update) | async-done | bytes 16777232 | tf_op jit(solution)/shard_map/all_gather | solution.py:57
  91.7 46.0 %reshape.200 = bf16[32,32,128,64]{3,2,1,0:T(8,128)(2,1)} reshape(bf16[32,32,8192]{2,1,0:T(8,128)(2,1)} %all-gather.3.cloned.1.call-done) | data formatting | bytes 33554432 | tf_op jit(solution)/shard_map/reshape | solution.py:63
  137.7 36.3 %copy.38 = bf16[32,32,128,64]{2,0,3,1:T(8,128)(2,1)} copy(bf16[32,32,128,64]{3,2,1,0:T(8,128)(2,1)} %reshape.200) | data formatting | bytes 33554432 | tf_op jit(solution)/shard_map/reshape | solution.py:63
  174.0 11.5 %convert_bitcast_fusion = bf16[5,32,128,64]{2,0,3,1:T(8,128)(2,1)} fusion(bf16[32,32,128,64]{2,0,3,1:T(8,128)(2,1)} %copy.38, f32[32,32]{0,1:T(8,128)S(1)} %copy.37, pred[5,32]{1,0:T(8,128)(4,1)S(1)} %fusion.23), kind=kOutput, calls=%fused_computation.7 | convolution fusion | flops 504637440 | bytes 19402912 | tf_op jit(solution)/shard_map/lkh,khnp->lhnp/dot_general | solution.py:64
  185.4 4.0 %conditional.5 = (f32[256,32,64]{0,2,1:T(8,128)S(1)}) conditional(s32[]{:T(128)} %convert_element_type.64, f32[256,32,64]{0,2,1:T(8,128)S(1)} %fusion.7, (f32[256,32]{0,1:T(8,128)S(1)}, bf16[256,128]{1,0:T(8,128)(2,1)S(1)}, bf16[5,32,128,64]{2,0,3,1:T(8,128)(2,1)}, f32[256,32,64]{0,2,1:T(8,128)S(1)}, f32[256,32]{0,1:T(8,128)S(1)}) %tuple.80), branch_computations={%region_3.4_spmd, %region_4.5_spmd} | conditional | flops 135274496 | bytes 15400968 | solution.py:77
  185.4 2.9 %copy.39 = bf16[5,32,128,64]{2,3,1,0:T(8,128)(2,1)S(1)} copy(bf16[5,32,128,64]{2,0,3,1:T(8,128)(2,1)} %get-tuple-element.160) | data formatting | bytes 5242880 | tf_op jit(solution)/shard_map
  188.8 0.6 multiply_add_fusion
  189.5 4.1 %conditional.6 = (f32[256,32,64]{0,2,1:T(8,128)S(1)}) conditional(s32[]{:T(128)} %convert_element_type.63, f32[256,32,64]{0,2,1:T(8,128)S(1)} %get-tuple-element.196, (f32[256,32]{0,1:T(8,128)S(1)}, bf16[256,128]{1,0:T(8,128)(2,1)S(1)}, bf16[5,32,128,64]{2,0,3,1:T(8,128)(2,1)}, f32[256,32,64]{0,2,1:T(8,128)S(1)}, f32[256,32]{0,1:T(8,128)S(1)}) %tuple.81), branch_computations={%region_5.6_spmd, %region_6.7_spmd} | conditional | flops 135274496 | bytes 15400968 | solution.py:77
  189.5 2.9 %copy.40 = bf16[5,32,128,64]{2,3,1,0:T(8,128)(2,1)S(1)} copy(bf16[5,32,128,64]{2,0,3,1:T(8,128)(2,1)} %get-tuple-element.165) | data formatting | bytes 5242880 | tf_op jit(solution)/shard_map
  192.9 0.6 multiply_add_fusion.1
  193.5 4.1 %conditional.7 = (f32[256,32,64]{0,2,1:T(8,128)S(1)}) conditional(s32[]{:T(128)} %convert_element_type.62, f32[256,32,64]{0,2,1:T(8,128)S(1)} %get-tuple-element.197, (f32[256,32]{0,1:T(8,128)S(1)}, bf16[256,128]{1,0:T(8,128)(2,1)S(1)}, bf16[5,32,128,64]{2,0,3,1:T(8,128)(2,1)}, f32[256,32,64]{0,2,1:T(8,128)S(1)}, f32[256,32]{0,1:T(8,128)S(1)}) %tuple.82), branch_computations={%region_7.8_spmd, %region_8.9_spmd} | conditional | flops 135274496 | bytes 15400968 | solution.py:77
  193.6 2.9 %copy.41 = bf16[5,32,128,64]{2,3,1,0:T(8,128)(2,1)S(1)} copy(bf16[5,32,128,64]{2,0,3,1:T(8,128)(2,1)} %get-tuple-element.170) | data formatting | bytes 5242880 | tf_op jit(solution)/shard_map
  197.0 0.6 multiply_add_fusion.2
  197.6 4.1 %conditional.8 = (f32[256,32,64]{0,2,1:T(8,128)S(1)}) conditional(s32[]{:T(128)} %convert_element_type.61, f32[256,32,64]{0,2,1:T(8,128)S(1)} %get-tuple-element.198, (f32[256,32]{0,1:T(8,128)S(1)}, bf16[256,128]{1,0:T(8,128)(2,1)S(1)}, bf16[5,32,128,64]{2,0,3,1:T(8,128)(2,1)}, f32[256,32,64]{0,2,1:T(8,128)S(1)}, f32[256,32]{0,1:T(8,128)S(1)}) %tuple.83), branch_computations={%region_9.10_spmd, %region_10.11_spmd} | conditional | flops 135274496 | bytes 15400968 | solution.py:77
  197.6 2.9 %copy.42 = bf16[5,32,128,64]{2,3,1,0:T(8,128)(2,1)S(1)} copy(bf16[5,32,128,64]{2,0,3,1:T(8,128)(2,1)} %get-tuple-element.175) | data formatting | bytes 5242880 | tf_op jit(solution)/shard_map
  201.0 0.6 multiply_add_fusion.3
  201.7 4.6 %conditional.9 = (bf16[256,2048]{1,0:T(8,128)(2,1)S(1)}) conditional(s32[]{:T(128)} %convert_element_type.60, f32[256,32,64]{0,2,1:T(8,128)S(1)} %get-tuple-element.199, (f32[256,32]{0,1:T(8,128)S(1)}, bf16[256,128]{1,0:T(8,128)(2,1)S(1)}, bf16[5,32,128,64]{2,0,3,1:T(8,128)(2,1)}, f32[256,32,64]{0,2,1:T(8,128)S(1)}, f32[256,32]{0,1:T(8,128)S(1)}) %tuple.84), branch_computations={%region_11.12_spmd, %region_12.13_spmd} | conditional | flops 135798784 | bytes 16449544 | solution.py:77
  201.7 2.9 %copy.43 = bf16[5,32,128,64]{2,3,1,0:T(8,128)(2,1)S(1)} copy(bf16[5,32,128,64]{2,0,3,1:T(8,128)(2,1)} %get-tuple-element.180) | data formatting | bytes 5242880 | tf_op jit(solution)/shard_map
  205.1 0.5 add_convert_fusion
  205.6 0.6 copy.47
  206.3 1.0 copy-done.3
  207.3 0.8 copy-done.1
  (51 shorter events, 3.9 us)
Async XLA Ops:
  6.5 3.7 %copy-start = (bf16[256,128]{1,0:T(8,128)(2,1)S(1)}, bf16[256,128]{1,0:T(8,128)(2,1)}, u32[]{:S(2)}) copy-start(bf16[256,128]{1,0:T(8,128)(2,1)} %param.16) | copy-start | bytes 196612
  6.5 85.1 %all-gather.3.cloned.1.call-start = ((), (), s32[]{:S(2)}) async-start(), calls=%async_computation | async-start | bytes 17301504 | tf_op jit(solution)/shard_map/all_gather | solution.py:57
  10.6 2.2 %copy-start.5 = (u32[256]{0:T(256)S(1)}, u32[256]{0:T(256)}, u32[]{:S(2)}) copy-start(u32[256]{0:T(256)} %constant.35) | copy-start | bytes 3076
  10.7 67.1 %copy-start.4 = (f32[6,32,256]{2,1,0:T(8,128)S(1)}, f32[6,32,256]{2,1,0:T(8,128)}, u32[]{:S(2)}) copy-start(f32[6,32,256]{2,1,0:T(8,128)} %param.19) | copy-start | bytes 589828
  10.7 67.1 %copy-start.2 = (bf16[256,128]{1,0:T(8,128)(2,1)S(1)}, bf16[256,128]{1,0:T(8,128)(2,1)}, u32[]{:S(2)}) copy-start(bf16[256,128]{1,0:T(8,128)(2,1)} %param.17) | copy-start | bytes 196612
  206.3 1.0 copy-start.3
  207.3 0.8 copy-start.1
Sparse Core Ops, SparseCore 0:
  12.9 78.6 all-gather.2
where the time goes:
time: 217 us; the launch traced here: 215 us
  local copies, waits for them, and re-layouts  105 us (48%)
  blocking collectives  63 us (29%)
  matrix products  16.9 us (8%)
  between operations  14.2 us (7%)
  waiting for transfers between devices  11 us (5%)
  other arithmetic  4.08 us (2%)
    reshape x2, local copies, waits for them, and re-layouts, body(): piece.reshape(width, head_count, state_rows, HEAD).astype(jnp.float32)  82.3 us
    unnamed x1, blocking collectives  63 us
    another operation x9, local copies, waits for them, and re-layouts  14.7 us
    dot_general x1, matrix products, body(): jnp.einsum('lkh,khnp->lhnp', weights, shaped, precision=lax.Precision.HIG...  11.5 us
    all_gather x1, waiting for transfers between devices, body(): piece = lax.all_gather(flat_ends, 'ctx', axis=0, tiled=True)  11 us
  transfers between devices with their start and end apart: 1, of which 1 were waited for; matrix products, arithmetic and copies ran while one was open for 2% of the time, Pallas kernels for 0%

commit v1 on v0

v1 whole, which is shorter than its diff:
```python
import functools

import jax
import jax.numpy as jnp
from jax import lax
from jax.experimental import pallas as pl
from jax.experimental.pallas import tpu as pltpu
from jax.sharding import PartitionSpec as P

HEADS = 32
HEAD = 64
STATE = 128
TOK = 256
LEVELS = 5
HALF = HEADS * HEAD // 2
PACK = STATE + 16
LOG2E = 1.4426950408889634
F32 = jnp.float32
BF16 = jnp.bfloat16
SMEM = pl.BlockSpec(memory_space=pltpu.SMEM)
VMEM = pl.BlockSpec(memory_space=pltpu.VMEM)


def split3(value):
    high = value.astype(BF16)
    rest = value - high.astype(F32)
    middle = rest.astype(BF16)
    low = (rest - middle.astype(F32)).astype(BF16)
    return high, middle, low


def exact_dot(zero_one, value, dims):
    return sum(
        lax.dot_general(zero_one, part, (dims, ((), ())), preferred_element_type=F32) for part in split3(value)
    )


def pad_heads(value):
    return jnp.concatenate([value, jnp.zeros((128 - HEADS, value.shape[1]), F32)], axis=0)


def spread(table, first):
    lane = lax.broadcasted_iota(jnp.int32, table.shape, 1)
    return jnp.take_along_axis(table, jnp.where(lane < HEAD, first, first + 1), axis=1)


def triangle(compare):
    rows = lax.broadcasted_iota(jnp.int32, (TOK, TOK), 0)
    columns = lax.broadcasted_iota(jnp.int32, (TOK, TOK), 1)
    return compare(rows, columns).astype(F32).astype(BF16)


def total_rows(sums):
    row = lax.broadcasted_iota(jnp.int32, sums.shape, 0)
    high, middle, low = (part.astype(F32) for part in split3(sums))
    rows = jnp.where(row == 0, high, jnp.where(row == 1, middle, jnp.where(row == 2, low, 0.0)))
    return rows.astype(BF16)


def read_total(rows):
    return jnp.sum(rows.astype(F32), axis=0, keepdims=True)


def ends_kernel(flags, decay_ref, key_ref, x_ref, packet_ref):
    core = flags[0]
    decay = pad_heads(decay_ref[...])
    after = exact_dot(triangle(lambda r, c: c > r), decay, ((1,), (1,)))
    sums = exact_dot(jnp.ones((16, TOK), BF16), decay, ((1,), (1,)))
    factor = jnp.exp(after)
    keys = key_ref[...]
    for which in range(2):
        half = 1 - core if which == 0 else core
        for chunk in range(HALF // 256):
            pieces = []
            for pair in range(2):
                first = half * (HEADS // 2) + chunk * 4 + pair * 2
                offset = pl.multiple_of(half * HALF + chunk * 256 + pair * 128, 128)
                x = x_ref[:, pl.ds(offset, 128)].astype(F32)
                pieces.append((x * spread(factor, first)).astype(BF16))
                lanes = pl.ds(chunk * 256 + pair * 128, 128)
                packet_ref[which, STATE:PACK, lanes] = total_rows(spread(sums, first))
            decayed = jnp.concatenate(pieces, axis=1)
            state = lax.dot_general(keys, decayed, (((0,), (0,)), ((), ())), preferred_element_type=F32)
            packet_ref[which, 0:STATE, pl.ds(chunk * 256, 256)] = state.astype(BF16)


def make_ends(flags, decay, keys, x):
    return pl.pallas_call(
        ends_kernel,
        out_shape=jax.ShapeDtypeStruct((2, PACK, HALF), BF16),
        in_specs=[SMEM, VMEM, VMEM, VMEM],
        out_specs=VMEM,
        cost_estimate=pl.CostEstimate(flops=2 * TOK * STATE * 2 * HALF, bytes_accessed=2 << 20, transcendentals=32768),
        name="ends",
    )(flags, decay, keys, x)


def merge_kernel(bit, flags, *refs):
    if bit == 0:
        own_ref, got_ref, state_ref, sum_ref, packet_ref = refs
        own = own_ref[0:STATE].astype(F32)
        own_sum = read_total(own_ref[STATE:PACK])
    else:
        own_ref, own_sum_ref, got_ref, state_ref, sum_ref, packet_ref = refs
        own = own_ref[...]
        own_sum = own_sum_ref[0:1]
    right = flags[1 + bit] == 1
    got = got_ref[0:STATE].astype(F32)
    got_sum = read_total(got_ref[STATE:PACK])
    decay = jnp.exp(jnp.where(right, own_sum, got_sum))
    state = jnp.where(right, got, own) * decay + jnp.where(right, own, got)
    sums = own_sum + got_sum
    state_ref[...] = state
    sum_ref[...] = jnp.broadcast_to(sums, (8, HALF))
    packet_ref[0:STATE] = state.astype(BF16)
    packet_ref[STATE:PACK] = total_rows(jnp.broadcast_to(sums, (16, HALF)))


def merge(bit, flags, *arrays):
    return pl.pallas_call(
        functools.partial(merge_kernel, bit),
        out_shape=[
            jax.ShapeDtypeStruct((STATE, HALF), F32),
            jax.ShapeDtypeStruct((8, HALF), F32),
            jax.ShapeDtypeStruct((PACK, HALF), BF16),
        ],
        in_specs=[SMEM] + [VMEM] * len(arrays),
        out_specs=[VMEM] * 3,
        cost_estimate=pl.CostEstimate(flops=1 << 19, bytes_accessed=1 << 20, transcendentals=4096),
        name="merge",
    )(flags, *arrays)


def local_kernel(flags, decay_ref, mix_ref, key_ref, query_ref, x_ref, total_ref, weight_ref, scores, column, row):
    decay = decay_ref[...]
    causal = triangle(lambda r, c: r >= c)
    cum_column = exact_dot(causal, pad_heads(decay), ((1,), (1,)))
    cum_row = cum_column.T[0:HEADS]
    row[...] = cum_row * LOG2E
    column[...] = (cum_column + jnp.log(pad_mix(mix_ref[0])).T) * LOG2E
    gate = jnp.exp(cum_row)
    weights = [
        mix_ref[level + 1] * gate * flags[1 + level].astype(F32) for level in range(LEVELS)
    ]
    weights.append(jnp.zeros((256 - HEADS * LEVELS, TOK), F32))
    weight_ref[...] = jnp.concatenate(weights, axis=0).T
    raw = lax.dot_general(query_ref[...], key_ref[...], (((1,), (1,)), ((), ())), preferred_element_type=F32)
    scores[...] = raw * causal.astype(F32)

    def pair_step(pair, _):
        offset = pl.multiple_of(pair * 128, 128)
        x = x_ref[:, pl.ds(offset, 128)]
        lane = lax.broadcasted_iota(jnp.int32, (TOK, 128), 1)
        result = jnp.zeros((TOK, 128), F32)
        for side in range(2):
            head = pair * 2 + side
            index = jnp.full((TOK, 128), head, jnp.int32)
            col = jnp.take_along_axis(column[...], index, axis=1)
            gap = jnp.concatenate([col, col], axis=1) - row[pl.ds(head, 1)]
            mixing = (scores[...] * jnp.exp2(jnp.minimum(gap, 1.0))).astype(BF16)
            chosen = jnp.where((lane < HEAD) == (side == 0), x, jnp.zeros_like(x))
            result = result + lax.dot_general(
                mixing, chosen, (((1,), (0,)), ((), ())), preferred_element_type=F32
            )
        total_ref[:, pl.ds(offset, 128)] = result
        return 0

    lax.fori_loop(0, HEADS // 2, pair_step, 0)


def pad_mix(value):
    return jnp.concatenate([value, jnp.ones((128 - HEADS, value.shape[1]), F32)], axis=0)


def make_local(flags, decay, mix, keys, queries, x):
    return pl.pallas_call(
        local_kernel,
        out_shape=[
            jax.ShapeDtypeStruct((TOK, 2 * HALF), F32),
            jax.ShapeDtypeStruct((TOK, 256), F32),
        ],
        in_specs=[SMEM] + [VMEM] * 5,
        out_specs=[VMEM] * 2,
        scratch_shapes=[pltpu.VMEM((TOK, TOK), F32), pltpu.VMEM((TOK, 128), F32), pltpu.VMEM((HEADS, TOK), F32)],
        cost_estimate=pl.CostEstimate(
            flops=4 * TOK * TOK * 2 * HALF, bytes_accessed=4 << 20, transcendentals=HEADS * TOK * TOK
        ),
        name="local",
    )(flags, decay, mix, keys, queries, x)


def levels_kernel(count, flags, total_ref, weight_ref, query_ref, *refs):
    packets, (out_ref, gap_ref) = refs[: 2 * count], refs[2 * count :]
    core = flags[0]
    queries = query_ref[...]
    for which in range(2):
        half = core if which == 0 else 1 - core
        gap = jnp.zeros((1, HALF), F32)
        for chunk in range(HALF // 256):
            lanes = pl.ds(chunk * 256, 256)
            columns = pl.ds(pl.multiple_of(half * HALF + chunk * 256, 256), 256)
            running = total_ref[:, columns]
            gap = jnp.zeros((1, 256), F32)
            for level in range(count):
                packet = packets[2 * level + which]
                product = jnp.dot(queries, packet[0:STATE, lanes], preferred_element_type=F32)
                first = level * HEADS + half * (HEADS // 2) + chunk * 4
                table = weight_ref[:, 0:128] if level < 4 else weight_ref[:, 128:256]
                if level >= 4:
                    first = first - 128
                weight = jnp.concatenate([spread(table, first), spread(table, first + 2)], axis=1)
                running = running + product * (weight * jnp.exp(gap))
                gap = gap + read_total(packet[STATE:PACK, lanes]) * flags[1 + level].astype(F32)
            out_ref[:, columns] = running
            gap_ref[:, pl.ds(which * HALF + chunk * 256, 256)] = jnp.broadcast_to(gap, (8, 256))


def add_levels(flags, total, weights, queries, *packets):
    count = len(packets) // 2
    return pl.pallas_call(
        functools.partial(levels_kernel, count),
        out_shape=[
            jax.ShapeDtypeStruct((TOK, 2 * HALF), F32),
            jax.ShapeDtypeStruct((8, 2 * HALF), F32),
        ],
        in_specs=[SMEM] + [VMEM] * (3 + 2 * count),
        out_specs=[VMEM] * 2,
        input_output_aliases={1: 0},
        cost_estimate=pl.CostEstimate(
            flops=2 * count * TOK * STATE * 2 * HALF, bytes_accessed=6 << 20, transcendentals=0
        ),
        name="levels",
    )(flags, total, weights, queries, *packets)


def last_kernel(flags, total_ref, gap_ref, weight_ref, query_ref, mine_ref, other_ref, out_ref):
    core = flags[0]
    queries = query_ref[...]
    table = weight_ref[:, 128:256]
    for which, packet in enumerate((mine_ref, other_ref)):
        half = core if which == 0 else 1 - core
        for chunk in range(HALF // 256):
            lanes = pl.ds(chunk * 256, 256)
            columns = pl.ds(pl.multiple_of(half * HALF + chunk * 256, 256), 256)
            product = jnp.dot(queries, packet[0:STATE, lanes], preferred_element_type=F32)
            first = half * (HEADS // 2) + chunk * 4
            weight = jnp.concatenate([spread(table, first), spread(table, first + 2)], axis=1)
            gap = gap_ref[0:1, pl.ds(which * HALF + chunk * 256, 256)]
            out_ref[:, columns] = (total_ref[:, columns] + product * (weight * jnp.exp(gap))).astype(BF16)


def add_last(flags, total, gap, weights, queries, mine, other):
    return pl.pallas_call(
        last_kernel,
        out_shape=jax.ShapeDtypeStruct((TOK, 2 * HALF), BF16),
        in_specs=[SMEM] + [VMEM] * 6,
        out_specs=VMEM,
        cost_estimate=pl.CostEstimate(
            flops=2 * TOK * STATE * 2 * HALF, bytes_accessed=4 << 20, transcendentals=0
        ),
        name="last",
    )(flags, total, gap, weights, queries, mine, other)


def body(inputs, write_keys, read_queries, decay_log, level_mix):
    devices = lax.axis_size("ctx")
    index = lax.axis_index("ctx")
    shifts = jnp.array([0, 0, 1, 2, 3, 4, 0, 0], jnp.int32)
    flags = (index >> shifts) & 1

    def swap(array, mask):
        return lax.ppermute(array, "ctx", [(i, i ^ mask) for i in range(devices)])

    packets = make_ends(flags, decay_log, write_keys, inputs)
    mine = [swap(packets[0], 1)]
    other = [swap(packets[1], 1)]
    total, weights = make_local(flags, decay_log, level_mix, write_keys, read_queries, inputs)
    state, sums, packet = merge(0, flags, packets[1], mine[0])
    for level in range(1, LEVELS):
        got = swap(packet, {1: 2, 2: 6, 3: 8, 4: 24}[level])
        mine.append(got)
        other.append(swap(got, 1))
        if level < LEVELS - 1:
            state, sums, packet = merge(level, flags, state, sums, got)
    order = [p for pair in zip(mine[:4], other[:4]) for p in pair]
    total, gap = add_levels(flags, total, weights, read_queries, *order)
    return add_last(flags, total, gap, weights, read_queries, mine[4], other[4])


def solution(mesh):
    placed = (
        P(("seq", "ctx"), None),
        P(("seq", "ctx"), None),
        P(("seq", "ctx"), None),
        P(None, ("seq", "ctx")),
        P(None, None, ("seq", "ctx")),
    )
    return jax.shard_map(
        body, mesh=mesh, in_specs=placed, out_specs=P(("seq", "ctx"), None), check_vma=False
    )
```

time: 217 us -> 78.4 us (0.36)
  the two profiles are of different devices: /device:TPU:31 before, /device:TPU:1 now
where the time goes in v1:
time: 78.4 us; the launch traced here: 78.1 us
  Pallas kernels  31.1 us (40%)
  waiting for transfers between devices  26.4 us (34%)
  starting transfers between devices  13 us (17%)
  local copies, waits for them, and re-layouts  6.33 us (8%)
  other arithmetic  1.19 us (2%)
    ppermute x10, waiting for transfers between devices, swap(): return lax.ppermute(array, 'ctx', [(i, i ^ mask) for i in range(devices)])  26.4 us
    ppermute x10, starting transfers between devices, swap(): return lax.ppermute(array, 'ctx', [(i, i ^ mask) for i in range(devices)])  13 us
    pallas_call x1, Pallas kernels, make_local(): pl.pallas_call(local_kernel, out_shape=[jax.ShapeDtypeStruct((TOK, 2 * HA...  8.94 us
    pallas_call x4, Pallas kernels, merge(): pl.pallas_call(functools.partial(merge_kernel, bit), out_shape=[jax.Shape...  8.6 us
    pallas_call x1, Pallas kernels, add_levels(): pl.pallas_call(functools.partial(levels_kernel, count), out_shape=[jax.Sh...  6.27 us
    unnamed x22, local copies, waits for them, and re-layouts  4.52 us
    pallas_call x1, Pallas kernels, make_ends(): pl.pallas_call(ends_kernel, out_shape=jax.ShapeDtypeStruct((2, PACK, HALF...  3.72 us
    pallas_call x1, Pallas kernels, add_last(): pl.pallas_call(last_kernel, out_shape=jax.ShapeDtypeStruct((TOK, 2 * HALF...  3.55 us
  transfers between devices with their start and end apart: 10, of which 5 were waited for; matrix products, arithmetic and copies ran while one was open for 0% of the time, Pallas kernels for 19%

profile of v1, /device:TPU:1, one launch (start us, length us, event | category | flops | bytes accessed | tf_op | source)
XLA Modules:
  0.0 78.1 jit_solution(7022517927463454664)
XLA Ops:
  0.0 1.2 %shift-right-arithmetic_and_fusion.flags = s32[8]{0:T(128)} fusion(s32[8]{0:T(128)} %constant.8.clone, s32[]{:T(128)S(6)} %axis_index.12), kind=kLoop, calls=%fused_computation.2 | loop fusion | flops 16 | bytes 68 | tf_op jit(solution)/shard_map/and | solution.py:269
  1.2 3.7 %ends.1 = bf16[2,144,1024]{2,1,0:T(8,128)(2,1)} custom-call(s32[8]{0:T(128)} %shift-right-arithmetic_and_fusion.flags, f32[32,256]{1,0:T(8,128)} %decay_ref.3, bf16[256,128]{1,0:T(8,128)(2,1)} %key_ref.3, bf16[256,2048]{1,0:T(8,128)(2,1)} %x_ref.3), custom_call_target="tpu_custom_call" | custom-call | flops 134217728 | bytes 2097152 | tf_op jit(solution)/shard_map/ends/pallas_call | solution.py:88
  4.9 1.8 %slice_bitcast_fusion = (bf16[144,1024]{1,0:T(8,128)(2,1)}, bf16[144,1024]{1,0:T(8,128)(2,1)S(1)}) fusion(bf16[2,144,1024]{2,1,0:T(8,128)(2,1)} %ends.1), kind=kLoop, calls=%fused_computation | loop fusion | bytes 1179648 | tf_op jit(solution)/shard_map/squeeze | solution.py:276
  6.7 3.2 %collective-permute-start = (bf16[144,1024]{1,0:T(8,128)(2,1)S(1)}, bf16[144,1024]{1,0:T(8,128)(2,1)S(1)}, u32[]{:S(2)}, u32[]{:S(2)}) collective-permute-start(bf16[144,1024]{1,0:T(8,128)(2,1)S(1)} %get-tuple-element.34), channel_id=1, source_target_pairs={{0,1},{1,0},{2,3},{3,2},{4,5},{5,4},{6,7},{7,6},{8,9},{9,8},{10,11... | collective-permute-start | bytes 884744 | tf_op jit(solution)/shard_map/ppermute | solution.py:272
  10.0 1.2 %collective-permute-done.refs_1_.refs_0_ = bf16[144,1024]{1,0:T(8,128)(2,1)S(1)} collective-permute-done((bf16[144,1024]{1,0:T(8,128)(2,1)S(1)}, bf16[144,1024]{1,0:T(8,128)(2,1)S(1)}, u32[]{:S(2)}, u32[]{:S(2)}) %collective-permute-start) | collective-permute-done | bytes 294944 | tf_op jit(solution)/shard_map/ppermute | solution.py:272
  11.2 0.7 copy-done
  11.9 2.1 %merge.4 = (f32[128,1024]{1,0:T(8,128)}, f32[8,1024]{1,0:T(8,128)}, bf16[144,1024]{1,0:T(8,128)(2,1)}) custom-call(s32[8]{0:T(128)} %shift-right-arithmetic_and_fusion.flags, bf16[144,1024]{1,0:T(8,128)(2,1)} %get-tuple-element.33.refs_0_, bf16[144,1024]{1,0:T(8,128)(2,1)} %copy-done), custom_call_target="tpu_custom_call" | custom-call | flops 524288 | bytes 1048576 | tf_op jit(solution)/shard_map/merge/pallas_call | solution.py:120
  14.0 8.4 %collective-permute-done.2.refs_2_ = bf16[144,1024]{1,0:T(8,128)(2,1)S(1)} collective-permute-done((bf16[144,1024]{1,0:T(8,128)(2,1)}, bf16[144,1024]{1,0:T(8,128)(2,1)S(1)}, u32[]{:S(2)}, u32[]{:S(2)}) %collective-permute-start.2) | collective-permute-done | bytes 294944 | tf_op jit(solution)/shard_map/ppermute | solution.py:272
  22.4 0.7 copy-done.1
  23.1 2.2 %merge.5 = (f32[128,1024]{1,0:T(8,128)}, f32[8,1024]{1,0:T(8,128)}, bf16[144,1024]{1,0:T(8,128)(2,1)}) custom-call(s32[8]{0:T(128)} %shift-right-arithmetic_and_fusion.flags, f32[128,1024]{1,0:T(8,128)} %get-tuple-element.22.refs_0_, f32[8,1024]{1,0:T(8,128)} %get-tuple-element.23.refs_1_, bf16[144,1024]{1,0:T(8,128)(2,1)} %copy-done.1), custom_call_target="tpu_custom_call" | custom-call | flops 524288 | bytes 1048576 | tf_op jit(solution)/shard_map/merge/pallas_call | solution.py:120
  25.3 0.7 collective-permute-start.4
  26.0 8.0 %collective-permute-done.4.refs_2_.refs_4_ = bf16[144,1024]{1,0:T(8,128)(2,1)S(1)} collective-permute-done((bf16[144,1024]{1,0:T(8,128)(2,1)}, bf16[144,1024]{1,0:T(8,128)(2,1)S(1)}, u32[]{:S(2)}, u32[]{:S(2)}) %collective-permute-start.4) | collective-permute-done | bytes 294944 | tf_op jit(solution)/shard_map/ppermute | solution.py:272
  34.0 0.7 copy-done.2
  34.7 2.2 %merge.6 = (f32[128,1024]{1,0:T(8,128)}, f32[8,1024]{1,0:T(8,128)}, bf16[144,1024]{1,0:T(8,128)(2,1)}) custom-call(s32[8]{0:T(128)} %shift-right-arithmetic_and_fusion.flags, f32[128,1024]{1,0:T(8,128)} %get-tuple-element.25.refs_0_, f32[8,1024]{1,0:T(8,128)} %get-tuple-element.26.refs_1_, bf16[144,1024]{1,0:T(8,128)(2,1)} %copy-done.2), custom_call_target="tpu_custom_call" | custom-call | flops 524288 | bytes 1048576 | tf_op jit(solution)/shard_map/merge/pallas_call | solution.py:120
  36.9 6.6 %collective-permute-done.6.refs_6_.refs_2_ = bf16[144,1024]{1,0:T(8,128)(2,1)S(1)} collective-permute-done((bf16[144,1024]{1,0:T(8,128)(2,1)}, bf16[144,1024]{1,0:T(8,128)(2,1)S(1)}, u32[]{:S(2)}, u32[]{:S(2)}) %collective-permute-start.6) | collective-permute-done | bytes 294944 | tf_op jit(solution)/shard_map/ppermute | solution.py:272
  43.5 0.7 copy-done.3
  44.2 2.2 %merge.7 = (f32[128,1024]{1,0:T(8,128)}, f32[8,1024]{1,0:T(8,128)}, bf16[144,1024]{1,0:T(8,128)(2,1)}) custom-call(s32[8]{0:T(128)} %shift-right-arithmetic_and_fusion.flags, f32[128,1024]{1,0:T(8,128)} %get-tuple-element.30.refs_0_, f32[8,1024]{1,0:T(8,128)} %get-tuple-element.31.refs_1_, bf16[144,1024]{1,0:T(8,128)(2,1)} %copy-done.3), custom_call_target="tpu_custom_call" | custom-call | flops 524288 | bytes 1048576 | tf_op jit(solution)/shard_map/merge/pallas_call | solution.py:120
  46.4 1.0 %collective-permute-start.8 = (bf16[144,1024]{1,0:T(8,128)(2,1)}, bf16[144,1024]{1,0:T(8,128)(2,1)S(1)}, u32[]{:S(2)}, u32[]{:S(2)}) collective-permute-start(bf16[144,1024]{1,0:T(8,128)(2,1)} %get-tuple-element.32), channel_id=1, source_target_pairs={{0,24},{1,25},{2,26},{3,27},{4,28},{5,29},{6,30},{7,31},{8,16},{9,... | collective-permute-start | bytes 884744 | tf_op jit(solution)/shard_map/ppermute | solution.py:272
  47.4 3.3 %collective-permute-start.1 = (bf16[144,1024]{1,0:T(8,128)(2,1)S(1)}, bf16[144,1024]{1,0:T(8,128)(2,1)S(1)}, u32[]{:S(2)}, u32[]{:S(2)}) collective-permute-start(bf16[144,1024]{1,0:T(8,128)(2,1)S(1)} %copy-done.4), channel_id=1, source_target_pairs={{0,1},{1,0},{2,3},{3,2},{4,5},{5,4},{6,7},{7,6},{8,9},{9,8},{10,11... | collective-permute-start | bytes 884744 | tf_op jit(solution)/shard_map/ppermute | solution.py:272
  50.7 0.0 collective-permute-start.3
  50.7 0.5 collective-permute-start.5
  51.2 0.0 collective-permute-start.7
  51.2 2.2 %collective-permute-done.8.mine_ref = bf16[144,1024]{1,0:T(8,128)(2,1)S(1)} collective-permute-done((bf16[144,1024]{1,0:T(8,128)(2,1)}, bf16[144,1024]{1,0:T(8,128)(2,1)S(1)}, u32[]{:S(2)}, u32[]{:S(2)}) %collective-permute-start.8) | collective-permute-done | bytes 294944 | tf_op jit(solution)/shard_map/ppermute | solution.py:272
  53.4 4.2 %collective-permute-start.9 = (bf16[144,1024]{1,0:T(8,128)(2,1)S(1)}, bf16[144,1024]{1,0:T(8,128)(2,1)S(1)}, u32[]{:S(2)}, u32[]{:S(2)}) collective-permute-start(bf16[144,1024]{1,0:T(8,128)(2,1)S(1)} %collective-permute-done.8.mine_ref), channel_id=1, source_target_pairs={{0,1},{1,0},{2,3},{3,2},{4,5},{5,4},{6,7},{7,6},{8,9},{9,8},{10,11... | collective-permute-start | bytes 884744 | tf_op jit(solution)/shard_map/ppermute | solution.py:272
  57.6 8.9 %local.1 = (f32[256,2048]{1,0:T(8,128)}, f32[256,256]{1,0:T(8,128)}) custom-call(s32[8]{0:T(128)} %shift-right-arithmetic_and_fusion.flags, f32[32,256]{1,0:T(8,128)} %decay_ref.3, f32[6,32,256]{2,1,0:T(8,128)} %mix_ref.1, bf16[256,128]{1,0:T(8,128)(2,1)} %key_ref.3, bf16[256,128]{1,0:T(8,128)(2,1)} %query_ref.5, bf16[256,2048]{1,0:T(8,128)(2,1)} %x_ref.3), custom_call_target="tpu_custom_call" | custom-call | flops 536870912 | bytes 4194304 | tf_op jit(solution)/shard_map/local/pallas_call | solution.py:176
  66.6 0.6 copy-done.6
  67.3 0.1 copy-done.7
  67.3 0.1 copy-done.8
  67.4 0.1 copy-done.10
  67.5 6.3 %levels.1 = (f32[256,2048]{1,0:T(8,128)}, f32[8,2048]{1,0:T(8,128)}) custom-call(s32[8]{0:T(128)} %shift-right-arithmetic_and_fusion.flags, f32[256,2048]{1,0:T(8,128)} %get-tuple-element.19.total_ref, f32[256,256]{1,0:T(8,128)} %get-tuple-element.20.weight_ref, bf16[256,128]{1,0:T(8,128)(2,1)} %query_ref.5, ...), custom_call_target="tpu_custom_call", output_to_operand_aliasing={{0}: (1, {})} | custom-call | flops 536870912 | bytes 6291456 | tf_op jit(solution)/shard_map/levels/pallas_call | solution.py:220
  73.8 0.7 copy-done.9
  74.5 3.6 %last.1 = bf16[256,2048]{1,0:T(8,128)(2,1)} custom-call(s32[8]{0:T(128)} %shift-right-arithmetic_and_fusion.flags, f32[256,2048]{1,0:T(8,128)} %get-tuple-element.28.total_ref, f32[8,2048]{1,0:T(8,128)} %get-tuple-element.29.gap_ref, f32[256,256]{1,0:T(8,128)} %get-tuple-element.20.weight_ref, bf16[256,128]{1,0:T(8,128)(2,1)} %query_ref.5, ...), custom_call_target="tpu_custom_call" | custom-call | flops 134217728 | bytes 4194304 | tf_op jit(solution)/shard_map/last/pallas_call | solution.py:253
  (20 shorter events, 0.0 us)
Async XLA Ops:
  6.7 40.7 %copy-start.4 = (bf16[144,1024]{1,0:T(8,128)(2,1)S(1)}, bf16[144,1024]{1,0:T(8,128)(2,1)}, u32[]{:S(2)}) copy-start(bf16[144,1024]{1,0:T(8,128)(2,1)} %get-tuple-element.33.refs_0_) | copy-start | bytes 884740
  6.7 4.5 %collective-permute-start = (bf16[144,1024]{1,0:T(8,128)(2,1)S(1)}, bf16[144,1024]{1,0:T(8,128)(2,1)S(1)}, u32[]{:S(2)}, u32[]{:S(2)}) collective-permute-start(bf16[144,1024]{1,0:T(8,128)(2,1)S(1)} %get-tuple-element.34), channel_id=1, source_target_pairs={{0,1},{1,0},{2,3},{3,2},{4,5},{5,4},{6,7},{7,6},{8,9},{9,8},{10,11... | collective-permute-start | bytes 884744 | tf_op jit(solution)/shard_map/ppermute | solution.py:272
  11.2 0.7 copy-start
  14.0 8.4 %collective-permute-start.2 = (bf16[144,1024]{1,0:T(8,128)(2,1)}, bf16[144,1024]{1,0:T(8,128)(2,1)S(1)}, u32[]{:S(2)}, u32[]{:S(2)}) collective-permute-start(bf16[144,1024]{1,0:T(8,128)(2,1)} %get-tuple-element.21), channel_id=1, source_target_pairs={{0,2},{1,3},{2,0},{3,1},{4,6},{5,7},{6,4},{7,5},{8,10},{9,11},{10,... | collective-permute-start | bytes 884744 | tf_op jit(solution)/shard_map/ppermute | solution.py:272
  22.4 0.7 copy-start.1
  25.3 8.7 %collective-permute-start.4 = (bf16[144,1024]{1,0:T(8,128)(2,1)}, bf16[144,1024]{1,0:T(8,128)(2,1)S(1)}, u32[]{:S(2)}, u32[]{:S(2)}) collective-permute-start(bf16[144,1024]{1,0:T(8,128)(2,1)} %get-tuple-element.24), channel_id=1, source_target_pairs={{0,6},{1,7},{2,4},{3,5},{4,2},{5,3},{6,0},{7,1},{8,14},{9,15},{10,... | collective-permute-start | bytes 884744 | tf_op jit(solution)/shard_map/ppermute | solution.py:272
  34.0 0.7 copy-start.2
  36.9 6.6 %collective-permute-start.6 = (bf16[144,1024]{1,0:T(8,128)(2,1)}, bf16[144,1024]{1,0:T(8,128)(2,1)S(1)}, u32[]{:S(2)}, u32[]{:S(2)}) collective-permute-start(bf16[144,1024]{1,0:T(8,128)(2,1)} %get-tuple-element.27), channel_id=1, source_target_pairs={{0,8},{1,9},{2,10},{3,11},{4,12},{5,13},{6,14},{7,15},{8,0},{9,1},... | collective-permute-start | bytes 884744 | tf_op jit(solution)/shard_map/ppermute | solution.py:272
  43.5 0.7 copy-start.3
  46.4 7.0 %collective-permute-start.8 = (bf16[144,1024]{1,0:T(8,128)(2,1)}, bf16[144,1024]{1,0:T(8,128)(2,1)S(1)}, u32[]{:S(2)}, u32[]{:S(2)}) collective-permute-start(bf16[144,1024]{1,0:T(8,128)(2,1)} %get-tuple-element.32), channel_id=1, source_target_pairs={{0,24},{1,25},{2,26},{3,27},{4,28},{5,29},{6,30},{7,31},{8,16},{9,... | collective-permute-start | bytes 884744 | tf_op jit(solution)/shard_map/ppermute | solution.py:272
  47.4 19.1 %collective-permute-start.1 = (bf16[144,1024]{1,0:T(8,128)(2,1)S(1)}, bf16[144,1024]{1,0:T(8,128)(2,1)S(1)}, u32[]{:S(2)}, u32[]{:S(2)}) collective-permute-start(bf16[144,1024]{1,0:T(8,128)(2,1)S(1)} %copy-done.4), channel_id=1, source_target_pairs={{0,1},{1,0},{2,3},{3,2},{4,5},{5,4},{6,7},{7,6},{8,9},{9,8},{10,11... | collective-permute-start | bytes 884744 | tf_op jit(solution)/shard_map/ppermute | solution.py:272
  50.7 15.8 %collective-permute-start.3 = (bf16[144,1024]{1,0:T(8,128)(2,1)}, bf16[144,1024]{1,0:T(8,128)(2,1)S(1)}, u32[]{:S(2)}, u32[]{:S(2)}) collective-permute-start(bf16[144,1024]{1,0:T(8,128)(2,1)} %copy-done.1), channel_id=1, source_target_pairs={{0,1},{1,0},{2,3},{3,2},{4,5},{5,4},{6,7},{7,6},{8,9},{9,8},{10,11... | collective-permute-start | bytes 884744 | tf_op jit(solution)/shard_map/ppermute | solution.py:272
  50.7 15.8 %collective-permute-start.5 = (bf16[144,1024]{1,0:T(8,128)(2,1)}, bf16[144,1024]{1,0:T(8,128)(2,1)S(1)}, u32[]{:S(2)}, u32[]{:S(2)}) collective-permute-start(bf16[144,1024]{1,0:T(8,128)(2,1)} %copy-done.2), channel_id=1, source_target_pairs={{0,1},{1,0},{2,3},{3,2},{4,5},{5,4},{6,7},{7,6},{8,9},{9,8},{10,11... | collective-permute-start | bytes 884744 | tf_op jit(solution)/shard_map/ppermute | solution.py:272
  51.2 15.3 %collective-permute-start.7 = (bf16[144,1024]{1,0:T(8,128)(2,1)}, bf16[144,1024]{1,0:T(8,128)(2,1)S(1)}, u32[]{:S(2)}, u32[]{:S(2)}) collective-permute-start(bf16[144,1024]{1,0:T(8,128)(2,1)} %copy-done.3), channel_id=1, source_target_pairs={{0,1},{1,0},{2,3},{3,2},{4,5},{5,4},{6,7},{7,6},{8,9},{9,8},{10,11... | collective-permute-start | bytes 884744 | tf_op jit(solution)/shard_map/ppermute | solution.py:272
  53.4 20.4 %copy-start.5 = (bf16[144,1024]{1,0:T(8,128)(2,1)}, bf16[144,1024]{1,0:T(8,128)(2,1)S(1)}, u32[]{:S(2)}) copy-start(bf16[144,1024]{1,0:T(8,128)(2,1)S(1)} %collective-permute-done.8.mine_ref) | copy-start | bytes 884740
  53.4 20.4 %collective-permute-start.9 = (bf16[144,1024]{1,0:T(8,128)(2,1)S(1)}, bf16[144,1024]{1,0:T(8,128)(2,1)S(1)}, u32[]{:S(2)}, u32[]{:S(2)}) collective-permute-start(bf16[144,1024]{1,0:T(8,128)(2,1)S(1)} %collective-permute-done.8.mine_ref), channel_id=1, source_target_pairs={{0,1},{1,0},{2,3},{3,2},{4,5},{5,4},{6,7},{7,6},{8,9},{9,8},{10,11... | collective-permute-start | bytes 884744 | tf_op jit(solution)/shard_map/ppermute | solution.py:272
  66.5 0.7 copy-start.6
  66.6 0.8 %copy-start.7 = (bf16[144,1024]{1,0:T(8,128)(2,1)}, bf16[144,1024]{1,0:T(8,128)(2,1)S(1)}, u32[]{:S(2)}) copy-start(bf16[144,1024]{1,0:T(8,128)(2,1)S(1)} %collective-permute-done.3.refs_3_) | copy-start | bytes 884740
  66.6 0.9 %copy-start.8 = (bf16[144,1024]{1,0:T(8,128)(2,1)}, bf16[144,1024]{1,0:T(8,128)(2,1)S(1)}, u32[]{:S(2)}) copy-start(bf16[144,1024]{1,0:T(8,128)(2,1)S(1)} %collective-permute-done.5.refs_5_) | copy-start | bytes 884740
  66.6 1.0 %copy-start.10 = (bf16[144,1024]{1,0:T(8,128)(2,1)}, bf16[144,1024]{1,0:T(8,128)(2,1)S(1)}, u32[]{:S(2)}) copy-start(bf16[144,1024]{1,0:T(8,128)(2,1)S(1)} %collective-permute-done.7.refs_7_) | copy-start | bytes 884740
  73.8 0.7 copy-start.9

commit v2 on v0

v2 whole, which is shorter than its diff:
```python
import functools

import jax
import jax.numpy as jnp
from jax import lax
from jax.experimental import pallas as pl
from jax.experimental.pallas import tpu as pltpu
from jax.sharding import PartitionSpec as P

HEADS = 32
HEAD = 64
STATE = 128
TOK = 256
LEVELS = 5
HALF = HEADS * HEAD // 2
PAIRS = HEADS // 4
BODY = PAIRS * STATE
PACK = BODY + 16
LOG2E = 1.4426950408889634
F32 = jnp.float32
BF16 = jnp.bfloat16
VMEM = pl.BlockSpec(memory_space=pltpu.VMEM)
ANY = pl.BlockSpec(memory_space=pl.ANY)
KEPT = pltpu.MemorySpace.VMEM
PACKET = pltpu.VMEM((PACK, 128), BF16)
SUMS = pltpu.VMEM((8, 128), F32)


def split3(value):
    high = value.astype(BF16)
    rest = value - high.astype(F32)
    middle = rest.astype(BF16)
    low = (rest - middle.astype(F32)).astype(BF16)
    return high, middle, low


def exact_dot(zero_one, value, dims):
    return sum(
        lax.dot_general(zero_one, part, (dims, ((), ())), preferred_element_type=F32) for part in split3(value)
    )


def pad_heads(value):
    return jnp.concatenate([value, jnp.zeros((128 - HEADS, value.shape[1]), F32)], axis=0)


def spread(table, first):
    lane = lax.broadcasted_iota(jnp.int32, table.shape, 1)
    return jnp.take_along_axis(table, jnp.where(lane < HEAD, first, first + 1), axis=1)


def triangle(compare):
    rows = lax.broadcasted_iota(jnp.int32, (TOK, TOK), 0)
    columns = lax.broadcasted_iota(jnp.int32, (TOK, TOK), 1)
    return compare(rows, columns).astype(F32).astype(BF16)


def total_rows(sums):
    row = lax.broadcasted_iota(jnp.int32, sums.shape, 0)
    high, middle, low = (part.astype(F32) for part in split3(sums))
    rows = jnp.where(row == 0, high, jnp.where(row == 1, middle, jnp.where(row == 2, low, 0.0)))
    return rows.astype(BF16)


def read_total(rows):
    return jnp.sum(rows.astype(F32), axis=0, keepdims=True)


def position():
    index = lax.axis_index("ctx")
    return [(index >> bit) & 1 for bit in range(LEVELS)]


def call(kernel, outs, arrays, name, flops, exps=0, kept=(), far=(), out_specs=None, scratch=(), aliases=None):
    arrays = list(arrays)
    for place in kept:
        arrays[place] = pltpu.with_memory_space_constraint(arrays[place], KEPT)
    for place in far:
        arrays[place] = pltpu.with_memory_space_constraint(arrays[place], pltpu.MemorySpace.HBM)
    return pl.pallas_call(
        kernel,
        out_shape=outs,
        in_specs=[ANY if place in far else VMEM for place in range(len(arrays))],
        out_specs=out_specs or [VMEM] * len(outs),
        scratch_shapes=list(scratch),
        input_output_aliases=aliases or {},
        compiler_params=pltpu.CompilerParams(vmem_limit_bytes=20 << 20),
        cost_estimate=pl.CostEstimate(flops=flops, bytes_accessed=1 << 20, transcendentals=exps),
        name=name,
    )(*arrays)


def ends_kernel(decay_hbm, key_hbm, x_hbm, sent_ref, kept_ref, decay_ref, key_ref, x_ref, small, big):
    core = position()[0]
    copies = [
        pltpu.make_async_copy(decay_hbm, decay_ref, small.at[0]), pltpu.make_async_copy(key_hbm, key_ref, small.at[1])
    ]
    halves = (1 - core, core)
    for place, half in enumerate(halves):
        for chunk in range(2):
            columns = pl.ds(pl.multiple_of(half * HALF + chunk * 512, 512), 512)
            copies.append(
                pltpu.make_async_copy(x_hbm.at[:, columns], x_ref.at[:, columns], big.at[2 * place + chunk])
            )
    for copy in copies:
        copy.start()
    copies[0].wait()
    decay = pad_heads(decay_ref[...])
    after = exact_dot(triangle(lambda r, c: c > r), decay, ((1,), (1,)))
    sums = exact_dot(jnp.ones((16, TOK), BF16), decay, ((1,), (1,)))
    factor = jnp.exp(after)
    lane = lax.broadcasted_iota(jnp.int32, sums.shape, 1)
    copies[1].wait()
    keys = key_ref[...]
    for place, (half, packet_ref) in enumerate(zip(halves, (sent_ref, kept_ref))):
        packet_ref[BODY:PACK] = total_rows(jnp.take_along_axis(sums, (lane + half * (HEADS // 2)) & 127, axis=1))
        for duo in range(PAIRS // 2):
            if duo % 2 == 0:
                copies[2 + 2 * place + duo // 2].wait()
            pieces = []
            for pair in (2 * duo, 2 * duo + 1):
                x = x_ref[:, pl.ds(pl.multiple_of(half * HALF + pair * 128, 128), 128)].astype(F32)
                pieces.append((x * spread(factor, half * (HEADS // 2) + pair * 2)).astype(BF16))
            decayed = jnp.concatenate(pieces, axis=1)
            state = lax.dot_general(keys, decayed, (((0,), (0,)), ((), ())), preferred_element_type=F32)
            packet_ref[duo * 256 : duo * 256 + 128] = state[:, 0:128].astype(BF16)
            packet_ref[duo * 256 + 128 : duo * 256 + 256] = state[:, 128:256].astype(BF16)


def merge_kernel(bit, *refs):
    if bit == 0:
        own_ref, got_ref, state_ref, sum_ref, packet_ref = refs
        own_sum = read_total(own_ref[BODY:PACK])
    else:
        own_ref, own_sum_ref, got_ref, state_ref, sum_ref, packet_ref = refs
        own_sum = own_sum_ref[0:1]
    right = position()[bit] == 1
    got_sum = read_total(got_ref[BODY:PACK])
    decay = jnp.broadcast_to(jnp.exp(jnp.where(right, own_sum, got_sum)), (8, 128))
    sums = own_sum + got_sum
    sum_ref[...] = jnp.broadcast_to(sums, (8, 128))
    packet_ref[BODY:PACK] = total_rows(jnp.broadcast_to(sums, (16, 128)))
    for pair in range(PAIRS):
        rows = pl.ds(pair * STATE, STATE)
        own = own_ref[rows].astype(F32)
        got = got_ref[rows].astype(F32)
        factor = spread(decay, 2 * pair)[0:1]
        state = jnp.where(right, got, own) * factor + jnp.where(right, own, got)
        state_ref[rows] = state
        packet_ref[rows] = state.astype(BF16)


def merge(bit, *arrays):
    outs = [pltpu.VMEM((BODY, 128), F32), SUMS, PACKET]
    return call(functools.partial(merge_kernel, bit), outs, arrays, "merge", 1 << 19, 4096, range(len(arrays)))


def local_kernel(other, decay_ref, mix_ref, key_ref, query_ref, x_ref, *refs):
    if other:
        total_ref, scores, column, row = refs
    else:
        total_ref, weight_ref, scores, column, row = refs
    bits = position()
    half = 1 - bits[0] if other else bits[0]
    decay = decay_ref[...]
    causal = triangle(lambda r, c: r >= c)
    cum_column = exact_dot(causal, pad_heads(decay), ((1,), (1,)))
    cum_row = cum_column.T[0:HEADS]
    row[...] = cum_row * LOG2E
    mix = jnp.concatenate([mix_ref[0], jnp.ones((128 - HEADS, TOK), F32)], axis=0)
    column[...] = (cum_column + jnp.log(mix).T) * LOG2E
    if not other:
        gate = jnp.exp(cum_row)
        weights = [mix_ref[level + 1] * gate * bits[level].astype(F32) for level in range(LEVELS)]
        weights.append(jnp.zeros((256 - HEADS * LEVELS, TOK), F32))
        weight_ref[...] = jnp.concatenate(weights, axis=0).T
    raw = lax.dot_general(query_ref[...], key_ref[...], (((1,), (1,)), ((), ())), preferred_element_type=F32)
    scores[...] = raw * causal.astype(F32)

    def pair_step(pair, _):
        offset = pl.multiple_of(half * HALF + pair * 128, 128)
        x = x_ref[:, pl.ds(offset, 128)]
        lane = lax.broadcasted_iota(jnp.int32, (TOK, 128), 1)
        result = jnp.zeros((TOK, 128), F32)
        for side in range(2):
            head = half * (HEADS // 2) + pair * 2 + side
            index = jnp.full((TOK, 128), head, jnp.int32)
            col = jnp.take_along_axis(column[...], index, axis=1)
            gap = jnp.concatenate([col, col], axis=1) - row[pl.ds(head, 1)]
            mixing = (scores[...] * jnp.exp2(jnp.minimum(gap, 1.0))).astype(BF16)
            chosen = jnp.where((lane < HEAD) == (side == 0), x, jnp.zeros_like(x))
            result = result + lax.dot_general(
                mixing, chosen, (((1,), (0,)), ((), ())), preferred_element_type=F32
            )
        total_ref[:, pl.ds(pl.multiple_of(pair * 128, 128), 128)] = result
        return 0

    lax.fori_loop(0, PAIRS, pair_step, 0)


def make_local(other, *arrays):
    outs = [pltpu.VMEM((TOK, HALF), F32)]
    if not other:
        outs.append(pltpu.VMEM((TOK, 256), F32))
    scratch = [pltpu.VMEM((TOK, TOK), F32), pltpu.VMEM((TOK, 128), F32), pltpu.VMEM((HEADS, TOK), F32)]
    return call(
        functools.partial(local_kernel, other), outs, arrays, "local",
        4 * TOK * TOK * HALF, HEADS // 2 * TOK * TOK, kept=(0, 2, 4), scratch=scratch,
    )


def duo_columns(packet_ref, duo):
    rows = duo * 256
    return jnp.concatenate([packet_ref[rows : rows + 128], packet_ref[rows + 128 : rows + 256]], axis=1)


def duo_spread(table, first):
    return jnp.concatenate([spread(table, first), spread(table, first + 2)], axis=1)


def level_term(level, half, duo, queries, packet_ref, weight_ref, gap):
    product = jnp.dot(queries, duo_columns(packet_ref, duo), preferred_element_type=F32)
    first = (level * HEADS) % 128 + half * (HEADS // 2) + duo * 4
    table = weight_ref[:, 0:128] if level < 4 else weight_ref[:, 128:256]
    return product * (duo_spread(table, first) * duo_spread(gap, duo * 4)[0:1])


def levels_kernel(other, wanted, total_ref, gap_ref, weight_ref, query_ref, *refs):
    packets, (out_ref, gap_out_ref) = refs[: len(wanted)], refs[len(wanted) :]
    bits = position()
    half = 1 - bits[0] if other else bits[0]
    queries = query_ref[...]
    gap, gaps = gap_ref[...], []
    for level, packet in zip(wanted, packets):
        gaps.append(jnp.exp(gap))
        gap = gap + read_total(packet[BODY:PACK]) * bits[level].astype(F32)
    gap_out_ref[...] = gap
    for duo in range(PAIRS // 2):
        lanes = pl.ds(duo * 256, 256)
        running = total_ref[:, lanes]
        for level, packet, before in zip(wanted, packets, gaps):
            running = running + level_term(level, half, duo, queries, packet, weight_ref, before)
        out_ref[:, lanes] = running


def add_levels(other, wanted, total, gap, weights, queries, *packets):
    outs = [pltpu.VMEM((TOK, HALF), F32), SUMS]
    return call(
        functools.partial(levels_kernel, other, wanted), outs, [total, gap, weights, queries, *packets], "levels",
        2 * len(wanted) * TOK * STATE * HALF, kept=(0, 1, 2, *range(4, 4 + len(wanted))), aliases={0: 0, 1: 1},
    )


def first_last_kernel(total_ref, gap_ref, weight_ref, query_ref, packet_ref, out_ref):
    half = position()[0]
    queries = query_ref[...]
    gap = jnp.exp(gap_ref[...])
    for duo in range(PAIRS // 2):
        lanes = pl.ds(duo * 256, 256)
        term = level_term(LEVELS - 1, half, duo, queries, packet_ref, weight_ref, gap)
        out_ref[:, lanes] = (total_ref[:, lanes] + term).astype(BF16)


def second_last_kernel(done_ref, total_ref, gap_ref, weight_ref, query_ref, packet_ref, out_ref, buffer, done_sem, sems):
    core = position()[0]
    half = 1 - core
    mine = pltpu.make_async_copy(
        done_ref, out_ref.at[:, pl.ds(pl.multiple_of(core * HALF, HALF), HALF)], done_sem
    )
    mine.start()
    queries = query_ref[...]
    gap = jnp.exp(gap_ref[...])
    copies = []
    for duo in range(PAIRS // 2):
        lanes = pl.ds(duo * 256, 256)
        term = level_term(LEVELS - 1, half, duo, queries, packet_ref, weight_ref, gap)
        buffer[duo] = (total_ref[:, lanes] + term).astype(BF16)
        columns = pl.ds(pl.multiple_of(half * HALF + duo * 256, 256), 256)
        copies.append(pltpu.make_async_copy(buffer.at[duo], out_ref.at[:, columns], sems.at[duo]))
        copies[-1].start()
    mine.wait()
    for copy in copies:
        copy.wait()


def body(inputs, write_keys, read_queries, decay_log, level_mix):
    devices = lax.axis_size("ctx")

    def swap(array, mask):
        return lax.ppermute(array, "ctx", [(i, i ^ mask) for i in range(devices)])

    def after(*arrays):
        return lax.optimization_barrier(arrays)

    masks = (1, 2, 6, 8, 24)
    sent, kept, decay, keys, x = call(
        ends_kernel,
        [PACKET, PACKET, pltpu.VMEM((HEADS, TOK), F32), pltpu.VMEM((TOK, STATE), BF16), pltpu.VMEM((TOK, 2 * HALF), BF16)],
        [decay_log, write_keys, inputs], "ends", 4 * TOK * STATE * HALF, 32768, far=(0, 1, 2),
        scratch=[pltpu.SemaphoreType.DMA((2,)), pltpu.SemaphoreType.DMA((4,))],
    )
    mine = [swap(sent, 1)]
    state, sums, packet = merge(0, kept, mine[0])
    got = swap(packet, masks[1])
    other = [swap(kept, 1)]
    total, weights = make_local(False, decay, level_mix, keys, read_queries, x)
    zero = jnp.zeros((8, 128), F32)
    got, total, weights = after(got, total, weights)
    mine.append(got)
    state, sums, packet = merge(1, state, sums, got)
    got = swap(packet, masks[2])
    other.append(swap(mine[1], 1))
    other_total, = make_local(True, decay, level_mix, keys, read_queries, x)
    got, other_total = after(got, other_total)
    mine.append(got)
    state, sums, packet = merge(2, state, sums, got)
    got = swap(packet, masks[3])
    other.append(swap(mine[2], 1))
    total, gap = add_levels(False, (0, 1, 2), total, zero, weights, read_queries, *mine)
    got, total, gap = after(got, total, gap)
    mine.append(got)
    state, sums, packet = merge(3, state, sums, got)
    got = swap(packet, masks[4])
    other.append(swap(mine[3], 1))
    total, gap = add_levels(False, (3,), total, gap, weights, read_queries, mine[3])
    other_total, other_gap = add_levels(True, (0, 1, 2, 3), other_total, zero, weights, read_queries, *other)
    got, total, gap, other_total, other_gap = after(got, total, gap, other_total, other_gap)
    got_other = swap(got, 1)
    flops = 2 * TOK * STATE * HALF
    done, = call(
        first_last_kernel, [pltpu.VMEM((TOK, HALF), BF16)], [total, gap, weights, read_queries, got], "last", flops,
        kept=(0, 1, 2, 4),
    )
    got_other, done = after(got_other, done)
    out, = call(
        second_last_kernel, [jax.ShapeDtypeStruct((TOK, 2 * HALF), BF16)],
        [done, other_total, other_gap, weights, read_queries, got_other], "last", flops, kept=(0, 1, 2, 3, 5),
        out_specs=[ANY],
        scratch=[
            pltpu.VMEM((PAIRS // 2, TOK, 256), BF16), pltpu.SemaphoreType.DMA, pltpu.SemaphoreType.DMA((PAIRS // 2,))
        ],
    )
    return out


def solution(mesh):
    placed = (
        P(("seq", "ctx"), None),
        P(("seq", "ctx"), None),
        P(("seq", "ctx"), None),
        P(None, ("seq", "ctx")),
        P(None, None, ("seq", "ctx")),
    )
    return jax.shard_map(
        body, mesh=mesh, in_specs=placed, out_specs=P(("seq", "ctx"), None), check_vma=False
    )
```

time: 217 us -> 46.3 us (0.21)
  the two profiles are of different devices: /device:TPU:31 before, /device:TPU:1 now
where the time goes in v2:
time: 46.3 us; the launch traced here: 46.1 us
  waiting for transfers between devices  16.9 us (37%)
  Pallas kernels  16.5 us (36%)
  starting transfers between devices  11.9 us (26%)
  local copies, waits for them, and re-layouts  0.71 us (2%)
    ppermute x10, waiting for transfers between devices, swap(): return lax.ppermute(array, 'ctx', [(i, i ^ mask) for i in range(devices)])  16.9 us
    pallas_call x12, Pallas kernels, call(): pl.pallas_call(kernel, out_shape=outs, in_specs=[ANY if place in far else...  16.5 us
    ppermute x10, starting transfers between devices, swap(): return lax.ppermute(array, 'ctx', [(i, i ^ mask) for i in range(devices)])  11.9 us
  transfers between devices with their start and end apart: 10, of which 6 were waited for; matrix products, arithmetic and copies ran while one was open for 0% of the time, Pallas kernels for 25%

profile of v2, /device:TPU:1, one launch (start us, length us, event | category | flops | bytes accessed | tf_op | source)
XLA Modules:
  0.0 46.1 jit_solution(11278173140798449713)
XLA Ops:
  0.0 3.2 %ends.1 = (bf16[1040,128]{1,0:T(8,128)(2,1)S(1)}, bf16[1040,128]{1,0:T(8,128)(2,1)S(1)}, f32[32,256]{1,0:T(8,128)S(1)}, bf16[256,128]{1,0:T(8,128)(2,1)S(1)}, bf16[256,2048]{1,0:T(8,128)(2,1)S(1)}) custom-call(f32[32,256]{1,0:T(8,128)} %decay_hbm.1, bf16[256,128]{1,0:T(8,128)(2,1)} %key_hbm.1, bf16[256,2048]{1,0:T(8,128)(2,1)} %x_hbm.1), custom_call_target="tpu_custom_call" | custom-call | flops 134217728 | bytes 1048576 | tf_op jit(solution)/shard_map/ends/pallas_call | solution.py:80
  3.2 3.3 %collective-permute-start = (bf16[1040,128]{1,0:T(8,128)(2,1)S(1)}, bf16[1040,128]{1,0:T(8,128)(2,1)S(1)}, u32[]{:S(2)}, u32[]{:S(2)}) collective-permute-start(bf16[1040,128]{1,0:T(8,128)(2,1)S(1)} %get-tuple-element.44), channel_id=1, source_target_pairs={{0,1},{1,0},{2,3},{3,2},{4,5},{5,4},{6,7},{7,6},{8,9},{9,8},{10,11... | collective-permute-start | bytes 798728 | tf_op jit(solution)/shard_map/ppermute | solution.py:290
  6.6 1.2 %collective-permute-done.refs_1_.refs_0_ = bf16[1040,128]{1,0:T(8,128)(2,1)S(1)} collective-permute-done((bf16[1040,128]{1,0:T(8,128)(2,1)S(1)}, bf16[1040,128]{1,0:T(8,128)(2,1)S(1)}, u32[]{:S(2)}, u32[]{:S(2)}) %collective-permute-start) | collective-permute-done | bytes 266272 | tf_op jit(solution)/shard_map/ppermute | solution.py:290
  7.7 0.2 merge.4
  7.9 0.1 collective-permute-start.1
  8.0 0.6 %copy-done = bf16[256,128]{1,0:T(8,128)(2,1)S(1)} copy-done((bf16[256,128]{1,0:T(8,128)(2,1)S(1)}, bf16[256,128]{1,0:T(8,128)(2,1)}, u32[]{:S(2)}) %copy-start) | copy-done | bytes 65560
  8.6 0.1 copy-done.1
  8.7 3.3 %local.2 = (f32[256,1024]{1,0:T(8,128)S(1)}, f32[256,256]{1,0:T(8,128)S(1)}) custom-call(f32[32,256]{1,0:T(8,128)S(1)} %get-tuple-element.48.decay_ref, f32[6,32,256]{2,1,0:T(8,128)S(1)} %copy-done.1, bf16[256,128]{1,0:T(8,128)(2,1)S(1)} %get-tuple-element.49.key_ref, bf16[256,128]{1,0:T(8,128)(2,1)S(1)} %copy-done, ...), custom_call_target="tpu_custom_call" | custom-call | flops 268435456 | bytes 1048576 | tf_op jit(solution)/shard_map/local/pallas_call | solution.py:80
  12.0 3.6 %collective-permute-done.1.refs_2_.refs_1_ = bf16[1040,128]{1,0:T(8,128)(2,1)S(1)} collective-permute-done((bf16[1040,128]{1,0:T(8,128)(2,1)S(1)}, bf16[1040,128]{1,0:T(8,128)(2,1)S(1)}, u32[]{:S(2)}, u32[]{:S(2)}) %collective-permute-start.1) | collective-permute-done | bytes 266272 | tf_op jit(solution)/shard_map/ppermute | solution.py:290
  15.6 0.1 merge.5
  15.8 0.8 %collective-permute-start.2 = (bf16[1040,128]{1,0:T(8,128)(2,1)S(1)}, bf16[1040,128]{1,0:T(8,128)(2,1)S(1)}, u32[]{:S(2)}, u32[]{:S(2)}) collective-permute-start(bf16[1040,128]{1,0:T(8,128)(2,1)S(1)} %get-tuple-element.56), channel_id=1, source_target_pairs={{0,6},{1,7},{2,4},{3,5},{4,2},{5,3},{6,0},{7,1},{8,14},{9,15},{10,... | collective-permute-start | bytes 798728 | tf_op jit(solution)/shard_map/ppermute | solution.py:290
  16.6 3.2 %local.3.total_ref = f32[256,1024]{1,0:T(8,128)S(1)} custom-call(f32[32,256]{1,0:T(8,128)S(1)} %get-tuple-element.48.decay_ref, f32[6,32,256]{2,1,0:T(8,128)S(1)} %copy-done.1, bf16[256,128]{1,0:T(8,128)(2,1)S(1)} %get-tuple-element.49.key_ref, bf16[256,128]{1,0:T(8,128)(2,1)S(1)} %copy-done, bf16[256,2048]{1,0:T(8,128)(2,1)S(1)} %get-tuple-element.50.x_ref), custom_call_target="tpu_custom_call" | custom-call | flops 268435456 | bytes 1048576 | tf_op jit(solution)/shard_map/local/pallas_call | solution.py:80
  19.8 3.9 %collective-permute-done.2.refs_2_ = bf16[1040,128]{1,0:T(8,128)(2,1)S(1)} collective-permute-done((bf16[1040,128]{1,0:T(8,128)(2,1)S(1)}, bf16[1040,128]{1,0:T(8,128)(2,1)S(1)}, u32[]{:S(2)}, u32[]{:S(2)}) %collective-permute-start.2) | collective-permute-done | bytes 266272 | tf_op jit(solution)/shard_map/ppermute | solution.py:290
  23.7 0.1 merge.6
  23.9 0.1 collective-permute-start.3
  24.0 2.2 %collective-permute-start.5 = (bf16[1040,128]{1,0:T(8,128)(2,1)S(1)}, bf16[1040,128]{1,0:T(8,128)(2,1)S(1)}, u32[]{:S(2)}, u32[]{:S(2)}) collective-permute-start(bf16[1040,128]{1,0:T(8,128)(2,1)S(1)} %get-tuple-element.43.refs_0_), channel_id=1, source_target_pairs={{0,1},{1,0},{2,3},{3,2},{4,5},{5,4},{6,7},{7,6},{8,9},{9,8},{10,11... | collective-permute-start | bytes 798728 | tf_op jit(solution)/shard_map/ppermute | solution.py:290
  26.2 0.1 collective-permute-start.6
  26.3 0.4 collective-permute-start.7
  26.7 1.3 %levels.3 = (f32[256,1024]{1,0:T(8,128)S(1)}, f32[8,128]{1,0:T(8,128)S(1)}) custom-call(f32[256,1024]{1,0:T(8,128)S(1)} %get-tuple-element.61.total_ref, f32[8,128]{1,0:T(8,128)S(1)} %broadcast_in_dim.3.clone.gap_ref, f32[256,256]{1,0:T(8,128)S(1)} %get-tuple-element.62.weight_ref, ...), custom_call_target="tpu_custom_call", output_to_operand_aliasing={{0}: (0, {}), {1}: (1, {})} | custom-call | flops 201326592 | bytes 1048576 | tf_op jit(solution)/shard_map/levels/pallas_call | solution.py:80
  28.1 1.7 %collective-permute-done.3.refs_2_.refs_0_ = bf16[1040,128]{1,0:T(8,128)(2,1)S(1)} collective-permute-done((bf16[1040,128]{1,0:T(8,128)(2,1)S(1)}, bf16[1040,128]{1,0:T(8,128)(2,1)S(1)}, u32[]{:S(2)}, u32[]{:S(2)}) %collective-permute-start.3) | collective-permute-done | bytes 266272 | tf_op jit(solution)/shard_map/ppermute | solution.py:290
  29.7 3.0 %collective-permute-start.8 = (bf16[1040,128]{1,0:T(8,128)(2,1)S(1)}, bf16[1040,128]{1,0:T(8,128)(2,1)S(1)}, u32[]{:S(2)}, u32[]{:S(2)}) collective-permute-start(bf16[1040,128]{1,0:T(8,128)(2,1)S(1)} %collective-permute-done.3.refs_2_.refs_0_), channel_id=1, source_target_pairs={{0,1},{1,0},{2,3},{3,2},{4,5},{5,4},{6,7},{7,6},{8,9},{9,8},{10,11... | collective-permute-start | bytes 798728 | tf_op jit(solution)/shard_map/ppermute | solution.py:290
  32.8 0.9 %merge.7 = (f32[1024,128]{1,0:T(8,128)}, f32[8,128]{1,0:T(8,128)}, bf16[1040,128]{1,0:T(8,128)(2,1)S(1)}) custom-call(f32[1024,128]{1,0:T(8,128)S(1)} %get-tuple-element.58.refs_0_, f32[8,128]{1,0:T(8,128)S(1)} %get-tuple-element.59.refs_1_, bf16[1040,128]{1,0:T(8,128)(2,1)S(1)} %collective-permute-done.3.refs_2_.refs_0_), custom_call_target="tpu_custom_call" | custom-call | flops 524288 | bytes 1048576 | tf_op jit(solution)/shard_map/merge/pallas_call | solution.py:80
  33.7 1.0 %collective-permute-start.4 = (bf16[1040,128]{1,0:T(8,128)(2,1)S(1)}, bf16[1040,128]{1,0:T(8,128)(2,1)S(1)}, u32[]{:S(2)}, u32[]{:S(2)}) collective-permute-start(bf16[1040,128]{1,0:T(8,128)(2,1)S(1)} %get-tuple-element.66), channel_id=1, source_target_pairs={{0,24},{1,25},{2,26},{3,27},{4,28},{5,29},{6,30},{7,31},{8,16},{9,... | collective-permute-start | bytes 798728 | tf_op jit(solution)/shard_map/ppermute | solution.py:290
  34.7 0.6 %levels.4 = (f32[256,1024]{1,0:T(8,128)S(1)}, f32[8,128]{1,0:T(8,128)S(1)}) custom-call(f32[256,1024]{1,0:T(8,128)S(1)} %get-tuple-element.67.total_ref, f32[8,128]{1,0:T(8,128)S(1)} %get-tuple-element.68.gap_ref, f32[256,256]{1,0:T(8,128)S(1)} %get-tuple-element.62.weight_ref, ...), custom_call_target="tpu_custom_call", output_to_operand_aliasing={{0}: (0, {}), {1}: (1, {})} | custom-call | flops 67108864 | bytes 1048576 | tf_op jit(solution)/shard_map/levels/pallas_call | solution.py:80
  35.3 0.0 collective-permute-done.5.refs_0_
  35.3 0.0 collective-permute-done.7.refs_2_
  35.4 1.7 %levels.5 = (f32[256,1024]{1,0:T(8,128)S(1)}, f32[8,128]{1,0:T(8,128)S(1)}) custom-call(f32[256,1024]{1,0:T(8,128)S(1)} %local.3.total_ref, f32[8,128]{1,0:T(8,128)S(1)} %broadcast_in_dim.3.gap_ref, f32[256,256]{1,0:T(8,128)S(1)} %get-tuple-element.62.weight_ref, bf16[256,128]{1,0:T(8,128)(2,1)S(1)} %copy-done, ...), custom_call_target="tpu_custom_call", output_to_operand_aliasing={{0}: (0, {}), {1}: (1, {})} | custom-call | flops 268435456 | bytes 1048576 | tf_op jit(solution)/shard_map/levels/pallas_call | solution.py:80
  37.1 5.9 %collective-permute-done.4.packet_ref = bf16[1040,128]{1,0:T(8,128)(2,1)S(1)} collective-permute-done((bf16[1040,128]{1,0:T(8,128)(2,1)S(1)}, bf16[1040,128]{1,0:T(8,128)(2,1)S(1)}, u32[]{:S(2)}, u32[]{:S(2)}) %collective-permute-start.4) | collective-permute-done | bytes 266272 | tf_op jit(solution)/shard_map/ppermute | solution.py:290
  43.0 0.8 %collective-permute-start.9 = (bf16[1040,128]{1,0:T(8,128)(2,1)S(1)}, bf16[1040,128]{1,0:T(8,128)(2,1)S(1)}, u32[]{:S(2)}, u32[]{:S(2)}) collective-permute-start(bf16[1040,128]{1,0:T(8,128)(2,1)S(1)} %collective-permute-done.4.packet_ref), channel_id=1, source_target_pairs={{0,1},{1,0},{2,3},{3,2},{4,5},{5,4},{6,7},{7,6},{8,9},{9,8},{10,11... | collective-permute-start | bytes 798728 | tf_op jit(solution)/shard_map/ppermute | solution.py:290
  43.8 0.5 %last.2.done_ref = bf16[256,1024]{1,0:T(8,128)(2,1)S(1)} custom-call(f32[256,1024]{1,0:T(8,128)S(1)} %get-tuple-element.75.total_ref, f32[8,128]{1,0:T(8,128)S(1)} %get-tuple-element.76.gap_ref, f32[256,256]{1,0:T(8,128)S(1)} %get-tuple-element.62.weight_ref, bf16[256,128]{1,0:T(8,128)(2,1)S(1)} %copy-done, ...), custom_call_target="tpu_custom_call" | custom-call | flops 67108864 | bytes 1048576 | tf_op jit(solution)/shard_map/last/pallas_call | solution.py:80
  44.3 0.6 %collective-permute-done.9.packet_ref = bf16[1040,128]{1,0:T(8,128)(2,1)S(1)} collective-permute-done((bf16[1040,128]{1,0:T(8,128)(2,1)S(1)}, bf16[1040,128]{1,0:T(8,128)(2,1)S(1)}, u32[]{:S(2)}, u32[]{:S(2)}) %collective-permute-start.9) | collective-permute-done | bytes 266272 | tf_op jit(solution)/shard_map/ppermute | solution.py:290
  44.9 1.2 %last.3 = bf16[256,2048]{1,0:T(8,128)(2,1)} custom-call(bf16[256,1024]{1,0:T(8,128)(2,1)S(1)} %last.2.done_ref, f32[256,1024]{1,0:T(8,128)S(1)} %get-tuple-element.78.total_ref, f32[8,128]{1,0:T(8,128)S(1)} %get-tuple-element.79.gap_ref, f32[256,256]{1,0:T(8,128)S(1)} %get-tuple-element.62.weight_ref, bf16[256,128]{1,0:T(8,128)(2,1)S(1)} %copy-done, ...), custom_call_target="tpu_custom_call" | custom-call | flops 67108864 | bytes 1048576 | tf_op jit(solution)/shard_map/last/pallas_call | solution.py:80
  (6 shorter events, 0.0 us)
Async XLA Ops:
  3.2 4.5 %collective-permute-start = (bf16[1040,128]{1,0:T(8,128)(2,1)S(1)}, bf16[1040,128]{1,0:T(8,128)(2,1)S(1)}, u32[]{:S(2)}, u32[]{:S(2)}) collective-permute-start(bf16[1040,128]{1,0:T(8,128)(2,1)S(1)} %get-tuple-element.44), channel_id=1, source_target_pairs={{0,1},{1,0},{2,3},{3,2},{4,5},{5,4},{6,7},{7,6},{8,9},{9,8},{10,11... | collective-permute-start | bytes 798728 | tf_op jit(solution)/shard_map/ppermute | solution.py:290
  7.7 0.8 %copy-start = (bf16[256,128]{1,0:T(8,128)(2,1)S(1)}, bf16[256,128]{1,0:T(8,128)(2,1)}, u32[]{:S(2)}) copy-start(bf16[256,128]{1,0:T(8,128)(2,1)} %query_ref.13) | copy-start | bytes 196612
  7.7 1.0 %copy-start.1 = (f32[6,32,256]{2,1,0:T(8,128)S(1)}, f32[6,32,256]{2,1,0:T(8,128)}, u32[]{:S(2)}) copy-start(f32[6,32,256]{2,1,0:T(8,128)} %mix_ref.3) | copy-start | bytes 589828
  7.9 7.7 %collective-permute-start.1 = (bf16[1040,128]{1,0:T(8,128)(2,1)S(1)}, bf16[1040,128]{1,0:T(8,128)(2,1)S(1)}, u32[]{:S(2)}, u32[]{:S(2)}) collective-permute-start(bf16[1040,128]{1,0:T(8,128)(2,1)S(1)} %get-tuple-element.47), channel_id=1, source_target_pairs={{0,2},{1,3},{2,0},{3,1},{4,6},{5,7},{6,4},{7,5},{8,10},{9,11},{10,... | collective-permute-start | bytes 798728 | tf_op jit(solution)/shard_map/ppermute | solution.py:290
  15.8 8.0 %collective-permute-start.2 = (bf16[1040,128]{1,0:T(8,128)(2,1)S(1)}, bf16[1040,128]{1,0:T(8,128)(2,1)S(1)}, u32[]{:S(2)}, u32[]{:S(2)}) collective-permute-start(bf16[1040,128]{1,0:T(8,128)(2,1)S(1)} %get-tuple-element.56), channel_id=1, source_target_pairs={{0,6},{1,7},{2,4},{3,5},{4,2},{5,3},{6,0},{7,1},{8,14},{9,15},{10,... | collective-permute-start | bytes 798728 | tf_op jit(solution)/shard_map/ppermute | solution.py:290
  23.9 5.9 %collective-permute-start.3 = (bf16[1040,128]{1,0:T(8,128)(2,1)S(1)}, bf16[1040,128]{1,0:T(8,128)(2,1)S(1)}, u32[]{:S(2)}, u32[]{:S(2)}) collective-permute-start(bf16[1040,128]{1,0:T(8,128)(2,1)S(1)} %get-tuple-element.60), channel_id=1, source_target_pairs={{0,8},{1,9},{2,10},{3,11},{4,12},{5,13},{6,14},{7,15},{8,0},{9,1},... | collective-permute-start | bytes 798728 | tf_op jit(solution)/shard_map/ppermute | solution.py:290
  24.0 11.3 %collective-permute-start.5 = (bf16[1040,128]{1,0:T(8,128)(2,1)S(1)}, bf16[1040,128]{1,0:T(8,128)(2,1)S(1)}, u32[]{:S(2)}, u32[]{:S(2)}) collective-permute-start(bf16[1040,128]{1,0:T(8,128)(2,1)S(1)} %get-tuple-element.43.refs_0_), channel_id=1, source_target_pairs={{0,1},{1,0},{2,3},{3,2},{4,5},{5,4},{6,7},{7,6},{8,9},{9,8},{10,11... | collective-permute-start | bytes 798728 | tf_op jit(solution)/shard_map/ppermute | solution.py:290
  26.2 9.1 %collective-permute-start.6 = (bf16[1040,128]{1,0:T(8,128)(2,1)S(1)}, bf16[1040,128]{1,0:T(8,128)(2,1)S(1)}, u32[]{:S(2)}, u32[]{:S(2)}) collective-permute-start(bf16[1040,128]{1,0:T(8,128)(2,1)S(1)} %collective-permute-done.1.refs_2_.refs_1_), channel_id=1, source_target_pairs={{0,1},{1,0},{2,3},{3,2},{4,5},{5,4},{6,7},{7,6},{8,9},{9,8},{10,11... | collective-permute-start | bytes 798728 | tf_op jit(solution)/shard_map/ppermute | solution.py:290
  26.3 9.0 %collective-permute-start.7 = (bf16[1040,128]{1,0:T(8,128)(2,1)S(1)}, bf16[1040,128]{1,0:T(8,128)(2,1)S(1)}, u32[]{:S(2)}, u32[]{:S(2)}) collective-permute-start(bf16[1040,128]{1,0:T(8,128)(2,1)S(1)} %collective-permute-done.2.refs_2_), channel_id=1, source_target_pairs={{0,1},{1,0},{2,3},{3,2},{4,5},{5,4},{6,7},{7,6},{8,9},{9,8},{10,11... | collective-permute-start | bytes 798728 | tf_op jit(solution)/shard_map/ppermute | solution.py:290
  29.7 5.6 %collective-permute-start.8 = (bf16[1040,128]{1,0:T(8,128)(2,1)S(1)}, bf16[1040,128]{1,0:T(8,128)(2,1)S(1)}, u32[]{:S(2)}, u32[]{:S(2)}) collective-permute-start(bf16[1040,128]{1,0:T(8,128)(2,1)S(1)} %collective-permute-done.3.refs_2_.refs_0_), channel_id=1, source_target_pairs={{0,1},{1,0},{2,3},{3,2},{4,5},{5,4},{6,7},{7,6},{8,9},{9,8},{10,11... | collective-permute-start | bytes 798728 | tf_op jit(solution)/shard_map/ppermute | solution.py:290
  33.7 9.2 %collective-permute-start.4 = (bf16[1040,128]{1,0:T(8,128)(2,1)S(1)}, bf16[1040,128]{1,0:T(8,128)(2,1)S(1)}, u32[]{:S(2)}, u32[]{:S(2)}) collective-permute-start(bf16[1040,128]{1,0:T(8,128)(2,1)S(1)} %get-tuple-element.66), channel_id=1, source_target_pairs={{0,24},{1,25},{2,26},{3,27},{4,28},{5,29},{6,30},{7,31},{8,16},{9,... | collective-permute-start | bytes 798728 | tf_op jit(solution)/shard_map/ppermute | solution.py:290
  43.0 2.0 %collective-permute-start.9 = (bf16[1040,128]{1,0:T(8,128)(2,1)S(1)}, bf16[1040,128]{1,0:T(8,128)(2,1)S(1)}, u32[]{:S(2)}, u32[]{:S(2)}) collective-permute-start(bf16[1040,128]{1,0:T(8,128)(2,1)S(1)} %collective-permute-done.4.packet_ref), channel_id=1, source_target_pairs={{0,1},{1,0},{2,3},{3,2},{4,5},{5,4},{6,7},{7,6},{8,9},{9,8},{10,11... | collective-permute-start | bytes 798728 | tf_op jit(solution)/shard_map/ppermute | solution.py:290

commit v3 on v2

v3 whole, which is shorter than its diff:
```python
import functools

import jax
import jax.numpy as jnp
from jax import lax
from jax.experimental import pallas as pl
from jax.experimental.pallas import tpu as pltpu
from jax.sharding import PartitionSpec as P

HEADS = 32
HEAD = 64
STATE = 128
TOK = 256
LEVELS = 5
SHARE = HEADS // 2
CHUNKS = 2
PAIRS = SHARE // 2 // CHUNKS
WIDTH = PAIRS * 128
BODY = PAIRS * STATE
PACK = BODY + 16
LOG2E = 1.4426950408889634
F32 = jnp.float32
BF16 = jnp.bfloat16
VMEM = pl.BlockSpec(memory_space=pltpu.VMEM)
ANY = pl.BlockSpec(memory_space=pl.ANY)
KEPT = pltpu.MemorySpace.VMEM
PACKET = pltpu.VMEM((PACK, 128), BF16)
SUMS = pltpu.VMEM((8, 128), F32)
TABLE = pltpu.VMEM((TOK, 128), F32)
PART = pltpu.VMEM((TOK, WIDTH), F32)
X_PART = pltpu.VMEM((2, TOK, WIDTH), BF16)


def split3(value):
    high = value.astype(BF16)
    rest = value - high.astype(F32)
    middle = rest.astype(BF16)
    low = (rest - middle.astype(F32)).astype(BF16)
    return high, middle, low


def exact_dot(zero_one, value, dims):
    return sum(
        lax.dot_general(zero_one, part, (dims, ((), ())), preferred_element_type=F32) for part in split3(value)
    )


def pad_heads(value):
    return jnp.concatenate([value, jnp.zeros((128 - HEADS, value.shape[1]), F32)], axis=0)


def spread(table, first):
    lane = lax.broadcasted_iota(jnp.int32, table.shape, 1)
    return jnp.take_along_axis(table, jnp.where(lane < HEAD, first, first + 1), axis=1)


def triangle(compare):
    rows = lax.broadcasted_iota(jnp.int32, (TOK, TOK), 0)
    columns = lax.broadcasted_iota(jnp.int32, (TOK, TOK), 1)
    return compare(rows, columns).astype(F32).astype(BF16)


def total_rows(sums):
    row = lax.broadcasted_iota(jnp.int32, sums.shape, 0)
    high, middle, low = (part.astype(F32) for part in split3(sums))
    rows = jnp.where(row == 0, high, jnp.where(row == 1, middle, jnp.where(row == 2, low, 0.0)))
    return rows.astype(BF16)


def read_total(rows):
    return jnp.sum(rows.astype(F32), axis=0, keepdims=True)


def position():
    index = lax.axis_index("ctx")
    return [(index >> bit) & 1 for bit in range(LEVELS)]


def call(kernel, outs, arrays, name, flops, exps=0, kept=(), far=(), out_specs=None, scratch=(), aliases=None):
    arrays = list(arrays)
    for place in kept:
        arrays[place] = pltpu.with_memory_space_constraint(arrays[place], KEPT)
    for place in far:
        arrays[place] = pltpu.with_memory_space_constraint(arrays[place], pltpu.MemorySpace.HBM)
    return pl.pallas_call(
        kernel,
        out_shape=outs,
        in_specs=[ANY if place in far else VMEM for place in range(len(arrays))],
        out_specs=out_specs or [VMEM] * len(outs),
        scratch_shapes=list(scratch),
        input_output_aliases=aliases or {},
        compiler_params=pltpu.CompilerParams(vmem_limit_bytes=20 << 20),
        cost_estimate=pl.CostEstimate(flops=flops, bytes_accessed=1 << 20, transcendentals=exps),
        name=name,
    )(*arrays)


def ends_kernel(chunk, *refs):
    core = position()[0]
    if chunk == 0:
        decay_hbm, key_hbm, x_hbm, sent_ref, kept_ref, x_ref, decay_ref, key_ref, factor_ref, sum_ref, small, big = refs
    else:
        x_hbm, key_ref, factor_ref, sum_ref, sent_ref, kept_ref, x_ref, big = refs
    halves = (1 - core, core)
    copies = []
    if chunk == 0:
        copies.append(pltpu.make_async_copy(decay_hbm, decay_ref, small.at[0]))
        copies.append(pltpu.make_async_copy(key_hbm, key_ref, small.at[1]))
    for place, half in enumerate(halves):
        columns = pl.ds(pl.multiple_of(half * (CHUNKS * WIDTH) + chunk * WIDTH, WIDTH), WIDTH)
        copies.append(pltpu.make_async_copy(x_hbm.at[:, columns], x_ref.at[place], big.at[place]))
    for copy in copies:
        copy.start()
    if chunk == 0:
        copies[0].wait()
        decay = pad_heads(decay_ref[...])
        after = exact_dot(triangle(lambda r, c: c > r), decay, ((1,), (1,)))
        sums = exact_dot(jnp.ones((16, TOK), BF16), decay, ((1,), (1,)))
        factor = jnp.exp(after)
        factor_ref[...] = factor
        sum_ref[...] = sums
        copies[1].wait()
    else:
        factor = factor_ref[...]
        sums = sum_ref[...]
    lane = lax.broadcasted_iota(jnp.int32, sums.shape, 1)
    keys = key_ref[...]
    for place, (half, packet_ref) in enumerate(zip(halves, (sent_ref, kept_ref))):
        packet_ref[BODY:PACK] = total_rows(jnp.take_along_axis(sums, (lane + half * SHARE) & 127, axis=1))
        copies[place - 2].wait()
        for duo in range(PAIRS // 2):
            pieces = []
            for pair in (2 * duo, 2 * duo + 1):
                x = x_ref[place, :, pair * 128 : pair * 128 + 128].astype(F32)
                pieces.append((x * spread(factor, half * SHARE + (chunk * PAIRS + pair) * 2)).astype(BF16))
            decayed = jnp.concatenate(pieces, axis=1)
            state = lax.dot_general(keys, decayed, (((0,), (0,)), ((), ())), preferred_element_type=F32)
            packet_ref[duo * 256 : duo * 256 + 128] = state[:, 0:128].astype(BF16)
            packet_ref[duo * 256 + 128 : duo * 256 + 256] = state[:, 128:256].astype(BF16)


def merge_kernel(bit, chunk, *refs):
    state_ref = sum_ref = None
    if bit == 0:
        own_ref, got_ref, packet_ref, state_ref, sum_ref = refs
        own_sum = read_total(own_ref[BODY:PACK])
    else:
        own_ref, own_sum_ref, got_ref, packet_ref = refs[:4]
        own_sum = own_sum_ref[0:1]
        if bit < LEVELS - 2:
            state_ref, sum_ref = refs[4:]
    right = position()[bit] == 1
    got_sum = read_total(got_ref[BODY:PACK])
    decay = jnp.broadcast_to(jnp.exp(jnp.where(right, own_sum, got_sum)), (8, 128))
    sums = own_sum + got_sum
    if sum_ref is not None:
        sum_ref[...] = jnp.broadcast_to(sums, (8, 128))
    packet_ref[BODY:PACK] = total_rows(jnp.broadcast_to(sums, (16, 128)))
    for pair in range(PAIRS):
        rows = pl.ds(pair * STATE, STATE)
        own = own_ref[rows].astype(F32)
        got = got_ref[rows].astype(F32)
        factor = spread(decay, 2 * (chunk * PAIRS + pair))[0:1]
        state = jnp.where(right, got, own) * factor + jnp.where(right, own, got)
        if state_ref is not None:
            state_ref[rows] = state
        packet_ref[rows] = state.astype(BF16)


def merge(bit, chunk, *arrays):
    outs = [PACKET] + ([pltpu.VMEM((BODY, 128), F32), SUMS] if bit < LEVELS - 2 else [])
    return call(
        functools.partial(merge_kernel, bit, chunk), outs, arrays, "merge", 1 << 19, 4096, range(len(arrays))
    )


def tables_kernel(decay_ref, mix_ref, key_ref, query_ref, scores_ref, column_ref, row_ref, own_ref, sent_ref):
    bits = position()
    core = bits[0]
    decay = decay_ref[...]
    causal = triangle(lambda r, c: r >= c)
    cum_column = exact_dot(causal, pad_heads(decay), ((1,), (1,)))
    cum_row = cum_column.T[0:HEADS]
    row_ref[...] = cum_row * LOG2E
    mix = jnp.concatenate([mix_ref[0], jnp.ones((128 - HEADS, TOK), F32)], axis=0)
    column_ref[...] = (cum_column + jnp.log(mix).T) * LOG2E
    gate = jnp.exp(cum_row)
    weights = [mix_ref[level + 1] * gate * bits[level].astype(F32) for level in range(LEVELS)]
    unused = [jnp.zeros((128 - SHARE * LEVELS, TOK), F32)]
    low = jnp.concatenate([weight[:SHARE] for weight in weights] + unused, axis=0).T
    high = jnp.concatenate([weight[SHARE:] for weight in weights] + unused, axis=0).T
    own_ref[...] = jnp.where(core == 0, low, high)
    sent_ref[...] = jnp.where(core == 0, high, low)
    raw = lax.dot_general(query_ref[...], key_ref[...], (((1,), (1,)), ((), ())), preferred_element_type=F32)
    scores_ref[...] = raw * causal.astype(F32)


def local_kernel(place, chunk, scores_ref, column_ref, row_ref, x_ref, total_ref):
    core = position()[0]
    half = core if place == 1 else 1 - core
    upper = TOK // 2
    lane = lax.broadcasted_iota(jnp.int32, (TOK, 128), 1)

    def pair_step(pair, _):
        offset = pl.multiple_of(pair * 128, 128)
        x = x_ref[place, :, pl.ds(offset, 128)]
        top = jnp.zeros((upper, 128), F32)
        bottom = jnp.zeros((upper, 128), F32)
        for side in range(2):
            head = half * SHARE + (chunk * PAIRS + pair) * 2 + side
            column = jnp.take_along_axis(column_ref[...], jnp.full((TOK, 128), head, jnp.int32), axis=1)
            row = row_ref[pl.ds(head, 1)]
            chosen = jnp.where((lane < HEAD) == (side == 0), x, jnp.zeros_like(x))
            gap = column[:upper] - row[:, :upper]
            mixing = (scores_ref[:upper, :upper] * jnp.exp2(jnp.minimum(gap, 1.0))).astype(BF16)
            top = top + jnp.dot(mixing, chosen[:upper], preferred_element_type=F32)
            below = column[upper:]
            gap = jnp.concatenate([below, below], axis=1) - row
            mixing = (scores_ref[upper:] * jnp.exp2(jnp.minimum(gap, 1.0))).astype(BF16)
            bottom = bottom + jnp.dot(mixing, chosen, preferred_element_type=F32)
        total_ref[:upper, pl.ds(offset, 128)] = top
        total_ref[upper:, pl.ds(offset, 128)] = bottom
        return 0

    lax.fori_loop(0, PAIRS, pair_step, 0)


def make_local(place, chunk, *arrays):
    return call(
        functools.partial(local_kernel, place, chunk), [PART], arrays, "local", 4 * TOK * TOK * WIDTH,
        2 * PAIRS * TOK * TOK, kept=range(4),
    )[0]


def duo_columns(packet_ref, duo):
    rows = duo * 256
    return jnp.concatenate([packet_ref[rows : rows + 128], packet_ref[rows + 128 : rows + 256]], axis=1)


def duo_spread(table, first):
    return jnp.concatenate([spread(table, first), spread(table, first + 2)], axis=1)


def level_term(level, chunk, duo, queries, packet_ref, weight_ref, gap):
    product = jnp.dot(queries, duo_columns(packet_ref, duo), preferred_element_type=F32)
    pair = chunk * PAIRS + duo * 2
    return product * (duo_spread(weight_ref[...], level * SHARE + pair * 2) * duo_spread(gap, pair * 2)[0:1])


def levels_kernel(wanted, chunk, *refs):
    bits = position()
    weight_refs, query_refs = refs[0:2], refs[2:4]
    if wanted[0] == 0:
        total_ref, kept_ref, *packets = refs[4:-4]
        totals = (total_ref, None)
        gaps = [jnp.zeros((8, 128), F32)] * 2
    else:
        totals, gaps, packets = refs[4:6], [refs[6][...], refs[7][...]], refs[8:-4]
        kept_ref = None
    outs, gap_outs = refs[-4:-2], refs[-2:]
    for side in range(2):
        queries = query_refs[side][...]
        used = [kept_ref if side == 1 and level == 0 else packet for level, packet in zip(wanted, packets)]
        gap, before = gaps[side], []
        for level, packet in zip(wanted, used):
            before.append(jnp.exp(gap))
            bit = 1 - bits[0] if side == 1 and level == 0 else bits[level]
            gap = gap + read_total(packet[BODY:PACK]) * bit.astype(F32)
        gap_outs[side][...] = gap
        for duo in range(PAIRS // 2):
            lanes = slice(duo * 256, duo * 256 + 256)
            running = None if totals[side] is None else totals[side][:, lanes]
            for level, packet, factor in zip(wanted, used, before):
                term = level_term(level, chunk, duo, queries, packet, weight_refs[side], factor)
                running = term if running is None else running + term
            outs[side][:, lanes] = running


def add_levels(wanted, chunk, *arrays):
    return call(
        functools.partial(levels_kernel, wanted, chunk), [PART, PART, SUMS, SUMS], arrays, "levels",
        4 * len(wanted) * TOK * STATE * WIDTH, kept=range(len(arrays)),
    )


def last_kernel(chunk, weight_ref, query_ref, total_ref, gap_ref, packet_ref, out_ref):
    queries = query_ref[...]
    gap = jnp.exp(gap_ref[...])
    for duo in range(PAIRS // 2):
        lanes = slice(duo * 256, duo * 256 + 256)
        term = level_term(LEVELS - 1, chunk, duo, queries, packet_ref, weight_ref, gap)
        out_ref[:, lanes] = (total_ref[:, lanes] + term).astype(BF16)


def add_last(chunk, *arrays):
    return call(
        functools.partial(last_kernel, chunk), [pltpu.VMEM((TOK, WIDTH), BF16)], arrays, "last",
        2 * TOK * STATE * WIDTH, kept=range(5),
    )[0]


def finish_kernel(*refs):
    done, totals, parts = refs[:CHUNKS], refs[CHUNKS : 2 * CHUNKS], refs[2 * CHUNKS : 3 * CHUNKS]
    out_ref, buffer, sems = refs[3 * CHUNKS :]
    core = position()[0]
    copies = []

    def send(source, half, chunk):
        columns = pl.ds(pl.multiple_of(half * (CHUNKS * WIDTH) + chunk * WIDTH, WIDTH), WIDTH)
        copies.append(pltpu.make_async_copy(source, out_ref.at[:, columns], sems.at[len(copies)]))
        copies[-1].start()

    for chunk in range(CHUNKS):
        send(done[chunk], core, chunk)
    for chunk in range(CHUNKS):
        buffer[chunk] = (totals[chunk][...] + parts[chunk][...].astype(F32)).astype(BF16)
        send(buffer.at[chunk], 1 - core, chunk)
    for copy in copies:
        copy.wait()


def body(inputs, write_keys, read_queries, decay_log, level_mix):
    devices = lax.axis_size("ctx")

    def swap(array, mask):
        return lax.ppermute(array, "ctx", [(i, i ^ mask) for i in range(devices)])

    def after(*arrays):
        return lax.optimization_barrier(arrays)

    chunks = range(CHUNKS)
    masks = (1, 2, 6, 8, 24)
    kept, x, got, state, packet = ([None] * CHUNKS for _ in range(5))
    history = [[] for _ in chunks]
    for c in chunks:
        semaphores = pltpu.SemaphoreType.DMA((2,))
        kernel, flops = functools.partial(ends_kernel, c), 4 * TOK * STATE * WIDTH
        if c == 0:
            sent, kept[c], x[c], decay, keys, factor, sums = call(
                kernel,
                [
                    PACKET, PACKET, X_PART, pltpu.VMEM((HEADS, TOK), F32), pltpu.VMEM((TOK, STATE), BF16), TABLE,
                    pltpu.VMEM((16, 128), F32),
                ],
                [decay_log, write_keys, inputs], "ends", flops, 32768, far=(0, 1, 2), scratch=[semaphores, semaphores],
            )
        else:
            sent, kept[c], x[c] = call(
                kernel, [PACKET, PACKET, X_PART], [inputs, keys, factor, sums], "ends", flops, far=(0,),
                kept=(1, 2, 3), scratch=[semaphores],
            )
        got[c] = swap(sent, masks[0])

    def advance(level, c):
        history[c].append(got[c])
        if level == 0:
            packet[c], *state[c] = merge(0, c, kept[c], got[c])
        else:
            packet[c], *state[c] = merge(level, c, *state[c], got[c])
        got[c] = swap(packet[c], masks[level + 1])

    for c in chunks:
        advance(0, c)
    queries, level_mix, _ = after(read_queries, level_mix, packet[-1])
    scores, column, row, weights, sent = call(
        tables_kernel, [pltpu.VMEM((TOK, TOK), F32), TABLE, pltpu.VMEM((HEADS, TOK), F32), TABLE, TABLE],
        [decay, level_mix, keys, queries], "tables", 4 * TOK * TOK * STATE, 16384, kept=(0, 1, 2, 3),
    )
    far_weights, far_queries = swap(sent, 1), swap(queries, 1)
    total, rest = [None] * CHUNKS, [None] * CHUNKS
    for level, place, results in ((1, 1, total), (2, 0, rest)):
        for c in chunks:
            results[c] = make_local(place, c, scores, column, row, x[c])
            got[c], results[c] = after(got[c], results[c])
            advance(level, c)
    shared = (weights, far_weights, queries, far_queries)
    far_total, gap, far_gap = [None] * CHUNKS, [None] * CHUNKS, [None] * CHUNKS
    for c in chunks:
        total[c], far_total[c], gap[c], far_gap[c] = add_levels((0, 1, 2), c, *shared, total[c], kept[c], *history[c])
        got[c], total[c] = after(got[c], total[c])
        advance(3, c)
    done, parts = [None] * CHUNKS, [None] * CHUNKS
    for c in chunks:
        total[c], far_total[c], gap[c], far_gap[c] = add_levels(
            (3,), c, *shared, total[c], far_total[c], gap[c], far_gap[c], history[c][3]
        )
        got[c], total[c] = after(got[c], total[c])
        part = add_last(c, far_weights, far_queries, far_total[c], far_gap[c], got[c])
        parts[c] = swap(part, 1)
        late, _ = after(got[c], part)
        done[c] = add_last(c, weights, queries, total[c], gap[c], late)
        parts[c], done[c] = after(parts[c], done[c])
    out, = call(
        finish_kernel, [jax.ShapeDtypeStruct((TOK, HEADS * HEAD), BF16)], [*done, *rest, *parts], "finish",
        TOK * CHUNKS * WIDTH, kept=range(3 * CHUNKS), out_specs=[ANY],
        scratch=[pltpu.VMEM((CHUNKS, TOK, WIDTH), BF16), pltpu.SemaphoreType.DMA((2 * CHUNKS,))],
    )
    return out


def solution(mesh):
    placed = (
        P(("seq", "ctx"), None),
        P(("seq", "ctx"), None),
        P(("seq", "ctx"), None),
        P(None, ("seq", "ctx")),
        P(None, None, ("seq", "ctx")),
    )
    return jax.shard_map(
        body, mesh=mesh, in_specs=placed, out_specs=P(("seq", "ctx"), None), check_vma=False
    )
```

time: 46.3 us -> 42.4 us (0.916)
  waiting for transfers between devices: 16.9 us -> 6 us
  starting transfers between devices: 11.9 us -> 19.1 us
  local copies, waits for them, and re-layouts: 0.71 us -> 0.01 us
    ppermute x10 -> x14, waiting for transfers between devices: 16.9 us -> 6 us  [swap(): return lax.ppermute(array, 'ctx', [(i, i ^ mask) for i in range(devices)])]
    ppermute x10 -> x14, starting transfers between devices: 11.9 us -> 19.1 us  [swap(): return lax.ppermute(array, 'ctx', [(i, i ^ mask) for i in range(devices)])]
    unnamed x4, local copies, waits for them, and re-layouts: 0.7 us -> 0.01 us
    pallas_call x12 -> x24, Pallas kernels: 16.5 us -> 16.7 us  [call(): pl.pallas_call(kernel, out_shape=outs, in_specs=[ANY if place in far else...]
  transfers between devices with their start and end apart: 10 -> 14, of which waited for: 6 -> 8; matrix products, arithmetic and copies ran while one was open for 0% -> 0% of each run, Pallas kernels for 25% -> 27%
where the time goes in v3:
time: 42.4 us; the launch traced here: 42.2 us
  starting transfers between devices  19.1 us (45%)
  Pallas kernels  16.7 us (39%)
  waiting for transfers between devices  6 us (14%)
    ppermute x14, starting transfers between devices, swap(): return lax.ppermute(array, 'ctx', [(i, i ^ mask) for i in range(devices)])  19.1 us
    pallas_call x24, Pallas kernels, call(): pl.pallas_call(kernel, out_shape=outs, in_specs=[ANY if place in far else...  16.7 us
    ppermute x14, waiting for transfers between devices, swap(): return lax.ppermute(array, 'ctx', [(i, i ^ mask) for i in range(devices)])  6 us
  transfers between devices with their start and end apart: 14, of which 8 were waited for; matrix products, arithmetic and copies ran while one was open for 0% of the time, Pallas kernels for 27%

profile of v3, /device:TPU:1, one launch (start us, length us, event | category | flops | bytes accessed | tf_op | source)
XLA Modules:
  0.0 42.2 jit_solution(1999795084711098883)
XLA Ops:
  0.0 2.2 %ends.2 = (bf16[528,128]{1,0:T(8,128)(2,1)S(1)}, bf16[528,128]{1,0:T(8,128)(2,1)S(1)}, bf16[2,256,512]{2,1,0:T(8,128)(2,1)S(1)}, f32[32,256]{1,0:T(8,128)S(1)}, ...) custom-call(f32[32,256]{1,0:T(8,128)} %refs_0_.2, bf16[256,128]{1,0:T(8,128)(2,1)} %refs_1_.1, ...), custom_call_target="tpu_custom_call" | custom-call | flops 67108864 | bytes 1048576 | tf_op jit(solution)/shard_map/ends/pallas_call | solution.py:85
  2.2 2.0 %ends.3 = (bf16[528,128]{1,0:T(8,128)(2,1)S(1)}, bf16[528,128]{1,0:T(8,128)(2,1)S(1)}, bf16[2,256,512]{2,1,0:T(8,128)(2,1)S(1)}) custom-call(bf16[256,2048]{1,0:T(8,128)(2,1)} %refs_0_.3, bf16[256,128]{1,0:T(8,128)(2,1)S(1)} %get-tuple-element.79.refs_1_.key_ref, f32[256,128]{1,0:T(8,128)S(1)} %get-tuple-element.80.refs_2_, ...), custom_call_target="tpu_custom_call" | custom-call | flops 67108864 | bytes 1048576 | tf_op jit(solution)/shard_map/ends/pallas_call | solution.py:85
  4.2 3.3 %collective-permute-start = (bf16[528,128]{1,0:T(8,128)(2,1)S(1)}, bf16[528,128]{1,0:T(8,128)(2,1)S(1)}, u32[]{:S(2)}, u32[]{:S(2)}) collective-permute-start(bf16[528,128]{1,0:T(8,128)(2,1)S(1)} %get-tuple-element.83), channel_id=1, source_target_pairs={{0,1},{1,0},{2,3},{3,2},{4,5},{5,4},{6,7},{7,6},{8,9},{9,8},{10,11... | collective-permute-start | bytes 405512 | tf_op jit(solution)/shard_map/ppermute | solution.py:326
  7.6 0.9 %collective-permute-done.refs_1_.refs_6_ = bf16[528,128]{1,0:T(8,128)(2,1)S(1)} collective-permute-done((bf16[528,128]{1,0:T(8,128)(2,1)S(1)}, bf16[528,128]{1,0:T(8,128)(2,1)S(1)}, u32[]{:S(2)}, u32[]{:S(2)}) %collective-permute-start) | collective-permute-done | bytes 135200 | tf_op jit(solution)/shard_map/ppermute | solution.py:326
  9.0 1.4 %collective-permute-start.4 = (bf16[528,128]{1,0:T(8,128)(2,1)S(1)}, bf16[528,128]{1,0:T(8,128)(2,1)S(1)}, u32[]{:S(2)}, u32[]{:S(2)}) collective-permute-start(bf16[528,128]{1,0:T(8,128)(2,1)S(1)} %get-tuple-element.93), channel_id=1, source_target_pairs={{0,2},{1,3},{2,0},{3,1},{4,6},{5,7},{6,4},{7,5},{8,10},{9,11},{10,... | collective-permute-start | bytes 405512 | tf_op jit(solution)/shard_map/ppermute | solution.py:326
  10.4 0.5 %tables.1 = (f32[256,256]{1,0:T(8,128)S(1)}, f32[256,128]{1,0:T(8,128)S(1)}, f32[32,256]{1,0:T(8,128)S(1)}, f32[256,128]{1,0:T(8,128)S(1)}, f32[256,128]{1,0:T(8,128)S(1)}) custom-call(f32[32,256]{1,0:T(8,128)S(1)} %get-tuple-element.78.decay_ref, f32[6,32,256]{2,1,0:T(8,128)S(1)} %copy-done.1, bf16[256,128]{1,0:T(8,128)(2,1)S(1)} %get-tuple-element.79.refs_1_.key_ref, ...), custom_call_target="tpu_custom_call" | custom-call | flops 33554432 | bytes 1048576 | tf_op jit(solution)/shard_map/tables/pallas_call | solution.py:85
  10.9 1.4 %local.6.refs_4_ = f32[256,512]{1,0:T(8,128)S(1)} custom-call(f32[256,256]{1,0:T(8,128)S(1)} %get-tuple-element.94.scores_ref, f32[256,128]{1,0:T(8,128)S(1)} %get-tuple-element.95.column_ref, f32[32,256]{1,0:T(8,128)S(1)} %get-tuple-element.96.row_ref, bf16[2,256,512]{2,1,0:T(8,128)(2,1)S(1)} %get-tuple-element.123.x_ref), custom_call_target="tpu_custom_call" | custom-call | flops 134217728 | bytes 1048576 | tf_op jit(solution)/shard_map/local/pallas_call | solution.py:85
  12.3 1.3 %collective-permute-done.9.refs_2_.refs_7_ = bf16[528,128]{1,0:T(8,128)(2,1)S(1)} collective-permute-done((bf16[528,128]{1,0:T(8,128)(2,1)S(1)}, bf16[528,128]{1,0:T(8,128)(2,1)S(1)}, u32[]{:S(2)}, u32[]{:S(2)}) %collective-permute-start.9) | collective-permute-done | bytes 135200 | tf_op jit(solution)/shard_map/ppermute | solution.py:326
  13.7 0.8 %collective-permute-start.10 = (bf16[528,128]{1,0:T(8,128)(2,1)S(1)}, bf16[528,128]{1,0:T(8,128)(2,1)S(1)}, u32[]{:S(2)}, u32[]{:S(2)}) collective-permute-start(bf16[528,128]{1,0:T(8,128)(2,1)S(1)} %get-tuple-element.127), channel_id=1, source_target_pairs={{0,6},{1,7},{2,4},{3,5},{4,2},{5,3},{6,0},{7,1},{8,14},{9,15},{10,... | collective-permute-start | bytes 405512 | tf_op jit(solution)/shard_map/ppermute | solution.py:326
  14.5 1.4 %local.4.refs_4_ = f32[256,512]{1,0:T(8,128)S(1)} custom-call(f32[256,256]{1,0:T(8,128)S(1)} %get-tuple-element.94.scores_ref, f32[256,128]{1,0:T(8,128)S(1)} %get-tuple-element.95.column_ref, f32[32,256]{1,0:T(8,128)S(1)} %get-tuple-element.96.row_ref, bf16[2,256,512]{2,1,0:T(8,128)(2,1)S(1)} %get-tuple-element.97.x_ref), custom_call_target="tpu_custom_call" | custom-call | flops 134217728 | bytes 1048576 | tf_op jit(solution)/shard_map/local/pallas_call | solution.py:85
  15.9 0.6 %collective-permute-done.4.refs_2_.refs_7_ = bf16[528,128]{1,0:T(8,128)(2,1)S(1)} collective-permute-done((bf16[528,128]{1,0:T(8,128)(2,1)S(1)}, bf16[528,128]{1,0:T(8,128)(2,1)S(1)}, u32[]{:S(2)}, u32[]{:S(2)}) %collective-permute-start.4) | collective-permute-done | bytes 135200 | tf_op jit(solution)/shard_map/ppermute | solution.py:326
  16.6 1.5 %collective-permute-start.5 = (bf16[528,128]{1,0:T(8,128)(2,1)S(1)}, bf16[528,128]{1,0:T(8,128)(2,1)S(1)}, u32[]{:S(2)}, u32[]{:S(2)}) collective-permute-start(bf16[528,128]{1,0:T(8,128)(2,1)S(1)} %get-tuple-element.101), channel_id=1, source_target_pairs={{0,6},{1,7},{2,4},{3,5},{4,2},{5,3},{6,0},{7,1},{8,14},{9,15},{10,... | collective-permute-start | bytes 405512 | tf_op jit(solution)/shard_map/ppermute | solution.py:326
  18.0 2.5 %collective-permute-start.1 = (f32[256,128]{1,0:T(8,128)S(1)}, f32[256,128]{1,0:T(8,128)S(1)}, u32[]{:S(2)}, u32[]{:S(2)}) collective-permute-start(f32[256,128]{1,0:T(8,128)S(1)} %get-tuple-element.87), channel_id=1, source_target_pairs={{0,1},{1,0},{2,3},{3,2},{4,5},{5,4},{6,7},{7,6},{8,9},{9,8},{10,11... | collective-permute-start | bytes 393224 | tf_op jit(solution)/shard_map/ppermute | solution.py:326
  20.6 1.4 %local.7.refs_3_ = f32[256,512]{1,0:T(8,128)S(1)} custom-call(f32[256,256]{1,0:T(8,128)S(1)} %get-tuple-element.94.scores_ref, f32[256,128]{1,0:T(8,128)S(1)} %get-tuple-element.95.column_ref, f32[32,256]{1,0:T(8,128)S(1)} %get-tuple-element.96.row_ref, bf16[2,256,512]{2,1,0:T(8,128)(2,1)S(1)} %get-tuple-element.123.x_ref), custom_call_target="tpu_custom_call" | custom-call | flops 134217728 | bytes 1048576 | tf_op jit(solution)/shard_map/local/pallas_call | solution.py:85
  22.2 1.4 %local.5.refs_2_ = f32[256,512]{1,0:T(8,128)S(1)} custom-call(f32[256,256]{1,0:T(8,128)S(1)} %get-tuple-element.94.scores_ref, f32[256,128]{1,0:T(8,128)S(1)} %get-tuple-element.95.column_ref, f32[32,256]{1,0:T(8,128)S(1)} %get-tuple-element.96.row_ref, bf16[2,256,512]{2,1,0:T(8,128)(2,1)S(1)} %get-tuple-element.97.x_ref), custom_call_target="tpu_custom_call" | custom-call | flops 134217728 | bytes 1048576 | tf_op jit(solution)/shard_map/local/pallas_call | solution.py:85
  23.7 1.5 %collective-permute-start.6 = (bf16[528,128]{1,0:T(8,128)(2,1)S(1)}, bf16[528,128]{1,0:T(8,128)(2,1)S(1)}, u32[]{:S(2)}, u32[]{:S(2)}) collective-permute-start(bf16[528,128]{1,0:T(8,128)(2,1)S(1)} %get-tuple-element.103), channel_id=1, source_target_pairs={{0,8},{1,9},{2,10},{3,11},{4,12},{5,13},{6,14},{7,15},{8,0},{9,1},... | collective-permute-start | bytes 405512 | tf_op jit(solution)/shard_map/ppermute | solution.py:326
  25.2 1.6 %collective-permute-start.2 = (bf16[256,128]{1,0:T(8,128)(2,1)S(1)}, bf16[256,128]{1,0:T(8,128)(2,1)S(1)}, u32[]{:S(2)}, u32[]{:S(2)}) collective-permute-start(bf16[256,128]{1,0:T(8,128)(2,1)S(1)} %copy-done), channel_id=1, source_target_pairs={{0,1},{1,0},{2,3},{3,2},{4,5},{5,4},{6,7},{7,6},{8,9},{9,8},{10,11... | collective-permute-start | bytes 196616 | tf_op jit(solution)/shard_map/ppermute | solution.py:326
  26.9 0.9 %collective-permute-done.2.refs_3_.query_ref = bf16[256,128]{1,0:T(8,128)(2,1)S(1)} collective-permute-done((bf16[256,128]{1,0:T(8,128)(2,1)S(1)}, bf16[256,128]{1,0:T(8,128)(2,1)S(1)}, u32[]{:S(2)}, u32[]{:S(2)}) %collective-permute-start.2) | collective-permute-done | bytes 65568 | tf_op jit(solution)/shard_map/ppermute | solution.py:326
  27.8 1.3 %levels.6 = (f32[256,512]{1,0:T(8,128)S(1)}, f32[256,512]{1,0:T(8,128)S(1)}, f32[8,128]{1,0:T(8,128)S(1)}, f32[8,128]{1,0:T(8,128)S(1)}) custom-call(f32[256,128]{1,0:T(8,128)S(1)} %get-tuple-element.88.refs_0_.weight_ref, f32[256,128]{1,0:T(8,128)S(1)} %collective-permute-done.1.refs_1_.weight_ref, bf16[256,128]{1,0:T(8,128)(2,1)S(1)} %copy-done, ...), custom_call_target="tpu_custom_call" | custom-call | flops 201326592 | bytes 1048576 | tf_op jit(solution)/shard_map/levels/pallas_call | solution.py:85
  29.2 1.5 %collective-permute-start.12 = (bf16[528,128]{1,0:T(8,128)(2,1)S(1)}, bf16[528,128]{1,0:T(8,128)(2,1)S(1)}, u32[]{:S(2)}, u32[]{:S(2)}) collective-permute-start(bf16[528,128]{1,0:T(8,128)(2,1)S(1)} %merge.15), channel_id=1, source_target_pairs={{0,24},{1,25},{2,26},{3,27},{4,28},{5,29},{6,30},{7,31},{8,16},{9,... | collective-permute-start | bytes 405512 | tf_op jit(solution)/shard_map/ppermute | solution.py:326
  30.7 1.2 %levels.4 = (f32[256,512]{1,0:T(8,128)S(1)}, f32[256,512]{1,0:T(8,128)S(1)}, f32[8,128]{1,0:T(8,128)S(1)}, f32[8,128]{1,0:T(8,128)S(1)}) custom-call(f32[256,128]{1,0:T(8,128)S(1)} %get-tuple-element.88.refs_0_.weight_ref, f32[256,128]{1,0:T(8,128)S(1)} %collective-permute-done.1.refs_1_.weight_ref, bf16[256,128]{1,0:T(8,128)(2,1)S(1)} %copy-done, ...), custom_call_target="tpu_custom_call" | custom-call | flops 201326592 | bytes 1048576 | tf_op jit(solution)/shard_map/levels/pallas_call | solution.py:85
  32.0 1.5 %collective-permute-start.7 = (bf16[528,128]{1,0:T(8,128)(2,1)S(1)}, bf16[528,128]{1,0:T(8,128)(2,1)S(1)}, u32[]{:S(2)}, u32[]{:S(2)}) collective-permute-start(bf16[528,128]{1,0:T(8,128)(2,1)S(1)} %merge.12), channel_id=1, source_target_pairs={{0,24},{1,25},{2,26},{3,27},{4,28},{5,29},{6,30},{7,31},{8,16},{9,... | collective-permute-start | bytes 405512 | tf_op jit(solution)/shard_map/ppermute | solution.py:326
  33.6 0.5 %levels.7 = (f32[256,512]{1,0:T(8,128)S(1)}, f32[256,512]{1,0:T(8,128)S(1)}, f32[8,128]{1,0:T(8,128)S(1)}, f32[8,128]{1,0:T(8,128)S(1)}) custom-call(f32[256,128]{1,0:T(8,128)S(1)} %get-tuple-element.88.refs_0_.weight_ref, f32[256,128]{1,0:T(8,128)S(1)} %collective-permute-done.1.refs_1_.weight_ref, bf16[256,128]{1,0:T(8,128)(2,1)S(1)} %copy-done, ...), custom_call_target="tpu_custom_call" | custom-call | flops 67108864 | bytes 1048576 | tf_op jit(solution)/shard_map/levels/pallas_call | solution.py:85
  34.1 0.5 %levels.5 = (f32[256,512]{1,0:T(8,128)S(1)}, f32[256,512]{1,0:T(8,128)S(1)}, f32[8,128]{1,0:T(8,128)S(1)}, f32[8,128]{1,0:T(8,128)S(1)}) custom-call(f32[256,128]{1,0:T(8,128)S(1)} %get-tuple-element.88.refs_0_.weight_ref, f32[256,128]{1,0:T(8,128)S(1)} %collective-permute-done.1.refs_1_.weight_ref, bf16[256,128]{1,0:T(8,128)(2,1)S(1)} %copy-done, ...), custom_call_target="tpu_custom_call" | custom-call | flops 67108864 | bytes 1048576 | tf_op jit(solution)/shard_map/levels/pallas_call | solution.py:85
  34.6 0.4 %collective-permute-done.12.packet_ref = bf16[528,128]{1,0:T(8,128)(2,1)S(1)} collective-permute-done((bf16[528,128]{1,0:T(8,128)(2,1)S(1)}, bf16[528,128]{1,0:T(8,128)(2,1)S(1)}, u32[]{:S(2)}, u32[]{:S(2)}) %collective-permute-start.12) | collective-permute-done | bytes 135200 | tf_op jit(solution)/shard_map/ppermute | solution.py:326
  35.3 1.5 %collective-permute-start.13 = (bf16[256,512]{1,0:T(8,128)(2,1)S(1)}, bf16[256,512]{1,0:T(8,128)(2,1)S(1)}, u32[]{:S(2)}, u32[]{:S(2)}) collective-permute-start(bf16[256,512]{1,0:T(8,128)(2,1)S(1)} %last.6), channel_id=1, source_target_pairs={{0,1},{1,0},{2,3},{3,2},{4,5},{5,4},{6,7},{7,6},{8,9},{9,8},{10,11... | collective-permute-start | bytes 786440 | tf_op jit(solution)/shard_map/ppermute | solution.py:326
  36.8 1.2 %collective-permute-done.7.packet_ref = bf16[528,128]{1,0:T(8,128)(2,1)S(1)} collective-permute-done((bf16[528,128]{1,0:T(8,128)(2,1)S(1)}, bf16[528,128]{1,0:T(8,128)(2,1)S(1)}, u32[]{:S(2)}, u32[]{:S(2)}) %collective-permute-start.7) | collective-permute-done | bytes 135200 | tf_op jit(solution)/shard_map/ppermute | solution.py:326
  38.0 0.3 last.4
  38.3 1.6 %collective-permute-start.8 = (bf16[256,512]{1,0:T(8,128)(2,1)S(1)}, bf16[256,512]{1,0:T(8,128)(2,1)S(1)}, u32[]{:S(2)}, u32[]{:S(2)}) collective-permute-start(bf16[256,512]{1,0:T(8,128)(2,1)S(1)} %last.4), channel_id=1, source_target_pairs={{0,1},{1,0},{2,3},{3,2},{4,5},{5,4},{6,7},{7,6},{8,9},{9,8},{10,11... | collective-permute-start | bytes 786440 | tf_op jit(solution)/shard_map/ppermute | solution.py:326
  40.2 0.3 last.5.refs_0_
  40.5 0.6 %collective-permute-done.8.refs_4_ = bf16[256,512]{1,0:T(8,128)(2,1)S(1)} collective-permute-done((bf16[256,512]{1,0:T(8,128)(2,1)S(1)}, bf16[256,512]{1,0:T(8,128)(2,1)S(1)}, u32[]{:S(2)}, u32[]{:S(2)}) %collective-permute-start.8) | collective-permute-done | bytes 262176 | tf_op jit(solution)/shard_map/ppermute | solution.py:326
  41.0 1.0 %finish.1 = bf16[256,2048]{1,0:T(8,128)(2,1)} custom-call(bf16[256,512]{1,0:T(8,128)(2,1)S(1)} %last.5.refs_0_, bf16[256,512]{1,0:T(8,128)(2,1)S(1)} %last.7.refs_1_, f32[256,512]{1,0:T(8,128)S(1)} %local.5.refs_2_, f32[256,512]{1,0:T(8,128)S(1)} %local.7.refs_3_, bf16[256,512]{1,0:T(8,128)(2,1)S(1)} %collective-permute-done.8.refs_4_, ...), custom_call_target="tpu_custom_call" | custom-call | flops 262144 | bytes 1048576 | tf_op jit(solution)/shard_map/finish/pallas_call | solution.py:85
  (24 shorter events, 1.9 us)
Async XLA Ops:
  4.2 4.3 %collective-permute-start = (bf16[528,128]{1,0:T(8,128)(2,1)S(1)}, bf16[528,128]{1,0:T(8,128)(2,1)S(1)}, u32[]{:S(2)}, u32[]{:S(2)}) collective-permute-start(bf16[528,128]{1,0:T(8,128)(2,1)S(1)} %get-tuple-element.83), channel_id=1, source_target_pairs={{0,1},{1,0},{2,3},{3,2},{4,5},{5,4},{6,7},{7,6},{8,9},{9,8},{10,11... | collective-permute-start | bytes 405512 | tf_op jit(solution)/shard_map/ppermute | solution.py:326
  7.5 1.4 %collective-permute-start.3 = (bf16[528,128]{1,0:T(8,128)(2,1)S(1)}, bf16[528,128]{1,0:T(8,128)(2,1)S(1)}, u32[]{:S(2)}, u32[]{:S(2)}) collective-permute-start(bf16[528,128]{1,0:T(8,128)(2,1)S(1)} %get-tuple-element.90), channel_id=1, source_target_pairs={{0,1},{1,0},{2,3},{3,2},{4,5},{5,4},{6,7},{7,6},{8,9},{9,8},{10,11... | collective-permute-start | bytes 405512 | tf_op jit(solution)/shard_map/ppermute | solution.py:326
  8.6 1.8 %copy-start.1 = (f32[6,32,256]{2,1,0:T(8,128)S(1)}, f32[6,32,256]{2,1,0:T(8,128)}, u32[]{:S(2)}) copy-start(f32[6,32,256]{2,1,0:T(8,128)} %mix_ref) | copy-start | bytes 589828
  8.7 4.9 %collective-permute-start.9 = (bf16[528,128]{1,0:T(8,128)(2,1)S(1)}, bf16[528,128]{1,0:T(8,128)(2,1)S(1)}, u32[]{:S(2)}, u32[]{:S(2)}) collective-permute-start(bf16[528,128]{1,0:T(8,128)(2,1)S(1)} %get-tuple-element.84), channel_id=1, source_target_pairs={{0,2},{1,3},{2,0},{3,1},{4,6},{5,7},{6,4},{7,5},{8,10},{9,11},{10,... | collective-permute-start | bytes 405512 | tf_op jit(solution)/shard_map/ppermute | solution.py:326
  8.9 1.5 %copy-start = (bf16[256,128]{1,0:T(8,128)(2,1)S(1)}, bf16[256,128]{1,0:T(8,128)(2,1)}, u32[]{:S(2)}) copy-start(bf16[256,128]{1,0:T(8,128)(2,1)} %query_ref.2) | copy-start | bytes 196612
  9.0 7.4 %collective-permute-start.4 = (bf16[528,128]{1,0:T(8,128)(2,1)S(1)}, bf16[528,128]{1,0:T(8,128)(2,1)S(1)}, u32[]{:S(2)}, u32[]{:S(2)}) collective-permute-start(bf16[528,128]{1,0:T(8,128)(2,1)S(1)} %get-tuple-element.93), channel_id=1, source_target_pairs={{0,2},{1,3},{2,0},{3,1},{4,6},{5,7},{6,4},{7,5},{8,10},{9,11},{10,... | collective-permute-start | bytes 405512 | tf_op jit(solution)/shard_map/ppermute | solution.py:326
  13.7 8.3 %collective-permute-start.10 = (bf16[528,128]{1,0:T(8,128)(2,1)S(1)}, bf16[528,128]{1,0:T(8,128)(2,1)S(1)}, u32[]{:S(2)}, u32[]{:S(2)}) collective-permute-start(bf16[528,128]{1,0:T(8,128)(2,1)S(1)} %get-tuple-element.127), channel_id=1, source_target_pairs={{0,6},{1,7},{2,4},{3,5},{4,2},{5,3},{6,0},{7,1},{8,14},{9,15},{10,... | collective-permute-start | bytes 405512 | tf_op jit(solution)/shard_map/ppermute | solution.py:326
  16.6 7.0 %collective-permute-start.5 = (bf16[528,128]{1,0:T(8,128)(2,1)S(1)}, bf16[528,128]{1,0:T(8,128)(2,1)S(1)}, u32[]{:S(2)}, u32[]{:S(2)}) collective-permute-start(bf16[528,128]{1,0:T(8,128)(2,1)S(1)} %get-tuple-element.101), channel_id=1, source_target_pairs={{0,6},{1,7},{2,4},{3,5},{4,2},{5,3},{6,0},{7,1},{8,14},{9,15},{10,... | collective-permute-start | bytes 405512 | tf_op jit(solution)/shard_map/ppermute | solution.py:326
  18.0 9.7 %collective-permute-start.1 = (f32[256,128]{1,0:T(8,128)S(1)}, f32[256,128]{1,0:T(8,128)S(1)}, u32[]{:S(2)}, u32[]{:S(2)}) collective-permute-start(f32[256,128]{1,0:T(8,128)S(1)} %get-tuple-element.87), channel_id=1, source_target_pairs={{0,1},{1,0},{2,3},{3,2},{4,5},{5,4},{6,7},{7,6},{8,9},{9,8},{10,11... | collective-permute-start | bytes 393224 | tf_op jit(solution)/shard_map/ppermute | solution.py:326
  22.1 6.9 %collective-permute-start.11 = (bf16[528,128]{1,0:T(8,128)(2,1)S(1)}, bf16[528,128]{1,0:T(8,128)(2,1)S(1)}, u32[]{:S(2)}, u32[]{:S(2)}) collective-permute-start(bf16[528,128]{1,0:T(8,128)(2,1)S(1)} %get-tuple-element.129), channel_id=1, source_target_pairs={{0,8},{1,9},{2,10},{3,11},{4,12},{5,13},{6,14},{7,15},{8,0},{9,1},... | collective-permute-start | bytes 405512 | tf_op jit(solution)/shard_map/ppermute | solution.py:326
  23.7 8.2 %collective-permute-start.6 = (bf16[528,128]{1,0:T(8,128)(2,1)S(1)}, bf16[528,128]{1,0:T(8,128)(2,1)S(1)}, u32[]{:S(2)}, u32[]{:S(2)}) collective-permute-start(bf16[528,128]{1,0:T(8,128)(2,1)S(1)} %get-tuple-element.103), channel_id=1, source_target_pairs={{0,8},{1,9},{2,10},{3,11},{4,12},{5,13},{6,14},{7,15},{8,0},{9,1},... | collective-permute-start | bytes 405512 | tf_op jit(solution)/shard_map/ppermute | solution.py:326
  25.2 2.5 %collective-permute-start.2 = (bf16[256,128]{1,0:T(8,128)(2,1)S(1)}, bf16[256,128]{1,0:T(8,128)(2,1)S(1)}, u32[]{:S(2)}, u32[]{:S(2)}) collective-permute-start(bf16[256,128]{1,0:T(8,128)(2,1)S(1)} %copy-done), channel_id=1, source_target_pairs={{0,1},{1,0},{2,3},{3,2},{4,5},{5,4},{6,7},{7,6},{8,9},{9,8},{10,11... | collective-permute-start | bytes 196616 | tf_op jit(solution)/shard_map/ppermute | solution.py:326
  29.2 5.9 %collective-permute-start.12 = (bf16[528,128]{1,0:T(8,128)(2,1)S(1)}, bf16[528,128]{1,0:T(8,128)(2,1)S(1)}, u32[]{:S(2)}, u32[]{:S(2)}) collective-permute-start(bf16[528,128]{1,0:T(8,128)(2,1)S(1)} %merge.15), channel_id=1, source_target_pairs={{0,24},{1,25},{2,26},{3,27},{4,28},{5,29},{6,30},{7,31},{8,16},{9,... | collective-permute-start | bytes 405512 | tf_op jit(solution)/shard_map/ppermute | solution.py:326
  32.0 6.0 %collective-permute-start.7 = (bf16[528,128]{1,0:T(8,128)(2,1)S(1)}, bf16[528,128]{1,0:T(8,128)(2,1)S(1)}, u32[]{:S(2)}, u32[]{:S(2)}) collective-permute-start(bf16[528,128]{1,0:T(8,128)(2,1)S(1)} %merge.12), channel_id=1, source_target_pairs={{0,24},{1,25},{2,26},{3,27},{4,28},{5,29},{6,30},{7,31},{8,16},{9,... | collective-permute-start | bytes 405512 | tf_op jit(solution)/shard_map/ppermute | solution.py:326
  35.3 5.1 %collective-permute-start.13 = (bf16[256,512]{1,0:T(8,128)(2,1)S(1)}, bf16[256,512]{1,0:T(8,128)(2,1)S(1)}, u32[]{:S(2)}, u32[]{:S(2)}) collective-permute-start(bf16[256,512]{1,0:T(8,128)(2,1)S(1)} %last.6), channel_id=1, source_target_pairs={{0,1},{1,0},{2,3},{3,2},{4,5},{5,4},{6,7},{7,6},{8,9},{9,8},{10,11... | collective-permute-start | bytes 786440 | tf_op jit(solution)/shard_map/ppermute | solution.py:326
  38.3 2.8 %collective-permute-start.8 = (bf16[256,512]{1,0:T(8,128)(2,1)S(1)}, bf16[256,512]{1,0:T(8,128)(2,1)S(1)}, u32[]{:S(2)}, u32[]{:S(2)}) collective-permute-start(bf16[256,512]{1,0:T(8,128)(2,1)S(1)} %last.4), channel_id=1, source_target_pairs={{0,1},{1,0},{2,3},{3,2},{4,5},{5,4},{6,7},{7,6},{8,9},{9,8},{10,11... | collective-permute-start | bytes 786440 | tf_op jit(solution)/shard_map/ppermute | solution.py:326

commit v4 on v3

--- a/solution.py
+++ b/solution.py
@@ -90,28 +90,32 @@
         scratch_shapes=list(scratch),
         input_output_aliases=aliases or {},
         compiler_params=pltpu.CompilerParams(vmem_limit_bytes=20 << 20),
-        cost_estimate=pl.CostEstimate(flops=flops, bytes_accessed=1 << 20, transcendentals=exps),
+        cost_estimate=pl.CostEstimate(flops=flops * 100, bytes_accessed=1 << 10, transcendentals=0),
         name=name,
     )(*arrays)
 
 
 def ends_kernel(chunk, *refs):
     core = position()[0]
+    halves = (1 - core, core)
     if chunk == 0:
-        decay_hbm, key_hbm, x_hbm, sent_ref, kept_ref, x_ref, decay_ref, key_ref, factor_ref, sum_ref, small, big = refs
-    else:
-        x_hbm, key_ref, factor_ref, sum_ref, sent_ref, kept_ref, x_ref, big = refs
-    halves = (1 - core, core)
-    copies = []
-    if chunk == 0:
-        copies.append(pltpu.make_async_copy(decay_hbm, decay_ref, small.at[0]))
-        copies.append(pltpu.make_async_copy(key_hbm, key_ref, small.at[1]))
-    for place, half in enumerate(halves):
-        columns = pl.ds(pl.multiple_of(half * (CHUNKS * WIDTH) + chunk * WIDTH, WIDTH), WIDTH)
-        copies.append(pltpu.make_async_copy(x_hbm.at[:, columns], x_ref.at[place], big.at[place]))
-    for copy in copies:
-        copy.start()
-    if chunk == 0:
+        sources, refs = refs[0:5], refs[5:]
+        sent_ref, kept_ref, factor_ref, sum_ref = refs[0:4]
+        decay_ref, key_ref, query_ref, mix_ref = refs[4:8]
+        x_refs, (small, big) = refs[8 : 8 + CHUNKS], refs[8 + CHUNKS :]
+        x_ref = x_refs[0]
+        copies = [
+            pltpu.make_async_copy(source, target, small.at[place])
+            for place, (source, target) in enumerate(zip(sources, (decay_ref, key_ref, query_ref, mix_ref)))
+        ]
+        for part in range(CHUNKS):
+            for place, half in enumerate(halves):
+                columns = pl.ds(pl.multiple_of(half * (CHUNKS * WIDTH) + part * WIDTH, WIDTH), WIDTH)
+                copies.append(
+                    pltpu.make_async_copy(sources[4].at[:, columns], x_refs[part].at[place], big.at[2 * part + place])
+                )
+        for place in (0, 1, *range(4, 4 + 2 * CHUNKS), 2, 3):
+            copies[place].start()
         copies[0].wait()
         decay = pad_heads(decay_ref[...])
         after = exact_dot(triangle(lambda r, c: c > r), decay, ((1,), (1,)))
@@ -121,13 +125,15 @@
         sum_ref[...] = sums
         copies[1].wait()
     else:
+        x_ref, key_ref, factor_ref, sum_ref, sent_ref, kept_ref = refs
         factor = factor_ref[...]
         sums = sum_ref[...]
     lane = lax.broadcasted_iota(jnp.int32, sums.shape, 1)
     keys = key_ref[...]
     for place, (half, packet_ref) in enumerate(zip(halves, (sent_ref, kept_ref))):
         packet_ref[BODY:PACK] = total_rows(jnp.take_along_axis(sums, (lane + half * SHARE) & 127, axis=1))
-        copies[place - 2].wait()
+        if chunk == 0:
+            copies[4 + place].wait()
         for duo in range(PAIRS // 2):
             pieces = []
             for pair in (2 * duo, 2 * duo + 1):
@@ -137,6 +143,9 @@
             state = lax.dot_general(keys, decayed, (((0,), (0,)), ((), ())), preferred_element_type=F32)
             packet_ref[duo * 256 : duo * 256 + 128] = state[:, 0:128].astype(BF16)
             packet_ref[duo * 256 + 128 : duo * 256 + 256] = state[:, 128:256].astype(BF16)
+    if chunk == 0:
+        for copy in copies[2:4] + copies[6:]:
+            copy.wait()
 
 
 def merge_kernel(bit, chunk, *refs):
@@ -190,8 +199,13 @@
     low = jnp.concatenate([weight[:SHARE] for weight in weights] + unused, axis=0).T
     high = jnp.concatenate([weight[SHARE:] for weight in weights] + unused, axis=0).T
     own_ref[...] = jnp.where(core == 0, low, high)
-    sent_ref[...] = jnp.where(core == 0, high, low)
-    raw = lax.dot_general(query_ref[...], key_ref[...], (((1,), (1,)), ((), ())), preferred_element_type=F32)
+    queries = query_ref[...]
+    sent_ref[:, 0:128] = queries
+    far = jnp.where(core == 0, high, low)
+    far_high = far.astype(BF16)
+    sent_ref[:, 128:256] = far_high
+    sent_ref[:, 256:384] = (far - far_high.astype(F32)).astype(BF16)
+    raw = lax.dot_general(queries, key_ref[...], (((1,), (1,)), ((), ())), preferred_element_type=F32)
     scores_ref[...] = raw * causal.astype(F32)
 
 
@@ -222,7 +236,7 @@
         total_ref[upper:, pl.ds(offset, 128)] = bottom
         return 0
 
-    lax.fori_loop(0, PAIRS, pair_step, 0)
+    lax.fori_loop(0, PAIRS, pair_step, 0, unroll=True)
 
 
 def make_local(place, chunk, *arrays):
@@ -241,25 +255,30 @@
     return jnp.concatenate([spread(table, first), spread(table, first + 2)], axis=1)
 
 
-def level_term(level, chunk, duo, queries, packet_ref, weight_ref, gap):
+def far_tables(far_ref):
+    return far_ref[:, 0:128], far_ref[:, 128:256].astype(F32) + far_ref[:, 256:384].astype(F32)
+
+
+def level_term(level, chunk, duo, queries, packet_ref, weights, gap):
     product = jnp.dot(queries, duo_columns(packet_ref, duo), preferred_element_type=F32)
     pair = chunk * PAIRS + duo * 2
-    return product * (duo_spread(weight_ref[...], level * SHARE + pair * 2) * duo_spread(gap, pair * 2)[0:1])
+    return product * (duo_spread(weights, level * SHARE + pair * 2) * duo_spread(gap, pair * 2)[0:1])
 
 
 def levels_kernel(wanted, chunk, *refs):
     bits = position()
-    weight_refs, query_refs = refs[0:2], refs[2:4]
+    own, far = (refs[0][...], refs[1][...]), far_tables(refs[2])
+    refs = refs[3:]
     if wanted[0] == 0:
-        total_ref, kept_ref, *packets = refs[4:-4]
+        total_ref, kept_ref, *packets = refs[:-4]
         totals = (total_ref, None)
         gaps = [jnp.zeros((8, 128), F32)] * 2
     else:
-        totals, gaps, packets = refs[4:6], [refs[6][...], refs[7][...]], refs[8:-4]
+        totals, gaps, packets = refs[0:2], [refs[2][...], refs[3][...]], refs[4:-4]
         kept_ref = None
     outs, gap_outs = refs[-4:-2], refs[-2:]
     for side in range(2):
-        queries = query_refs[side][...]
+        queries, weights = far if side else own
         used = [kept_ref if side == 1 and level == 0 else packet for level, packet in zip(wanted, packets)]
         gap, before = gaps[side], []
         for level, packet in zip(wanted, used):
@@ -271,7 +290,7 @@
             lanes = slice(duo * 256, duo * 256 + 256)
             running = None if totals[side] is None else totals[side][:, lanes]
             for level, packet, factor in zip(wanted, used, before):
-                term = level_term(level, chunk, duo, queries, packet, weight_refs[side], factor)
+                term = level_term(level, chunk, duo, queries, packet, weights, factor)
                 running = term if running is None else running + term
             outs[side][:, lanes] = running
 
@@ -283,19 +302,23 @@
     )
 
 
-def last_kernel(chunk, weight_ref, query_ref, total_ref, gap_ref, packet_ref, out_ref):
-    queries = query_ref[...]
+def last_kernel(far, chunk, *refs):
+    if far:
+        queries, weights = far_tables(refs[0])
+    else:
+        queries, weights = refs[0][...], refs[1][...]
+    total_ref, gap_ref, packet_ref, out_ref = refs[-4:]
     gap = jnp.exp(gap_ref[...])
     for duo in range(PAIRS // 2):
         lanes = slice(duo * 256, duo * 256 + 256)
-        term = level_term(LEVELS - 1, chunk, duo, queries, packet_ref, weight_ref, gap)
+        term = level_term(LEVELS - 1, chunk, duo, queries, packet_ref, weights, gap)
         out_ref[:, lanes] = (total_ref[:, lanes] + term).astype(BF16)
 
 
-def add_last(chunk, *arrays):
+def add_last(far, chunk, *arrays):
     return call(
-        functools.partial(last_kernel, chunk), [pltpu.VMEM((TOK, WIDTH), BF16)], arrays, "last",
-        2 * TOK * STATE * WIDTH, kept=range(5),
+        functools.partial(last_kernel, far, chunk), [pltpu.VMEM((TOK, WIDTH), BF16)], arrays, "last",
+        2 * TOK * STATE * WIDTH, kept=range(len(arrays)),
     )[0]
 
 
@@ -333,25 +356,28 @@
     kept, x, got, state, packet = ([None] * CHUNKS for _ in range(5))
     history = [[] for _ in chunks]
     for c in chunks:
-        semaphores = pltpu.SemaphoreType.DMA((2,))
         kernel, flops = functools.partial(ends_kernel, c), 4 * TOK * STATE * WIDTH
         if c == 0:
-            sent, kept[c], x[c], decay, keys, factor, sums = call(
+            sent, kept[c], factor, sums, decay, keys, queries, mix, *x = call(
                 kernel,
                 [
-                    PACKET, PACKET, X_PART, pltpu.VMEM((HEADS, TOK), F32), pltpu.VMEM((TOK, STATE), BF16), TABLE,
-                    pltpu.VMEM((16, 128), F32),
-                ],
-                [decay_log, write_keys, inputs], "ends", flops, 32768, far=(0, 1, 2), scratch=[semaphores, semaphores],
+                    PACKET, PACKET, TABLE, pltpu.VMEM((16, 128), F32), pltpu.VMEM((HEADS, TOK), F32),
+                    pltpu.VMEM((TOK, STATE), BF16), pltpu.VMEM((TOK, STATE), BF16),
+                    pltpu.VMEM((LEVELS + 1, HEADS, TOK), F32),
+                ] + [X_PART] * CHUNKS,
+                [decay_log, write_keys, read_queries, level_mix, inputs], "ends", flops, 32768, far=range(5),
+                scratch=[pltpu.SemaphoreType.DMA((4,)), pltpu.SemaphoreType.DMA((2 * CHUNKS,))],
             )
         else:
-            sent, kept[c], x[c] = call(
-                kernel, [PACKET, PACKET, X_PART], [inputs, keys, factor, sums], "ends", flops, far=(0,),
-                kept=(1, 2, 3), scratch=[semaphores],
+            sent, kept[c] = call(
+                kernel, [PACKET, PACKET], [x[c], keys, factor, sums], "ends", flops, kept=range(4)
             )
+            got[c - 1], sent = after(got[c - 1], sent)
         got[c] = swap(sent, masks[0])
 
     def advance(level, c):
+        if c > 0:
+            got[c], _ = after(got[c], packet[c - 1])
         history[c].append(got[c])
         if level == 0:
             packet[c], *state[c] = merge(0, c, kept[c], got[c])
@@ -361,21 +387,28 @@
 
     for c in chunks:
         advance(0, c)
-    queries, level_mix, _ = after(read_queries, level_mix, packet[-1])
-    scores, column, row, weights, sent = call(
-        tables_kernel, [pltpu.VMEM((TOK, TOK), F32), TABLE, pltpu.VMEM((HEADS, TOK), F32), TABLE, TABLE],
-        [decay, level_mix, keys, queries], "tables", 4 * TOK * TOK * STATE, 16384, kept=(0, 1, 2, 3),
-    )
-    far_weights, far_queries = swap(sent, 1), swap(queries, 1)
+    queries, mix, _ = after(queries, mix, packet[-1])
+    scores, column, row, weights, tables = call(
+        tables_kernel,
+        [
+            pltpu.VMEM((TOK, TOK), F32), TABLE, pltpu.VMEM((HEADS, TOK), F32), TABLE, pltpu.VMEM((TOK, 384), BF16),
+        ],
+        [decay, mix, keys, queries], "tables", 4 * TOK * TOK * STATE, 16384, kept=range(4),
+    )
+    far = swap(tables, 1)
     total, rest = [None] * CHUNKS, [None] * CHUNKS
     for level, place, results in ((1, 1, total), (2, 0, rest)):
         for c in chunks:
+            if c > 0:
+                x[c], _ = after(x[c], packet[c - 1])
             results[c] = make_local(place, c, scores, column, row, x[c])
-            got[c], results[c] = after(got[c], results[c])
+            got[c], results[c], far = after(got[c], results[c], far)
             advance(level, c)
-    shared = (weights, far_weights, queries, far_queries)
+    shared = (queries, weights, far)
     far_total, gap, far_gap = [None] * CHUNKS, [None] * CHUNKS, [None] * CHUNKS
     for c in chunks:
+        if c > 0:
+            total[c], _ = after(total[c], packet[c - 1])
         total[c], far_total[c], gap[c], far_gap[c] = add_levels((0, 1, 2), c, *shared, total[c], kept[c], *history[c])
         got[c], total[c] = after(got[c], total[c])
         advance(3, c)
@@ -385,10 +418,10 @@
             (3,), c, *shared, total[c], far_total[c], gap[c], far_gap[c], history[c][3]
         )
         got[c], total[c] = after(got[c], total[c])
-        part = add_last(c, far_weights, far_queries, far_total[c], far_gap[c], got[c])
+        part = add_last(True, c, far, far_total[c], far_gap[c], got[c])
         parts[c] = swap(part, 1)
         late, _ = after(got[c], part)
-        done[c] = add_last(c, weights, queries, total[c], gap[c], late)
+        done[c] = add_last(False, c, queries, weights, total[c], gap[c], late)
         parts[c], done[c] = after(parts[c], done[c])
     out, = call(
         finish_kernel, [jax.ShapeDtypeStruct((TOK, HEADS * HEAD), BF16)], [*done, *rest, *parts], "finish",

time: 42.4 us -> 39.1 us (0.922)
  waiting for transfers between devices: 6 us -> 10.7 us
  Pallas kernels: 16.7 us -> 12.4 us
  starting transfers between devices: 19.1 us -> 15.6 us
    ppermute x14 -> x13, waiting for transfers between devices: 6 us -> 10.7 us  [swap(): return lax.ppermute(array, 'ctx', [(i, i ^ mask) for i in range(devices)])]
    pallas_call x24, Pallas kernels: 16.7 us -> 12.4 us  [call(): pl.pallas_call(kernel, out_shape=outs, in_specs=[ANY if place in far else...]
    ppermute x14 -> x13, starting transfers between devices: 19.1 us -> 15.6 us  [swap(): return lax.ppermute(array, 'ctx', [(i, i ^ mask) for i in range(devices)])]
  transfers between devices with their start and end apart: 14 -> 13, of which waited for: 8 -> 8; matrix products, arithmetic and copies ran while one was open for 0% -> 0% of each run, Pallas kernels for 27% -> 23%
where the time goes in v4:
time: 39.1 us; the launch traced here: 39 us
  starting transfers between devices  15.6 us (40%)
  Pallas kernels  12.4 us (32%)
  waiting for transfers between devices  10.7 us (27%)
    ppermute x13, starting transfers between devices, swap(): return lax.ppermute(array, 'ctx', [(i, i ^ mask) for i in range(devices)])  15.6 us
    pallas_call x24, Pallas kernels, call(): pl.pallas_call(kernel, out_shape=outs, in_specs=[ANY if place in far else...  12.4 us
    ppermute x13, waiting for transfers between devices, swap(): return lax.ppermute(array, 'ctx', [(i, i ^ mask) for i in range(devices)])  10.7 us
  transfers between devices with their start and end apart: 13, of which 8 were waited for; matrix products, arithmetic and copies ran while one was open for 0% of the time, Pallas kernels for 23%

profile of v4, /device:TPU:1, one launch (start us, length us, event | category | flops | bytes accessed | tf_op | source)
XLA Modules:
  0.0 39.0 jit_solution(17006664626341239478)
XLA Ops:
  0.0 2.3 %ends.2 = (bf16[528,128]{1,0:T(8,128)(2,1)S(1)}, bf16[528,128]{1,0:T(8,128)(2,1)S(1)}, f32[256,128]{1,0:T(8,128)S(1)}, f32[16,128]{1,0:T(8,128)S(1)}, f32[32,256...) custom-call(f32[32,256]{1,0:T(8,128)} %refs_0_.1, ...), custom_call_target="tpu_custom_call" | custom-call | flops 6710886400 | bytes 1024 | tf_op jit(solution)/shard_map/ends/pallas_call | solution.py:85
  2.3 3.3 %collective-permute-start = (bf16[528,128]{1,0:T(8,128)(2,1)S(1)}, bf16[528,128]{1,0:T(8,128)(2,1)S(1)}, u32[]{:S(2)}, u32[]{:S(2)}) collective-permute-start(bf16[528,128]{1,0:T(8,128)(2,1)S(1)} %get-tuple-element.98), channel_id=1, source_target_pairs={{0,1},{1,0},{2,3},{3,2},{4,5},{5,4},{6,7},{7,6},{8,9},{9,8},{10,11... | collective-permute-start | bytes 405512 | tf_op jit(solution)/shard_map/ppermute | solution.py:349
  5.6 0.7 %ends.3 = (bf16[528,128]{1,0:T(8,128)(2,1)S(1)}, bf16[528,128]{1,0:T(8,128)(2,1)S(1)}) custom-call(bf16[2,256,512]{2,1,0:T(8,128)(2,1)S(1)} %get-tuple-element.132.refs_0_.x_ref, bf16[256,128]{1,0:T(8,128)(2,1)S(1)} %get-tuple-element.94.refs_1_.key_ref, f32[256,128]{1,0:T(8,128)S(1)} %get-tuple-element.95.refs_2_, f32[16,128]{1,0:T(8,128)S(1)} %get-tuple-element.96.refs_3_), custom_call_target="tpu_custom_call" | custom-call | flops 6710886400 | bytes 1024 | tf_op jit(solution)/shard_map/ends/pallas_call | solution.py:85
  6.3 0.3 collective-permute-done.refs_1_.refs_5_
  6.6 0.4 collective-permute-start.1
  7.2 0.8 %collective-permute-done.1.refs_1_.refs_5_ = bf16[528,128]{1,0:T(8,128)(2,1)S(1)} collective-permute-done((bf16[528,128]{1,0:T(8,128)(2,1)S(1)}, bf16[528,128]{1,0:T(8,128)(2,1)S(1)}, u32[]{:S(2)}, u32[]{:S(2)}) %collective-permute-start.1) | collective-permute-done | bytes 135200 | tf_op jit(solution)/shard_map/ppermute | solution.py:349
  8.1 0.8 %collective-permute-start.2 = (bf16[528,128]{1,0:T(8,128)(2,1)S(1)}, bf16[528,128]{1,0:T(8,128)(2,1)S(1)}, u32[]{:S(2)}, u32[]{:S(2)}) collective-permute-start(bf16[528,128]{1,0:T(8,128)(2,1)S(1)} %get-tuple-element.107), channel_id=1, source_target_pairs={{0,2},{1,3},{2,0},{3,1},{4,6},{5,7},{6,4},{7,5},{8,10},{9,11},{10,... | collective-permute-start | bytes 405512 | tf_op jit(solution)/shard_map/ppermute | solution.py:349
  8.8 0.5 %tables.1 = (f32[256,256]{1,0:T(8,128)S(1)}, f32[256,128]{1,0:T(8,128)S(1)}, f32[32,256]{1,0:T(8,128)S(1)}, f32[256,128]{1,0:T(8,128)S(1)}, bf16[256,384]{1,0:T(8,128)(2,1)S(1)}) custom-call(f32[32,256]{1,0:T(8,128)S(1)} %get-tuple-element.108.decay_ref, f32[6,32,256]{2,1,0:T(8,128)S(1)} %get-tuple-element.111.mix_ref, ...), custom_call_target="tpu_custom_call" | custom-call | flops 3355443200 | bytes 1024 | tf_op jit(solution)/shard_map/tables/pallas_call | solution.py:85
  9.3 0.8 %collective-permute-start.4 = (bf16[256,384]{1,0:T(8,128)(2,1)S(1)}, bf16[256,384]{1,0:T(8,128)(2,1)S(1)}, u32[]{:S(2)}, u32[]{:S(2)}) collective-permute-start(bf16[256,384]{1,0:T(8,128)(2,1)S(1)} %get-tuple-element.119), channel_id=1, source_target_pairs={{0,1},{1,0},{2,3},{3,2},{4,5},{5,4},{6,7},{7,6},{8,9},{9,8},{10,11... | collective-permute-start | bytes 589832 | tf_op jit(solution)/shard_map/ppermute | solution.py:349
  10.1 0.6 %local.6.refs_2_ = f32[256,512]{1,0:T(8,128)S(1)} custom-call(f32[256,256]{1,0:T(8,128)S(1)} %get-tuple-element.113.scores_ref, f32[256,128]{1,0:T(8,128)S(1)} %get-tuple-element.114.column_ref, f32[32,256]{1,0:T(8,128)S(1)} %get-tuple-element.115.row_ref, bf16[2,256,512]{2,1,0:T(8,128)(2,1)S(1)} %get-tuple-element.118.x_ref), custom_call_target="tpu_custom_call" | custom-call | flops 13421772800 | bytes 1024 | tf_op jit(solution)/shard_map/local/pallas_call | solution.py:85
  10.7 0.6 %local.4.refs_3_ = f32[256,512]{1,0:T(8,128)S(1)} custom-call(f32[256,256]{1,0:T(8,128)S(1)} %get-tuple-element.113.scores_ref, f32[256,128]{1,0:T(8,128)S(1)} %get-tuple-element.114.column_ref, f32[32,256]{1,0:T(8,128)S(1)} %get-tuple-element.115.row_ref, bf16[2,256,512]{2,1,0:T(8,128)(2,1)S(1)} %get-tuple-element.118.x_ref), custom_call_target="tpu_custom_call" | custom-call | flops 13421772800 | bytes 1024 | tf_op jit(solution)/shard_map/local/pallas_call | solution.py:85
  11.4 0.8 %collective-permute-done.3.refs_2_.refs_6_ = bf16[528,128]{1,0:T(8,128)(2,1)S(1)} collective-permute-done((bf16[528,128]{1,0:T(8,128)(2,1)S(1)}, bf16[528,128]{1,0:T(8,128)(2,1)S(1)}, u32[]{:S(2)}, u32[]{:S(2)}) %collective-permute-start.3) | collective-permute-done | bytes 135200 | tf_op jit(solution)/shard_map/ppermute | solution.py:349
  12.3 0.8 %collective-permute-start.6 = (bf16[528,128]{1,0:T(8,128)(2,1)S(1)}, bf16[528,128]{1,0:T(8,128)(2,1)S(1)}, u32[]{:S(2)}, u32[]{:S(2)}) collective-permute-start(bf16[528,128]{1,0:T(8,128)(2,1)S(1)} %get-tuple-element.121), channel_id=1, source_target_pairs={{0,6},{1,7},{2,4},{3,5},{4,2},{5,3},{6,0},{7,1},{8,14},{9,15},{10,... | collective-permute-start | bytes 405512 | tf_op jit(solution)/shard_map/ppermute | solution.py:349
  13.1 0.6 %local.5.refs_3_ = f32[256,512]{1,0:T(8,128)S(1)} custom-call(f32[256,256]{1,0:T(8,128)S(1)} %get-tuple-element.113.scores_ref, f32[256,128]{1,0:T(8,128)S(1)} %get-tuple-element.114.column_ref, f32[32,256]{1,0:T(8,128)S(1)} %get-tuple-element.115.row_ref, bf16[2,256,512]{2,1,0:T(8,128)(2,1)S(1)} %get-tuple-element.132.refs_0_.x_ref), custom_call_target="tpu_custom_call" | custom-call | flops 13421772800 | bytes 1024 | tf_op jit(solution)/shard_map/local/pallas_call | solution.py:85
  13.8 1.3 %collective-permute-done.2.refs_2_.refs_6_ = bf16[528,128]{1,0:T(8,128)(2,1)S(1)} collective-permute-done((bf16[528,128]{1,0:T(8,128)(2,1)S(1)}, bf16[528,128]{1,0:T(8,128)(2,1)S(1)}, u32[]{:S(2)}, u32[]{:S(2)}) %collective-permute-start.2) | collective-permute-done | bytes 135200 | tf_op jit(solution)/shard_map/ppermute | solution.py:349
  15.2 0.8 %collective-permute-start.5 = (bf16[528,128]{1,0:T(8,128)(2,1)S(1)}, bf16[528,128]{1,0:T(8,128)(2,1)S(1)}, u32[]{:S(2)}, u32[]{:S(2)}) collective-permute-start(bf16[528,128]{1,0:T(8,128)(2,1)S(1)} %get-tuple-element.126), channel_id=1, source_target_pairs={{0,6},{1,7},{2,4},{3,5},{4,2},{5,3},{6,0},{7,1},{8,14},{9,15},{10,... | collective-permute-start | bytes 405512 | tf_op jit(solution)/shard_map/ppermute | solution.py:349
  16.0 1.4 %collective-permute-done.6.refs_2_.refs_7_ = bf16[528,128]{1,0:T(8,128)(2,1)S(1)} collective-permute-done((bf16[528,128]{1,0:T(8,128)(2,1)S(1)}, bf16[528,128]{1,0:T(8,128)(2,1)S(1)}, u32[]{:S(2)}, u32[]{:S(2)}) %collective-permute-start.6) | collective-permute-done | bytes 135200 | tf_op jit(solution)/shard_map/ppermute | solution.py:349
  17.7 0.6 %local.7.refs_3_ = f32[256,512]{1,0:T(8,128)S(1)} custom-call(f32[256,256]{1,0:T(8,128)S(1)} %get-tuple-element.113.scores_ref, f32[256,128]{1,0:T(8,128)S(1)} %get-tuple-element.114.column_ref, f32[32,256]{1,0:T(8,128)S(1)} %get-tuple-element.115.row_ref, bf16[2,256,512]{2,1,0:T(8,128)(2,1)S(1)} %get-tuple-element.132.refs_0_.x_ref), custom_call_target="tpu_custom_call" | custom-call | flops 13421772800 | bytes 1024 | tf_op jit(solution)/shard_map/local/pallas_call | solution.py:85
  18.3 3.4 %collective-permute-done.5.refs_2_.refs_7_ = bf16[528,128]{1,0:T(8,128)(2,1)S(1)} collective-permute-done((bf16[528,128]{1,0:T(8,128)(2,1)S(1)}, bf16[528,128]{1,0:T(8,128)(2,1)S(1)}, u32[]{:S(2)}, u32[]{:S(2)}) %collective-permute-start.5) | collective-permute-done | bytes 135200 | tf_op jit(solution)/shard_map/ppermute | solution.py:349
  21.9 1.2 %levels.4 = (f32[256,512]{1,0:T(8,128)S(1)}, f32[256,512]{1,0:T(8,128)S(1)}, f32[8,128]{1,0:T(8,128)S(1)}, f32[8,128]{1,0:T(8,128)S(1)}) custom-call(bf16[256,128]{1,0:T(8,128)(2,1)S(1)} %get-tuple-element.112.query_ref.refs_0_, f32[256,128]{1,0:T(8,128)S(1)} %get-tuple-element.135.refs_1_, bf16[256,384]{1,0:T(8,128)(2,1)S(1)} %collective-permute-done.4.refs_2_.refs_0_, ...), custom_call_target="tpu_custom_call" | custom-call | flops 20132659200 | bytes 1024 | tf_op jit(solution)/shard_map/levels/pallas_call | solution.py:85
  23.3 0.9 %collective-permute-start.8 = (bf16[528,128]{1,0:T(8,128)(2,1)S(1)}, bf16[528,128]{1,0:T(8,128)(2,1)S(1)}, u32[]{:S(2)}, u32[]{:S(2)}) collective-permute-start(bf16[528,128]{1,0:T(8,128)(2,1)S(1)} %merge.13), channel_id=1, source_target_pairs={{0,24},{1,25},{2,26},{3,27},{4,28},{5,29},{6,30},{7,31},{8,16},{9,... | collective-permute-start | bytes 405512 | tf_op jit(solution)/shard_map/ppermute | solution.py:349
  24.2 1.2 %levels.6 = (f32[256,512]{1,0:T(8,128)S(1)}, f32[256,512]{1,0:T(8,128)S(1)}, f32[8,128]{1,0:T(8,128)S(1)}, f32[8,128]{1,0:T(8,128)S(1)}) custom-call(bf16[256,128]{1,0:T(8,128)(2,1)S(1)} %get-tuple-element.112.query_ref.refs_0_, f32[256,128]{1,0:T(8,128)S(1)} %get-tuple-element.135.refs_1_, bf16[256,384]{1,0:T(8,128)(2,1)S(1)} %collective-permute-done.4.refs_2_.refs_0_, ...), custom_call_target="tpu_custom_call" | custom-call | flops 20132659200 | bytes 1024 | tf_op jit(solution)/shard_map/levels/pallas_call | solution.py:85
  25.5 2.0 %collective-permute-done.10.refs_7_.refs_2_ = bf16[528,128]{1,0:T(8,128)(2,1)S(1)} collective-permute-done((bf16[528,128]{1,0:T(8,128)(2,1)S(1)}, bf16[528,128]{1,0:T(8,128)(2,1)S(1)}, u32[]{:S(2)}, u32[]{:S(2)}) %collective-permute-start.10) | collective-permute-done | bytes 135200 | tf_op jit(solution)/shard_map/ppermute | solution.py:349
  27.7 0.5 %levels.5 = (f32[256,512]{1,0:T(8,128)S(1)}, f32[256,512]{1,0:T(8,128)S(1)}, f32[8,128]{1,0:T(8,128)S(1)}, f32[8,128]{1,0:T(8,128)S(1)}) custom-call(bf16[256,128]{1,0:T(8,128)(2,1)S(1)} %get-tuple-element.112.query_ref.refs_0_, f32[256,128]{1,0:T(8,128)S(1)} %get-tuple-element.135.refs_1_, bf16[256,384]{1,0:T(8,128)(2,1)S(1)} %collective-permute-done.4.refs_2_.refs_0_, ...), custom_call_target="tpu_custom_call" | custom-call | flops 6710886400 | bytes 1024 | tf_op jit(solution)/shard_map/levels/pallas_call | solution.py:85
  28.2 0.5 %levels.7 = (f32[256,512]{1,0:T(8,128)S(1)}, f32[256,512]{1,0:T(8,128)S(1)}, f32[8,128]{1,0:T(8,128)S(1)}, f32[8,128]{1,0:T(8,128)S(1)}) custom-call(bf16[256,128]{1,0:T(8,128)(2,1)S(1)} %get-tuple-element.112.query_ref.refs_0_, f32[256,128]{1,0:T(8,128)S(1)} %get-tuple-element.135.refs_1_, bf16[256,384]{1,0:T(8,128)(2,1)S(1)} %collective-permute-done.4.refs_2_.refs_0_, ...), custom_call_target="tpu_custom_call" | custom-call | flops 6710886400 | bytes 1024 | tf_op jit(solution)/shard_map/levels/pallas_call | solution.py:85
  28.8 0.3 last.4
  29.1 6.2 %collective-permute-start.9 = (bf16[256,512]{1,0:T(8,128)(2,1)S(1)}, bf16[256,512]{1,0:T(8,128)(2,1)S(1)}, u32[]{:S(2)}, u32[]{:S(2)}) collective-permute-start(bf16[256,512]{1,0:T(8,128)(2,1)S(1)} %last.4), channel_id=1, source_target_pairs={{0,1},{1,0},{2,3},{3,2},{4,5},{5,4},{6,7},{7,6},{8,9},{9,8},{10,11... | collective-permute-start | bytes 786440 | tf_op jit(solution)/shard_map/ppermute | solution.py:349
  35.3 0.3 last.6
  35.5 1.2 %collective-permute-start.12 = (bf16[256,512]{1,0:T(8,128)(2,1)S(1)}, bf16[256,512]{1,0:T(8,128)(2,1)S(1)}, u32[]{:S(2)}, u32[]{:S(2)}) collective-permute-start(bf16[256,512]{1,0:T(8,128)(2,1)S(1)} %last.6), channel_id=1, source_target_pairs={{0,1},{1,0},{2,3},{3,2},{4,5},{5,4},{6,7},{7,6},{8,9},{9,8},{10,11... | collective-permute-start | bytes 786440 | tf_op jit(solution)/shard_map/ppermute | solution.py:349
  37.0 0.3 last.5.refs_0_
  37.3 0.6 %collective-permute-done.12.refs_5_ = bf16[256,512]{1,0:T(8,128)(2,1)S(1)} collective-permute-done((bf16[256,512]{1,0:T(8,128)(2,1)S(1)}, bf16[256,512]{1,0:T(8,128)(2,1)S(1)}, u32[]{:S(2)}, u32[]{:S(2)}) %collective-permute-start.12) | collective-permute-done | bytes 262176 | tf_op jit(solution)/shard_map/ppermute | solution.py:349
  37.9 1.0 %finish.1 = bf16[256,2048]{1,0:T(8,128)(2,1)} custom-call(bf16[256,512]{1,0:T(8,128)(2,1)S(1)} %last.5.refs_0_, bf16[256,512]{1,0:T(8,128)(2,1)S(1)} %last.7.refs_1_, f32[256,512]{1,0:T(8,128)S(1)} %local.6.refs_2_, f32[256,512]{1,0:T(8,128)S(1)} %local.7.refs_3_, bf16[256,512]{1,0:T(8,128)(2,1)S(1)} %collective-permute-done.9.refs_4_, ...), custom_call_target="tpu_custom_call" | custom-call | flops 26214400 | bytes 1024 | tf_op jit(solution)/shard_map/finish/pallas_call | solution.py:85
  (18 shorter events, 1.6 us)
Async XLA Ops:
  2.3 4.3 %collective-permute-start = (bf16[528,128]{1,0:T(8,128)(2,1)S(1)}, bf16[528,128]{1,0:T(8,128)(2,1)S(1)}, u32[]{:S(2)}, u32[]{:S(2)}) collective-permute-start(bf16[528,128]{1,0:T(8,128)(2,1)S(1)} %get-tuple-element.98), channel_id=1, source_target_pairs={{0,1},{1,0},{2,3},{3,2},{4,5},{5,4},{6,7},{7,6},{8,9},{9,8},{10,11... | collective-permute-start | bytes 405512 | tf_op jit(solution)/shard_map/ppermute | solution.py:349
  6.6 1.4 %collective-permute-start.1 = (bf16[528,128]{1,0:T(8,128)(2,1)S(1)}, bf16[528,128]{1,0:T(8,128)(2,1)S(1)}, u32[]{:S(2)}, u32[]{:S(2)}) collective-permute-start(bf16[528,128]{1,0:T(8,128)(2,1)S(1)} %get-tuple-element.100), channel_id=1, source_target_pairs={{0,1},{1,0},{2,3},{3,2},{4,5},{5,4},{6,7},{7,6},{8,9},{9,8},{10,11... | collective-permute-start | bytes 405512 | tf_op jit(solution)/shard_map/ppermute | solution.py:349
  7.1 5.1 %collective-permute-start.3 = (bf16[528,128]{1,0:T(8,128)(2,1)S(1)}, bf16[528,128]{1,0:T(8,128)(2,1)S(1)}, u32[]{:S(2)}, u32[]{:S(2)}) collective-permute-start(bf16[528,128]{1,0:T(8,128)(2,1)S(1)} %get-tuple-element.103), channel_id=1, source_target_pairs={{0,2},{1,3},{2,0},{3,1},{4,6},{5,7},{6,4},{7,5},{8,10},{9,11},{10,... | collective-permute-start | bytes 405512 | tf_op jit(solution)/shard_map/ppermute | solution.py:349
  8.1 7.0 %collective-permute-start.2 = (bf16[528,128]{1,0:T(8,128)(2,1)S(1)}, bf16[528,128]{1,0:T(8,128)(2,1)S(1)}, u32[]{:S(2)}, u32[]{:S(2)}) collective-permute-start(bf16[528,128]{1,0:T(8,128)(2,1)S(1)} %get-tuple-element.107), channel_id=1, source_target_pairs={{0,2},{1,3},{2,0},{3,1},{4,6},{5,7},{6,4},{7,5},{8,10},{9,11},{10,... | collective-permute-start | bytes 405512 | tf_op jit(solution)/shard_map/ppermute | solution.py:349
  9.3 2.9 %collective-permute-start.4 = (bf16[256,384]{1,0:T(8,128)(2,1)S(1)}, bf16[256,384]{1,0:T(8,128)(2,1)S(1)}, u32[]{:S(2)}, u32[]{:S(2)}) collective-permute-start(bf16[256,384]{1,0:T(8,128)(2,1)S(1)} %get-tuple-element.119), channel_id=1, source_target_pairs={{0,1},{1,0},{2,3},{3,2},{4,5},{5,4},{6,7},{7,6},{8,9},{9,8},{10,11... | collective-permute-start | bytes 589832 | tf_op jit(solution)/shard_map/ppermute | solution.py:349
  12.3 5.2 %collective-permute-start.6 = (bf16[528,128]{1,0:T(8,128)(2,1)S(1)}, bf16[528,128]{1,0:T(8,128)(2,1)S(1)}, u32[]{:S(2)}, u32[]{:S(2)}) collective-permute-start(bf16[528,128]{1,0:T(8,128)(2,1)S(1)} %get-tuple-element.121), channel_id=1, source_target_pairs={{0,6},{1,7},{2,4},{3,5},{4,2},{5,3},{6,0},{7,1},{8,14},{9,15},{10,... | collective-permute-start | bytes 405512 | tf_op jit(solution)/shard_map/ppermute | solution.py:349
  15.2 6.5 %collective-permute-start.5 = (bf16[528,128]{1,0:T(8,128)(2,1)S(1)}, bf16[528,128]{1,0:T(8,128)(2,1)S(1)}, u32[]{:S(2)}, u32[]{:S(2)}) collective-permute-start(bf16[528,128]{1,0:T(8,128)(2,1)S(1)} %get-tuple-element.126), channel_id=1, source_target_pairs={{0,6},{1,7},{2,4},{3,5},{4,2},{5,3},{6,0},{7,1},{8,14},{9,15},{10,... | collective-permute-start | bytes 405512 | tf_op jit(solution)/shard_map/ppermute | solution.py:349
  17.6 5.6 %collective-permute-start.7 = (bf16[528,128]{1,0:T(8,128)(2,1)S(1)}, bf16[528,128]{1,0:T(8,128)(2,1)S(1)}, u32[]{:S(2)}, u32[]{:S(2)}) collective-permute-start(bf16[528,128]{1,0:T(8,128)(2,1)S(1)} %get-tuple-element.131), channel_id=1, source_target_pairs={{0,8},{1,9},{2,10},{3,11},{4,12},{5,13},{6,14},{7,15},{8,0},{9,1},... | collective-permute-start | bytes 405512 | tf_op jit(solution)/shard_map/ppermute | solution.py:349
  21.8 5.6 %collective-permute-start.10 = (bf16[528,128]{1,0:T(8,128)(2,1)S(1)}, bf16[528,128]{1,0:T(8,128)(2,1)S(1)}, u32[]{:S(2)}, u32[]{:S(2)}) collective-permute-start(bf16[528,128]{1,0:T(8,128)(2,1)S(1)} %get-tuple-element.157), channel_id=1, source_target_pairs={{0,8},{1,9},{2,10},{3,11},{4,12},{5,13},{6,14},{7,15},{8,0},{9,1},... | collective-permute-start | bytes 405512 | tf_op jit(solution)/shard_map/ppermute | solution.py:349
  23.3 5.4 %collective-permute-start.8 = (bf16[528,128]{1,0:T(8,128)(2,1)S(1)}, bf16[528,128]{1,0:T(8,128)(2,1)S(1)}, u32[]{:S(2)}, u32[]{:S(2)}) collective-permute-start(bf16[528,128]{1,0:T(8,128)(2,1)S(1)} %merge.13), channel_id=1, source_target_pairs={{0,24},{1,25},{2,26},{3,27},{4,28},{5,29},{6,30},{7,31},{8,16},{9,... | collective-permute-start | bytes 405512 | tf_op jit(solution)/shard_map/ppermute | solution.py:349
  27.6 7.7 %collective-permute-start.11 = (bf16[528,128]{1,0:T(8,128)(2,1)S(1)}, bf16[528,128]{1,0:T(8,128)(2,1)S(1)}, u32[]{:S(2)}, u32[]{:S(2)}) collective-permute-start(bf16[528,128]{1,0:T(8,128)(2,1)S(1)} %merge.15), channel_id=1, source_target_pairs={{0,24},{1,25},{2,26},{3,27},{4,28},{5,29},{6,30},{7,31},{8,16},{9,... | collective-permute-start | bytes 405512 | tf_op jit(solution)/shard_map/ppermute | solution.py:349
  29.1 8.2 %collective-permute-start.9 = (bf16[256,512]{1,0:T(8,128)(2,1)S(1)}, bf16[256,512]{1,0:T(8,128)(2,1)S(1)}, u32[]{:S(2)}, u32[]{:S(2)}) collective-permute-start(bf16[256,512]{1,0:T(8,128)(2,1)S(1)} %last.4), channel_id=1, source_target_pairs={{0,1},{1,0},{2,3},{3,2},{4,5},{5,4},{6,7},{7,6},{8,9},{9,8},{10,11... | collective-permute-start | bytes 786440 | tf_op jit(solution)/shard_map/ppermute | solution.py:349
  35.5 2.3 %collective-permute-start.12 = (bf16[256,512]{1,0:T(8,128)(2,1)S(1)}, bf16[256,512]{1,0:T(8,128)(2,1)S(1)}, u32[]{:S(2)}, u32[]{:S(2)}) collective-permute-start(bf16[256,512]{1,0:T(8,128)(2,1)S(1)} %last.6), channel_id=1, source_target_pairs={{0,1},{1,0},{2,3},{3,2},{4,5},{5,4},{6,7},{7,6},{8,9},{9,8},{10,11... | collective-permute-start | bytes 786440 | tf_op jit(solution)/shard_map/ppermute | solution.py:349

commit v5 on v4

--- a/solution.py
+++ b/solution.py
@@ -39,9 +39,10 @@
     return high, middle, low
 
 
-def exact_dot(zero_one, value, dims):
+def exact_dot(zero_one, value, dims, terms=2):
     return sum(
-        lax.dot_general(zero_one, part, (dims, ((), ())), preferred_element_type=F32) for part in split3(value)
+        lax.dot_general(zero_one, part, (dims, ((), ())), preferred_element_type=F32)
+        for part in split3(value)[:terms]
     )
 
 
@@ -95,57 +96,60 @@
     )(*arrays)
 
 
-def ends_kernel(chunk, *refs):
+def fill_packet(place, chunk, x_ref, keys, factor, sums, packet_ref):
     core = position()[0]
-    halves = (1 - core, core)
-    if chunk == 0:
-        sources, refs = refs[0:5], refs[5:]
-        sent_ref, kept_ref, factor_ref, sum_ref = refs[0:4]
-        decay_ref, key_ref, query_ref, mix_ref = refs[4:8]
-        x_refs, (small, big) = refs[8 : 8 + CHUNKS], refs[8 + CHUNKS :]
-        x_ref = x_refs[0]
-        copies = [
-            pltpu.make_async_copy(source, target, small.at[place])
-            for place, (source, target) in enumerate(zip(sources, (decay_ref, key_ref, query_ref, mix_ref)))
-        ]
-        for part in range(CHUNKS):
-            for place, half in enumerate(halves):
-                columns = pl.ds(pl.multiple_of(half * (CHUNKS * WIDTH) + part * WIDTH, WIDTH), WIDTH)
-                copies.append(
-                    pltpu.make_async_copy(sources[4].at[:, columns], x_refs[part].at[place], big.at[2 * part + place])
-                )
-        for place in (0, 1, *range(4, 4 + 2 * CHUNKS), 2, 3):
-            copies[place].start()
-        copies[0].wait()
-        decay = pad_heads(decay_ref[...])
-        after = exact_dot(triangle(lambda r, c: c > r), decay, ((1,), (1,)))
-        sums = exact_dot(jnp.ones((16, TOK), BF16), decay, ((1,), (1,)))
-        factor = jnp.exp(after)
-        factor_ref[...] = factor
-        sum_ref[...] = sums
-        copies[1].wait()
-    else:
-        x_ref, key_ref, factor_ref, sum_ref, sent_ref, kept_ref = refs
-        factor = factor_ref[...]
-        sums = sum_ref[...]
+    first = (core if place == 1 else 1 - core) * SHARE
     lane = lax.broadcasted_iota(jnp.int32, sums.shape, 1)
-    keys = key_ref[...]
-    for place, (half, packet_ref) in enumerate(zip(halves, (sent_ref, kept_ref))):
-        packet_ref[BODY:PACK] = total_rows(jnp.take_along_axis(sums, (lane + half * SHARE) & 127, axis=1))
-        if chunk == 0:
-            copies[4 + place].wait()
-        for duo in range(PAIRS // 2):
-            pieces = []
-            for pair in (2 * duo, 2 * duo + 1):
-                x = x_ref[place, :, pair * 128 : pair * 128 + 128].astype(F32)
-                pieces.append((x * spread(factor, half * SHARE + (chunk * PAIRS + pair) * 2)).astype(BF16))
-            decayed = jnp.concatenate(pieces, axis=1)
-            state = lax.dot_general(keys, decayed, (((0,), (0,)), ((), ())), preferred_element_type=F32)
-            packet_ref[duo * 256 : duo * 256 + 128] = state[:, 0:128].astype(BF16)
-            packet_ref[duo * 256 + 128 : duo * 256 + 256] = state[:, 128:256].astype(BF16)
-    if chunk == 0:
-        for copy in copies[2:4] + copies[6:]:
-            copy.wait()
+    packet_ref[BODY:PACK] = total_rows(jnp.take_along_axis(sums, (lane + first) & 127, axis=1))
+    for duo in range(PAIRS // 2):
+        pieces = []
+        for pair in (2 * duo, 2 * duo + 1):
+            x = x_ref[place, :, pair * 128 : pair * 128 + 128].astype(F32)
+            pieces.append((x * spread(factor, first + (chunk * PAIRS + pair) * 2)).astype(BF16))
+        decayed = jnp.concatenate(pieces, axis=1)
+        state = lax.dot_general(keys, decayed, (((0,), (0,)), ((), ())), preferred_element_type=F32)
+        packet_ref[duo * 256 : duo * 256 + 128] = state[:, 0:128].astype(BF16)
+        packet_ref[duo * 256 + 128 : duo * 256 + 256] = state[:, 128:256].astype(BF16)
+
+
+def fetch_kernel(*refs):
+    sources, sent_ref, factor_ref, sum_ref = refs[0:5], *refs[5:8]
+    targets, x_refs, (small, big) = refs[8:12], refs[12 : 12 + CHUNKS], refs[12 + CHUNKS :]
+    core = position()[0]
+    copies = [
+        pltpu.make_async_copy(source, target, small.at[place])
+        for place, (source, target) in enumerate(zip(sources, targets))
+    ]
+    for chunk in range(CHUNKS):
+        for place, half in enumerate((1 - core, core)):
+            columns = pl.ds(pl.multiple_of(half * (CHUNKS * WIDTH) + chunk * WIDTH, WIDTH), WIDTH)
+            copies.append(
+                pltpu.make_async_copy(sources[4].at[:, columns], x_refs[chunk].at[place], big.at[2 * chunk + place])
+            )
+    for place in (0, 4, 1, *range(5, 4 + 2 * CHUNKS), 2, 3):
+        copies[place].start()
+    later = triangle(lambda r, c: c > r)
+    copies[0].wait()
+    decay = pad_heads(targets[0][...])
+    factor = jnp.exp(exact_dot(later, decay, ((1,), (1,))))
+    sums = exact_dot(jnp.ones((16, TOK), BF16), decay, ((1,), (1,)), 3)
+    factor_ref[...] = factor
+    sum_ref[...] = sums
+    copies[1].wait()
+    copies[4].wait()
+    fill_packet(0, 0, x_refs[0], targets[1][...], factor, sums, sent_ref)
+    for copy in copies[2:4] + copies[5:]:
+        copy.wait()
+
+
+def ends_kernel(place, chunk, x_ref, key_ref, factor_ref, sum_ref, packet_ref):
+    fill_packet(place, chunk, x_ref, key_ref[...], factor_ref[...], sum_ref[...], packet_ref)
+
+
+def make_ends(place, chunk, *arrays):
+    return call(
+        functools.partial(ends_kernel, place, chunk), [PACKET], arrays, "ends", 2 * TOK * STATE * WIDTH, kept=range(4)
+    )[0]
 
 
 def merge_kernel(bit, chunk, *refs):
@@ -322,31 +326,45 @@
     )[0]
 
 
-def finish_kernel(*refs):
-    done, totals, parts = refs[:CHUNKS], refs[CHUNKS : 2 * CHUNKS], refs[2 * CHUNKS : 3 * CHUNKS]
-    out_ref, buffer, sems = refs[3 * CHUNKS :]
+def finish_kernel(first, *refs):
+    out_ref, buffer, sems = refs[-3:]
     core = position()[0]
     copies = []
 
-    def send(source, half, chunk):
-        columns = pl.ds(pl.multiple_of(half * (CHUNKS * WIDTH) + chunk * WIDTH, WIDTH), WIDTH)
+    def send(source, half, chunk, start, width):
+        columns = pl.ds(pl.multiple_of(half * (CHUNKS * WIDTH) + chunk * WIDTH + start, 256), width)
         copies.append(pltpu.make_async_copy(source, out_ref.at[:, columns], sems.at[len(copies)]))
         copies[-1].start()
 
-    for chunk in range(CHUNKS):
-        send(done[chunk], core, chunk)
-    for chunk in range(CHUNKS):
-        buffer[chunk] = (totals[chunk][...] + parts[chunk][...].astype(F32)).astype(BF16)
-        send(buffer.at[chunk], 1 - core, chunk)
+    if first:
+        for chunk in range(CHUNKS):
+            send(refs[chunk], core, chunk, 0, WIDTH)
+        rest_ref, part_ref, chunk = refs[CHUNKS], refs[CHUNKS + 1], 0
+    else:
+        rest_ref, part_ref, chunk = refs[0], refs[1], CHUNKS - 1
+    for piece in range(WIDTH // 256):
+        lanes = slice(piece * 256, piece * 256 + 256)
+        buffer[piece] = (rest_ref[:, lanes] + part_ref[:, lanes].astype(F32)).astype(BF16)
+        send(buffer.at[piece], 1 - core, chunk, piece * 256, 256)
     for copy in copies:
         copy.wait()
 
 
+def finish(first, arrays, out=None):
+    count = len(arrays)
+    return call(
+        functools.partial(finish_kernel, first), [jax.ShapeDtypeStruct((TOK, HEADS * HEAD), BF16)],
+        [*arrays] if first else [*arrays, out], "finish", TOK * WIDTH, kept=range(count),
+        far=() if first else (count,), out_specs=[ANY], aliases=None if first else {count: 0},
+        scratch=[pltpu.VMEM((WIDTH // 256, TOK, 256), BF16), pltpu.SemaphoreType.DMA((CHUNKS + WIDTH // 256,))],
+    )[0]
+
+
 def body(inputs, write_keys, read_queries, decay_log, level_mix):
     devices = lax.axis_size("ctx")
 
-    def swap(array, mask):
-        return lax.ppermute(array, "ctx", [(i, i ^ mask) for i in range(devices)])
+    def swap(array, mask, senders=None):
+        return lax.ppermute(array, "ctx", [(i, i ^ mask) for i in range(senders or devices)])
 
     def after(*arrays):
         return lax.optimization_barrier(arrays)
@@ -355,35 +373,34 @@
     masks = (1, 2, 6, 8, 24)
     kept, x, got, state, packet = ([None] * CHUNKS for _ in range(5))
     history = [[] for _ in chunks]
-    for c in chunks:
-        kernel, flops = functools.partial(ends_kernel, c), 4 * TOK * STATE * WIDTH
-        if c == 0:
-            sent, kept[c], factor, sums, decay, keys, queries, mix, *x = call(
-                kernel,
-                [
-                    PACKET, PACKET, TABLE, pltpu.VMEM((16, 128), F32), pltpu.VMEM((HEADS, TOK), F32),
-                    pltpu.VMEM((TOK, STATE), BF16), pltpu.VMEM((TOK, STATE), BF16),
-                    pltpu.VMEM((LEVELS + 1, HEADS, TOK), F32),
-                ] + [X_PART] * CHUNKS,
-                [decay_log, write_keys, read_queries, level_mix, inputs], "ends", flops, 32768, far=range(5),
-                scratch=[pltpu.SemaphoreType.DMA((4,)), pltpu.SemaphoreType.DMA((2 * CHUNKS,))],
-            )
-        else:
-            sent, kept[c] = call(
-                kernel, [PACKET, PACKET], [x[c], keys, factor, sums], "ends", flops, kept=range(4)
-            )
-            got[c - 1], sent = after(got[c - 1], sent)
+    sent, factor, sums, decay, keys, queries, mix, *x = call(
+        fetch_kernel,
+        [
+            PACKET, TABLE, pltpu.VMEM((16, 128), F32), pltpu.VMEM((HEADS, TOK), F32), pltpu.VMEM((TOK, STATE), BF16),
+            pltpu.VMEM((TOK, STATE), BF16), pltpu.VMEM((LEVELS + 1, HEADS, TOK), F32),
+        ] + [X_PART] * CHUNKS,
+        [decay_log, write_keys, read_queries, level_mix, inputs], "fetch", 2 * TOK * STATE * WIDTH, far=range(5),
+        scratch=[pltpu.SemaphoreType.DMA((4,)), pltpu.SemaphoreType.DMA((2 * CHUNKS,))],
+    )
+    got[0] = swap(sent, masks[0])
+    for c in chunks[1:]:
+        sent = make_ends(0, c, x[c], keys, factor, sums)
         got[c] = swap(sent, masks[0])
+    x[0], _ = after(x[0], sent)
+    kept[0] = make_ends(1, 0, x[0], keys, factor, sums)
 
     def advance(level, c):
         if c > 0:
             got[c], _ = after(got[c], packet[c - 1])
+            if level == 0:
+                x[c], _ = after(x[c], packet[c - 1])
+                kept[c] = make_ends(1, c, x[c], keys, factor, sums)
         history[c].append(got[c])
         if level == 0:
             packet[c], *state[c] = merge(0, c, kept[c], got[c])
         else:
             packet[c], *state[c] = merge(level, c, *state[c], got[c])
-        got[c] = swap(packet[c], masks[level + 1])
+        got[c] = swap(packet[c], masks[level + 1], devices // 2 if level == 3 and c in (0, 1) else None)
 
     for c in chunks:
         advance(0, c)
@@ -396,39 +413,48 @@
         [decay, mix, keys, queries], "tables", 4 * TOK * TOK * STATE, 16384, kept=range(4),
     )
     far = swap(tables, 1)
-    total, rest = [None] * CHUNKS, [None] * CHUNKS
-    for level, place, results in ((1, 1, total), (2, 0, rest)):
-        for c in chunks:
-            if c > 0:
-                x[c], _ = after(x[c], packet[c - 1])
-            results[c] = make_local(place, c, scores, column, row, x[c])
-            got[c], results[c], far = after(got[c], results[c], far)
-            advance(level, c)
-    shared = (queries, weights, far)
-    far_total, gap, far_gap = [None] * CHUNKS, [None] * CHUNKS, [None] * CHUNKS
-    for c in chunks:
-        if c > 0:
-            total[c], _ = after(total[c], packet[c - 1])
-        total[c], far_total[c], gap[c], far_gap[c] = add_levels((0, 1, 2), c, *shared, total[c], kept[c], *history[c])
-        got[c], total[c] = after(got[c], total[c])
+    local = (scores, column, row)
+    levels = [None] * CHUNKS
+
+    def add(wanted, c):
+        arrays = [*levels[c], *(history[c][level] for level in wanted)]
+        levels[c] = add_levels(wanted, c, queries, weights, far, *arrays)
+
+    for c in chunks:
+        levels[c] = [make_local(1, c, *local, x[c]), kept[c]]
+    got[0], far, *levels = after(got[0], far, *levels)
+    for c in chunks:
+        advance(1, c)
+    rest = [None] * CHUNKS
+    x[0], levels[0], _ = after(x[0], levels[0], packet[1])
+    add((0, 1), 0)
+    rest[0] = make_local(0, 0, *local, x[0])
+    got[0], levels[0], rest[0] = after(got[0], levels[0], rest[0])
+    for c in chunks:
+        advance(2, c)
+    x[1], levels[0], levels[1], _ = after(x[1], *levels, packet[1])
+    add((0, 1), 1)
+    add((2,), 0)
+    rest[1] = make_local(0, 1, *local, x[1])
+    got[0], levels[0], levels[1], rest[1] = after(got[0], *levels, rest[1])
+    for c in chunks:
         advance(3, c)
+    levels[0], levels[1], _ = after(*levels, packet[1])
+    add((3,), 0)
+    add((2, 3), 1)
+    got[0], levels[0], levels[1] = after(got[0], *levels)
     done, parts = [None] * CHUNKS, [None] * CHUNKS
     for c in chunks:
-        total[c], far_total[c], gap[c], far_gap[c] = add_levels(
-            (3,), c, *shared, total[c], far_total[c], gap[c], far_gap[c], history[c][3]
-        )
-        got[c], total[c] = after(got[c], total[c])
-        part = add_last(True, c, far, far_total[c], far_gap[c], got[c])
+        total, far_total, gap, far_gap = levels[c]
+        part = add_last(True, c, far, far_total, far_gap, got[c])
         parts[c] = swap(part, 1)
         late, _ = after(got[c], part)
-        done[c] = add_last(False, c, queries, weights, total[c], gap[c], late)
-        parts[c], done[c] = after(parts[c], done[c])
-    out, = call(
-        finish_kernel, [jax.ShapeDtypeStruct((TOK, HEADS * HEAD), BF16)], [*done, *rest, *parts], "finish",
-        TOK * CHUNKS * WIDTH, kept=range(3 * CHUNKS), out_specs=[ANY],
-        scratch=[pltpu.VMEM((CHUNKS, TOK, WIDTH), BF16), pltpu.SemaphoreType.DMA((2 * CHUNKS,))],
-    )
-    return out
+        done[c] = add_last(False, c, queries, weights, total, gap, late)
+        if c == 0:
+            got[1], done[0] = after(got[1], done[0])
+    out = finish(True, [*done, rest[0], parts[0]])
+    parts[1], out = after(parts[1], out)
+    return finish(False, [rest[1], parts[1]], out)
 
 
 def solution(mesh):

time: 39.1 us -> 37 us (0.946); the launches traced: 39 us -> 36.5 us
  waiting for transfers between devices: 10.7 us -> 5.28 us
  starting transfers between devices: 15.6 us -> 17.5 us
  Pallas kernels: 12.4 us -> 13.3 us
    ppermute x13, waiting for transfers between devices: 10.7 us -> 5.28 us  [swap(): lax.ppermute(array, 'ctx', [(i, i ^ mask) for i in range(senders or devic...]
    ppermute x13, starting transfers between devices: 15.6 us -> 17.5 us  [swap(): lax.ppermute(array, 'ctx', [(i, i ^ mask) for i in range(senders or devic...]
    pallas_call x24 -> x28, Pallas kernels: 12.4 us -> 13.3 us  [call(): pl.pallas_call(kernel, out_shape=outs, in_specs=[ANY if place in far else...]
  transfers between devices with their start and end apart: 13 -> 13, of which waited for: 8 -> 5; matrix products, arithmetic and copies ran while one was open for 0% -> 0% of each run, Pallas kernels for 23% -> 30%
where the time goes in v5:
time: 37 us; the launch traced here: 36.5 us
  starting transfers between devices  17.5 us (47%)
  Pallas kernels  13.3 us (36%)
  waiting for transfers between devices  5.28 us (14%)
  between operations  0.41 us (1%)
    ppermute x13, starting transfers between devices, swap(): lax.ppermute(array, 'ctx', [(i, i ^ mask) for i in range(senders or devic...  17.5 us
    pallas_call x28, Pallas kernels, call(): pl.pallas_call(kernel, out_shape=outs, in_specs=[ANY if place in far else...  13.3 us
    ppermute x13, waiting for transfers between devices, swap(): lax.ppermute(array, 'ctx', [(i, i ^ mask) for i in range(senders or devic...  5.28 us
  transfers between devices with their start and end apart: 13, of which 5 were waited for; matrix products, arithmetic and copies ran while one was open for 0% of the time, Pallas kernels for 30%

profile of v5, /device:TPU:1, one launch (start us, length us, event | category | flops | bytes accessed | tf_op | source)
XLA Modules:
  0.0 36.5 jit_solution(13968480852994006124)
XLA Ops:
  0.0 1.6 %fetch.1 = (bf16[528,128]{1,0:T(8,128)(2,1)S(1)}, f32[256,128]{1,0:T(8,128)S(1)}, f32[16,128]{1,0:T(8,128)S(1)}, f32[32,256]{1,0:T(8,128)S(1)}, bf16[256,128]{1,...) custom-call(f32[32,256]{1,0:T(8,128)} %refs_0_.1, ...), custom_call_target="tpu_custom_call" | custom-call | flops 3355443200 | bytes 1024 | tf_op jit(solution)/shard_map/fetch/pallas_call | solution.py:86
  1.6 3.3 %collective-permute-start = (bf16[528,128]{1,0:T(8,128)(2,1)S(1)}, bf16[528,128]{1,0:T(8,128)(2,1)S(1)}, u32[]{:S(2)}, u32[]{:S(2)}) collective-permute-start(bf16[528,128]{1,0:T(8,128)(2,1)S(1)} %get-tuple-element.126), channel_id=1, source_target_pairs={{0,1},{1,0},{2,3},{3,2},{4,5},{5,4},{6,7},{7,6},{8,9},{9,8},{10,11... | collective-permute-start | bytes 405512 | tf_op jit(solution)/shard_map/ppermute | solution.py:367
  5.0 0.5 %ends.3 = bf16[528,128]{1,0:T(8,128)(2,1)S(1)} custom-call(bf16[2,256,512]{2,1,0:T(8,128)(2,1)S(1)} %get-tuple-element.187.x_ref, bf16[256,128]{1,0:T(8,128)(2,1)S(1)} %get-tuple-element.122.key_ref, f32[256,128]{1,0:T(8,128)S(1)} %get-tuple-element.123.factor_ref, f32[16,128]{1,0:T(8,128)S(1)} %get-tuple-element.124.sum_ref), custom_call_target="tpu_custom_call" | custom-call | flops 3355443200 | bytes 1024 | tf_op jit(solution)/shard_map/ends/pallas_call | solution.py:86
  5.6 0.5 %ends.4.refs_0_.refs_4_ = bf16[528,128]{1,0:T(8,128)(2,1)S(1)} custom-call(bf16[2,256,512]{2,1,0:T(8,128)(2,1)S(1)} %get-tuple-element.160.x_ref, bf16[256,128]{1,0:T(8,128)(2,1)S(1)} %get-tuple-element.122.key_ref, f32[256,128]{1,0:T(8,128)S(1)} %get-tuple-element.123.factor_ref, f32[16,128]{1,0:T(8,128)S(1)} %get-tuple-element.124.sum_ref), custom_call_target="tpu_custom_call" | custom-call | flops 3355443200 | bytes 1024 | tf_op jit(solution)/shard_map/ends/pallas_call | solution.py:86
  6.3 0.5 %ends.5.refs_0_.refs_4_ = bf16[528,128]{1,0:T(8,128)(2,1)S(1)} custom-call(bf16[2,256,512]{2,1,0:T(8,128)(2,1)S(1)} %get-tuple-element.187.x_ref, bf16[256,128]{1,0:T(8,128)(2,1)S(1)} %get-tuple-element.122.key_ref, f32[256,128]{1,0:T(8,128)S(1)} %get-tuple-element.123.factor_ref, f32[16,128]{1,0:T(8,128)S(1)} %get-tuple-element.124.sum_ref), custom_call_target="tpu_custom_call" | custom-call | flops 3355443200 | bytes 1024 | tf_op jit(solution)/shard_map/ends/pallas_call | solution.py:86
  7.0 1.5 %collective-permute-start.5 = (bf16[528,128]{1,0:T(8,128)(2,1)S(1)}, bf16[528,128]{1,0:T(8,128)(2,1)S(1)}, u32[]{:S(2)}, u32[]{:S(2)}) collective-permute-start(bf16[528,128]{1,0:T(8,128)(2,1)S(1)} %get-tuple-element.135), channel_id=1, source_target_pairs={{0,2},{1,3},{2,0},{3,1},{4,6},{5,7},{6,4},{7,5},{8,10},{9,11},{10,... | collective-permute-start | bytes 405512 | tf_op jit(solution)/shard_map/ppermute | solution.py:367
  8.5 0.4 %tables.1 = (f32[256,256]{1,0:T(8,128)S(1)}, f32[256,128]{1,0:T(8,128)S(1)}, f32[32,256]{1,0:T(8,128)S(1)}, f32[256,128]{1,0:T(8,128)S(1)}, bf16[256,384]{1,0:T(8,128)(2,1)S(1)}) custom-call(f32[32,256]{1,0:T(8,128)S(1)} %get-tuple-element.130.decay_ref, f32[6,32,256]{2,1,0:T(8,128)S(1)} %get-tuple-element.136.mix_ref, ...), custom_call_target="tpu_custom_call" | custom-call | flops 3355443200 | bytes 1024 | tf_op jit(solution)/shard_map/tables/pallas_call | solution.py:86
  8.9 1.1 %collective-permute-start.3 = (bf16[256,384]{1,0:T(8,128)(2,1)S(1)}, bf16[256,384]{1,0:T(8,128)(2,1)S(1)}, u32[]{:S(2)}, u32[]{:S(2)}) collective-permute-start(bf16[256,384]{1,0:T(8,128)(2,1)S(1)} %get-tuple-element.138), channel_id=1, source_target_pairs={{0,1},{1,0},{2,3},{3,2},{4,5},{5,4},{6,7},{7,6},{8,9},{9,8},{10,11... | collective-permute-start | bytes 589832 | tf_op jit(solution)/shard_map/ppermute | solution.py:367
  10.1 0.6 %local.5.refs_3_ = f32[256,512]{1,0:T(8,128)S(1)} custom-call(f32[256,256]{1,0:T(8,128)S(1)} %get-tuple-element.139.scores_ref, f32[256,128]{1,0:T(8,128)S(1)} %get-tuple-element.140.column_ref, f32[32,256]{1,0:T(8,128)S(1)} %get-tuple-element.141.row_ref, bf16[2,256,512]{2,1,0:T(8,128)(2,1)S(1)} %get-tuple-element.187.x_ref), custom_call_target="tpu_custom_call" | custom-call | flops 13421772800 | bytes 1024 | tf_op jit(solution)/shard_map/local/pallas_call | solution.py:86
  10.7 0.6 %local.4.refs_3_ = f32[256,512]{1,0:T(8,128)S(1)} custom-call(f32[256,256]{1,0:T(8,128)S(1)} %get-tuple-element.139.scores_ref, f32[256,128]{1,0:T(8,128)S(1)} %get-tuple-element.140.column_ref, f32[32,256]{1,0:T(8,128)S(1)} %get-tuple-element.141.row_ref, bf16[2,256,512]{2,1,0:T(8,128)(2,1)S(1)} %get-tuple-element.160.x_ref), custom_call_target="tpu_custom_call" | custom-call | flops 13421772800 | bytes 1024 | tf_op jit(solution)/shard_map/local/pallas_call | solution.py:86
  11.4 0.8 %collective-permute-start.4 = (bf16[528,128]{1,0:T(8,128)(2,1)S(1)}, bf16[528,128]{1,0:T(8,128)(2,1)S(1)}, u32[]{:S(2)}, u32[]{:S(2)}) collective-permute-start(bf16[528,128]{1,0:T(8,128)(2,1)S(1)} %get-tuple-element.145), channel_id=1, source_target_pairs={{0,6},{1,7},{2,4},{3,5},{4,2},{5,3},{6,0},{7,1},{8,14},{9,15},{10,... | collective-permute-start | bytes 405512 | tf_op jit(solution)/shard_map/ppermute | solution.py:367
  12.3 1.6 %collective-permute-done.5.refs_2_.refs_6_ = bf16[528,128]{1,0:T(8,128)(2,1)S(1)} collective-permute-done((bf16[528,128]{1,0:T(8,128)(2,1)S(1)}, bf16[528,128]{1,0:T(8,128)(2,1)S(1)}, u32[]{:S(2)}, u32[]{:S(2)}) %collective-permute-start.5) | collective-permute-done | bytes 135200 | tf_op jit(solution)/shard_map/ppermute | solution.py:367
  14.0 0.8 %collective-permute-start.7 = (bf16[528,128]{1,0:T(8,128)(2,1)S(1)}, bf16[528,128]{1,0:T(8,128)(2,1)S(1)}, u32[]{:S(2)}, u32[]{:S(2)}) collective-permute-start(bf16[528,128]{1,0:T(8,128)(2,1)S(1)} %get-tuple-element.153), channel_id=1, source_target_pairs={{0,6},{1,7},{2,4},{3,5},{4,2},{5,3},{6,0},{7,1},{8,14},{9,15},{10,... | collective-permute-start | bytes 405512 | tf_op jit(solution)/shard_map/ppermute | solution.py:367
  14.8 0.6 %local.6.refs_2_ = f32[256,512]{1,0:T(8,128)S(1)} custom-call(f32[256,256]{1,0:T(8,128)S(1)} %get-tuple-element.139.scores_ref, f32[256,128]{1,0:T(8,128)S(1)} %get-tuple-element.140.column_ref, f32[32,256]{1,0:T(8,128)S(1)} %get-tuple-element.141.row_ref, bf16[2,256,512]{2,1,0:T(8,128)(2,1)S(1)} %get-tuple-element.160.x_ref), custom_call_target="tpu_custom_call" | custom-call | flops 13421772800 | bytes 1024 | tf_op jit(solution)/shard_map/local/pallas_call | solution.py:86
  15.4 0.8 %levels.5 = (f32[256,512]{1,0:T(8,128)S(1)}, f32[256,512]{1,0:T(8,128)S(1)}, f32[8,128]{1,0:T(8,128)S(1)}, f32[8,128]{1,0:T(8,128)S(1)}) custom-call(bf16[256,128]{1,0:T(8,128)(2,1)S(1)} %get-tuple-element.137.query_ref.refs_0_, f32[256,128]{1,0:T(8,128)S(1)} %get-tuple-element.146.refs_1_, bf16[256,384]{1,0:T(8,128)(2,1)S(1)} %collective-permute-done.3.refs_2_.refs_0_, ...), custom_call_target="tpu_custom_call" | custom-call | flops 13421772800 | bytes 1024 | tf_op jit(solution)/shard_map/levels/pallas_call | solution.py:86
  16.2 0.4 %collective-permute-done.4.refs_2_.refs_7_ = bf16[528,128]{1,0:T(8,128)(2,1)S(1)} collective-permute-done((bf16[528,128]{1,0:T(8,128)(2,1)S(1)}, bf16[528,128]{1,0:T(8,128)(2,1)S(1)}, u32[]{:S(2)}, u32[]{:S(2)}) %collective-permute-start.4) | collective-permute-done | bytes 135200 | tf_op jit(solution)/shard_map/ppermute | solution.py:367
  16.7 1.0 %collective-permute-start.6 = (bf16[528,128]{1,0:T(8,128)(2,1)S(1)}, bf16[528,128]{1,0:T(8,128)(2,1)S(1)}, u32[]{:S(2)}, u32[]{:S(2)}) collective-permute-start(bf16[528,128]{1,0:T(8,128)(2,1)S(1)} %get-tuple-element.162), channel_id=1, source_target_pairs={{0,8},{1,9},{2,10},{3,11},{4,12},{5,13},{6,14},{7,15},{8,0},{9,1},... | collective-permute-start | bytes 405512 | tf_op jit(solution)/shard_map/ppermute | solution.py:367
  17.8 3.1 %collective-permute-done.7.refs_2_.refs_7_ = bf16[528,128]{1,0:T(8,128)(2,1)S(1)} collective-permute-done((bf16[528,128]{1,0:T(8,128)(2,1)S(1)}, bf16[528,128]{1,0:T(8,128)(2,1)S(1)}, u32[]{:S(2)}, u32[]{:S(2)}) %collective-permute-start.7) | collective-permute-done | bytes 135200 | tf_op jit(solution)/shard_map/ppermute | solution.py:367
  21.1 0.6 %local.7.refs_0_ = f32[256,512]{1,0:T(8,128)S(1)} custom-call(f32[256,256]{1,0:T(8,128)S(1)} %get-tuple-element.139.scores_ref, f32[256,128]{1,0:T(8,128)S(1)} %get-tuple-element.140.column_ref, f32[32,256]{1,0:T(8,128)S(1)} %get-tuple-element.141.row_ref, bf16[2,256,512]{2,1,0:T(8,128)(2,1)S(1)} %get-tuple-element.187.x_ref), custom_call_target="tpu_custom_call" | custom-call | flops 13421772800 | bytes 1024 | tf_op jit(solution)/shard_map/local/pallas_call | solution.py:86
  21.7 0.9 %levels.7 = (f32[256,512]{1,0:T(8,128)S(1)}, f32[256,512]{1,0:T(8,128)S(1)}, f32[8,128]{1,0:T(8,128)S(1)}, f32[8,128]{1,0:T(8,128)S(1)}) custom-call(bf16[256,128]{1,0:T(8,128)(2,1)S(1)} %get-tuple-element.137.query_ref.refs_0_, f32[256,128]{1,0:T(8,128)S(1)} %get-tuple-element.146.refs_1_, bf16[256,384]{1,0:T(8,128)(2,1)S(1)} %collective-permute-done.3.refs_2_.refs_0_, ...), custom_call_target="tpu_custom_call" | custom-call | flops 13421772800 | bytes 1024 | tf_op jit(solution)/shard_map/levels/pallas_call | solution.py:86
  22.6 0.5 %levels.6 = (f32[256,512]{1,0:T(8,128)S(1)}, f32[256,512]{1,0:T(8,128)S(1)}, f32[8,128]{1,0:T(8,128)S(1)}, f32[8,128]{1,0:T(8,128)S(1)}) custom-call(bf16[256,128]{1,0:T(8,128)(2,1)S(1)} %get-tuple-element.137.query_ref.refs_0_, f32[256,128]{1,0:T(8,128)S(1)} %get-tuple-element.146.refs_1_, bf16[256,384]{1,0:T(8,128)(2,1)S(1)} %collective-permute-done.3.refs_2_.refs_0_, ...), custom_call_target="tpu_custom_call" | custom-call | flops 6710886400 | bytes 1024 | tf_op jit(solution)/shard_map/levels/pallas_call | solution.py:86
  23.2 2.9 %collective-permute-start.8 = (bf16[528,128]{1,0:T(8,128)(2,1)S(1)}, bf16[528,128]{1,0:T(8,128)(2,1)S(1)}, u32[]{:S(2)}, u32[]{:S(2)}) collective-permute-start(bf16[528,128]{1,0:T(8,128)(2,1)S(1)} %merge.14), channel_id=1, source_target_pairs={{0,24},{1,25},{2,26},{3,27},{4,28},{5,29},{6,30},{7,31},{8,16},{9,... | collective-permute-start | bytes 405512 | tf_op jit(solution)/shard_map/ppermute | solution.py:367
  26.4 2.3 %collective-permute-start.10 = (bf16[528,128]{1,0:T(8,128)(2,1)S(1)}, bf16[528,128]{1,0:T(8,128)(2,1)S(1)}, u32[]{:S(2)}, u32[]{:S(2)}) collective-permute-start(bf16[528,128]{1,0:T(8,128)(2,1)S(1)} %merge.15), channel_id=1, source_target_pairs={{0,24},{1,25},{2,26},{3,27},{4,28},{5,29},{6,30},{7,31},{8,16},{9,... | collective-permute-start | bytes 405512 | tf_op jit(solution)/shard_map/ppermute | solution.py:367
  28.7 0.9 %levels.9 = (f32[256,512]{1,0:T(8,128)S(1)}, f32[256,512]{1,0:T(8,128)S(1)}, f32[8,128]{1,0:T(8,128)S(1)}, f32[8,128]{1,0:T(8,128)S(1)}) custom-call(bf16[256,128]{1,0:T(8,128)(2,1)S(1)} %get-tuple-element.137.query_ref.refs_0_, f32[256,128]{1,0:T(8,128)S(1)} %get-tuple-element.146.refs_1_, bf16[256,384]{1,0:T(8,128)(2,1)S(1)} %collective-permute-done.3.refs_2_.refs_0_, ...), custom_call_target="tpu_custom_call" | custom-call | flops 13421772800 | bytes 1024 | tf_op jit(solution)/shard_map/levels/pallas_call | solution.py:86
  29.5 0.5 %levels.8 = (f32[256,512]{1,0:T(8,128)S(1)}, f32[256,512]{1,0:T(8,128)S(1)}, f32[8,128]{1,0:T(8,128)S(1)}, f32[8,128]{1,0:T(8,128)S(1)}) custom-call(bf16[256,128]{1,0:T(8,128)(2,1)S(1)} %get-tuple-element.137.query_ref.refs_0_, f32[256,128]{1,0:T(8,128)S(1)} %get-tuple-element.146.refs_1_, bf16[256,384]{1,0:T(8,128)(2,1)S(1)} %collective-permute-done.3.refs_2_.refs_0_, ...), custom_call_target="tpu_custom_call" | custom-call | flops 6710886400 | bytes 1024 | tf_op jit(solution)/shard_map/levels/pallas_call | solution.py:86
  30.1 0.3 last.4
  30.3 3.0 %collective-permute-start.12 = (bf16[256,512]{1,0:T(8,128)(2,1)S(1)}, bf16[256,512]{1,0:T(8,128)(2,1)S(1)}, u32[]{:S(2)}, u32[]{:S(2)}) collective-permute-start(bf16[256,512]{1,0:T(8,128)(2,1)S(1)} %last.4), channel_id=1, source_target_pairs={{0,1},{1,0},{2,3},{3,2},{4,5},{5,4},{6,7},{7,6},{8,9},{9,8},{10,11... | collective-permute-start | bytes 786440 | tf_op jit(solution)/shard_map/ppermute | solution.py:367
  33.6 0.3 last.6
  33.9 0.4 %collective-permute-start.11 = (bf16[256,512]{1,0:T(8,128)(2,1)S(1)}, bf16[256,512]{1,0:T(8,128)(2,1)S(1)}, u32[]{:S(2)}, u32[]{:S(2)}) collective-permute-start(bf16[256,512]{1,0:T(8,128)(2,1)S(1)} %last.6), channel_id=1, source_target_pairs={{0,1},{1,0},{2,3},{3,2},{4,5},{5,4},{6,7},{7,6},{8,9},{9,8},{10,11... | collective-permute-start | bytes 786440 | tf_op jit(solution)/shard_map/ppermute | solution.py:367
  34.3 0.3 last.7.refs_1_
  34.6 0.9 %finish.2.refs_2_ = bf16[256,2048]{1,0:T(8,128)(2,1)} custom-call(bf16[256,512]{1,0:T(8,128)(2,1)S(1)} %last.5.refs_0_, bf16[256,512]{1,0:T(8,128)(2,1)S(1)} %last.7.refs_1_, f32[256,512]{1,0:T(8,128)S(1)} %local.6.refs_2_, bf16[256,512]{1,0:T(8,128)(2,1)S(1)} %collective-permute-done.12.refs_3_), custom_call_target="tpu_custom_call" | custom-call | flops 13107200 | bytes 1024 | tf_op jit(solution)/shard_map/finish/pallas_call | solution.py:86
  35.5 0.8 %finish.3 = bf16[256,2048]{1,0:T(8,128)(2,1)} custom-call(f32[256,512]{1,0:T(8,128)S(1)} %local.7.refs_0_, bf16[256,512]{1,0:T(8,128)(2,1)S(1)} %collective-permute-done.11.refs_1_, bf16[256,2048]{1,0:T(8,128)(2,1)} %finish.2.refs_2_), custom_call_target="tpu_custom_call", output_to_operand_aliasing={{}: (2, {})} | custom-call | flops 13107200 | bytes 1024 | tf_op jit(solution)/shard_map/finish/pallas_call | solution.py:86
  (22 shorter events, 1.7 us)
Async XLA Ops:
  1.6 4.4 %collective-permute-start = (bf16[528,128]{1,0:T(8,128)(2,1)S(1)}, bf16[528,128]{1,0:T(8,128)(2,1)S(1)}, u32[]{:S(2)}, u32[]{:S(2)}) collective-permute-start(bf16[528,128]{1,0:T(8,128)(2,1)S(1)} %get-tuple-element.126), channel_id=1, source_target_pairs={{0,1},{1,0},{2,3},{3,2},{4,5},{5,4},{6,7},{7,6},{8,9},{9,8},{10,11... | collective-permute-start | bytes 405512 | tf_op jit(solution)/shard_map/ppermute | solution.py:367
  5.5 1.4 %collective-permute-start.2 = (bf16[528,128]{1,0:T(8,128)(2,1)S(1)}, bf16[528,128]{1,0:T(8,128)(2,1)S(1)}, u32[]{:S(2)}, u32[]{:S(2)}) collective-permute-start(bf16[528,128]{1,0:T(8,128)(2,1)S(1)} %ends.3), channel_id=1, source_target_pairs={{0,1},{1,0},{2,3},{3,2},{4,5},{5,4},{6,7},{7,6},{8,9},{9,8},{10,11... | collective-permute-start | bytes 405512 | tf_op jit(solution)/shard_map/ppermute | solution.py:367
  6.2 5.1 %collective-permute-start.1 = (bf16[528,128]{1,0:T(8,128)(2,1)S(1)}, bf16[528,128]{1,0:T(8,128)(2,1)S(1)}, u32[]{:S(2)}, u32[]{:S(2)}) collective-permute-start(bf16[528,128]{1,0:T(8,128)(2,1)S(1)} %get-tuple-element.129), channel_id=1, source_target_pairs={{0,2},{1,3},{2,0},{3,1},{4,6},{5,7},{6,4},{7,5},{8,10},{9,11},{10,... | collective-permute-start | bytes 405512 | tf_op jit(solution)/shard_map/ppermute | solution.py:367
  7.0 6.8 %collective-permute-start.5 = (bf16[528,128]{1,0:T(8,128)(2,1)S(1)}, bf16[528,128]{1,0:T(8,128)(2,1)S(1)}, u32[]{:S(2)}, u32[]{:S(2)}) collective-permute-start(bf16[528,128]{1,0:T(8,128)(2,1)S(1)} %get-tuple-element.135), channel_id=1, source_target_pairs={{0,2},{1,3},{2,0},{3,1},{4,6},{5,7},{6,4},{7,5},{8,10},{9,11},{10,... | collective-permute-start | bytes 405512 | tf_op jit(solution)/shard_map/ppermute | solution.py:367
  8.9 2.4 %collective-permute-start.3 = (bf16[256,384]{1,0:T(8,128)(2,1)S(1)}, bf16[256,384]{1,0:T(8,128)(2,1)S(1)}, u32[]{:S(2)}, u32[]{:S(2)}) collective-permute-start(bf16[256,384]{1,0:T(8,128)(2,1)S(1)} %get-tuple-element.138), channel_id=1, source_target_pairs={{0,1},{1,0},{2,3},{3,2},{4,5},{5,4},{6,7},{7,6},{8,9},{9,8},{10,11... | collective-permute-start | bytes 589832 | tf_op jit(solution)/shard_map/ppermute | solution.py:367
  11.4 5.2 %collective-permute-start.4 = (bf16[528,128]{1,0:T(8,128)(2,1)S(1)}, bf16[528,128]{1,0:T(8,128)(2,1)S(1)}, u32[]{:S(2)}, u32[]{:S(2)}) collective-permute-start(bf16[528,128]{1,0:T(8,128)(2,1)S(1)} %get-tuple-element.145), channel_id=1, source_target_pairs={{0,6},{1,7},{2,4},{3,5},{4,2},{5,3},{6,0},{7,1},{8,14},{9,15},{10,... | collective-permute-start | bytes 405512 | tf_op jit(solution)/shard_map/ppermute | solution.py:367
  14.0 6.9 %collective-permute-start.7 = (bf16[528,128]{1,0:T(8,128)(2,1)S(1)}, bf16[528,128]{1,0:T(8,128)(2,1)S(1)}, u32[]{:S(2)}, u32[]{:S(2)}) collective-permute-start(bf16[528,128]{1,0:T(8,128)(2,1)S(1)} %get-tuple-element.153), channel_id=1, source_target_pairs={{0,6},{1,7},{2,4},{3,5},{4,2},{5,3},{6,0},{7,1},{8,14},{9,15},{10,... | collective-permute-start | bytes 405512 | tf_op jit(solution)/shard_map/ppermute | solution.py:367
  16.7 6.4 %collective-permute-start.6 = (bf16[528,128]{1,0:T(8,128)(2,1)S(1)}, bf16[528,128]{1,0:T(8,128)(2,1)S(1)}, u32[]{:S(2)}, u32[]{:S(2)}) collective-permute-start(bf16[528,128]{1,0:T(8,128)(2,1)S(1)} %get-tuple-element.162), channel_id=1, source_target_pairs={{0,8},{1,9},{2,10},{3,11},{4,12},{5,13},{6,14},{7,15},{8,0},{9,1},... | collective-permute-start | bytes 405512 | tf_op jit(solution)/shard_map/ppermute | solution.py:367
  21.0 5.2 %collective-permute-start.9 = (bf16[528,128]{1,0:T(8,128)(2,1)S(1)}, bf16[528,128]{1,0:T(8,128)(2,1)S(1)}, u32[]{:S(2)}, u32[]{:S(2)}) collective-permute-start(bf16[528,128]{1,0:T(8,128)(2,1)S(1)} %get-tuple-element.172), channel_id=1, source_target_pairs={{0,8},{1,9},{2,10},{3,11},{4,12},{5,13},{6,14},{7,15},{8,0},{9,1},... | collective-permute-start | bytes 405512 | tf_op jit(solution)/shard_map/ppermute | solution.py:367
  23.2 6.8 %collective-permute-start.8 = (bf16[528,128]{1,0:T(8,128)(2,1)S(1)}, bf16[528,128]{1,0:T(8,128)(2,1)S(1)}, u32[]{:S(2)}, u32[]{:S(2)}) collective-permute-start(bf16[528,128]{1,0:T(8,128)(2,1)S(1)} %merge.14), channel_id=1, source_target_pairs={{0,24},{1,25},{2,26},{3,27},{4,28},{5,29},{6,30},{7,31},{8,16},{9,... | collective-permute-start | bytes 405512 | tf_op jit(solution)/shard_map/ppermute | solution.py:367
  26.4 7.3 %collective-permute-start.10 = (bf16[528,128]{1,0:T(8,128)(2,1)S(1)}, bf16[528,128]{1,0:T(8,128)(2,1)S(1)}, u32[]{:S(2)}, u32[]{:S(2)}) collective-permute-start(bf16[528,128]{1,0:T(8,128)(2,1)S(1)} %merge.15), channel_id=1, source_target_pairs={{0,24},{1,25},{2,26},{3,27},{4,28},{5,29},{6,30},{7,31},{8,16},{9,... | collective-permute-start | bytes 405512 | tf_op jit(solution)/shard_map/ppermute | solution.py:367
  30.3 4.2 %collective-permute-start.12 = (bf16[256,512]{1,0:T(8,128)(2,1)S(1)}, bf16[256,512]{1,0:T(8,128)(2,1)S(1)}, u32[]{:S(2)}, u32[]{:S(2)}) collective-permute-start(bf16[256,512]{1,0:T(8,128)(2,1)S(1)} %last.4), channel_id=1, source_target_pairs={{0,1},{1,0},{2,3},{3,2},{4,5},{5,4},{6,7},{7,6},{8,9},{9,8},{10,11... | collective-permute-start | bytes 786440 | tf_op jit(solution)/shard_map/ppermute | solution.py:367
  33.9 1.6 %collective-permute-start.11 = (bf16[256,512]{1,0:T(8,128)(2,1)S(1)}, bf16[256,512]{1,0:T(8,128)(2,1)S(1)}, u32[]{:S(2)}, u32[]{:S(2)}) collective-permute-start(bf16[256,512]{1,0:T(8,128)(2,1)S(1)} %last.6), channel_id=1, source_target_pairs={{0,1},{1,0},{2,3},{3,2},{4,5},{5,4},{6,7},{7,6},{8,9},{9,8},{10,11... | collective-permute-start | bytes 786440 | tf_op jit(solution)/shard_map/ppermute | solution.py:367

commit v6 on v5

--- a/solution.py
+++ b/solution.py
@@ -306,22 +306,22 @@
     )
 
 
-def last_kernel(far, chunk, *refs):
+def last_kernel(far, chunk, duos, *refs):
     if far:
         queries, weights = far_tables(refs[0])
     else:
         queries, weights = refs[0][...], refs[1][...]
     total_ref, gap_ref, packet_ref, out_ref = refs[-4:]
     gap = jnp.exp(gap_ref[...])
-    for duo in range(PAIRS // 2):
+    for place, duo in enumerate(duos):
         lanes = slice(duo * 256, duo * 256 + 256)
         term = level_term(LEVELS - 1, chunk, duo, queries, packet_ref, weights, gap)
-        out_ref[:, lanes] = (total_ref[:, lanes] + term).astype(BF16)
-
-
-def add_last(far, chunk, *arrays):
-    return call(
-        functools.partial(last_kernel, far, chunk), [pltpu.VMEM((TOK, WIDTH), BF16)], arrays, "last",
+        out_ref[:, place * 256 : place * 256 + 256] = (total_ref[:, lanes] + term).astype(BF16)
+
+
+def add_last(far, chunk, *arrays, duos=tuple(range(PAIRS // 2))):
+    return call(
+        functools.partial(last_kernel, far, chunk, duos), [pltpu.VMEM((TOK, 256 * len(duos)), BF16)], arrays, "last",
         2 * TOK * STATE * WIDTH, kept=range(len(arrays)),
     )[0]
 
@@ -339,12 +339,13 @@
     if first:
         for chunk in range(CHUNKS):
             send(refs[chunk], core, chunk, 0, WIDTH)
-        rest_ref, part_ref, chunk = refs[CHUNKS], refs[CHUNKS + 1], 0
+        rest_ref, part_refs, chunk = refs[CHUNKS], [refs[CHUNKS + 1]], 0
     else:
-        rest_ref, part_ref, chunk = refs[0], refs[1], CHUNKS - 1
+        rest_ref, part_refs, chunk = refs[0], refs[1 : 1 + WIDTH // 256], CHUNKS - 1
     for piece in range(WIDTH // 256):
         lanes = slice(piece * 256, piece * 256 + 256)
-        buffer[piece] = (rest_ref[:, lanes] + part_ref[:, lanes].astype(F32)).astype(BF16)
+        part = part_refs[0][:, lanes] if first else part_refs[piece][...]
+        buffer[piece] = (rest_ref[:, lanes] + part.astype(F32)).astype(BF16)
         send(buffer.at[piece], 1 - core, chunk, piece * 256, 256)
     for copy in copies:
         copy.wait()
@@ -402,9 +403,8 @@
             packet[c], *state[c] = merge(level, c, *state[c], got[c])
         got[c] = swap(packet[c], masks[level + 1], devices // 2 if level == 3 and c in (0, 1) else None)
 
-    for c in chunks:
-        advance(0, c)
-    queries, mix, _ = after(queries, mix, packet[-1])
+    advance(0, 0)
+    queries, mix, _ = after(queries, mix, packet[0])
     scores, column, row, weights, tables = call(
         tables_kernel,
         [
@@ -412,7 +412,7 @@
         ],
         [decay, mix, keys, queries], "tables", 4 * TOK * TOK * STATE, 16384, kept=range(4),
     )
-    far = swap(tables, 1)
+    got[1], tables, scores = after(got[1], tables, scores)
     local = (scores, column, row)
     levels = [None] * CHUNKS
 
@@ -420,8 +420,12 @@
         arrays = [*levels[c], *(history[c][level] for level in wanted)]
         levels[c] = add_levels(wanted, c, queries, weights, far, *arrays)
 
-    for c in chunks:
-        levels[c] = [make_local(1, c, *local, x[c]), kept[c]]
+    advance(0, 1)
+    tables, _ = after(tables, packet[1])
+    far = swap(tables, 1)
+    first_0 = make_local(1, 0, *local, x[0])
+    first_1 = make_local(1, 1, *local, x[1])
+    levels = [[first_0, kept[0]], [first_1, kept[1]]]
     got[0], far, *levels = after(got[0], far, *levels)
     for c in chunks:
         advance(1, c)
@@ -446,15 +450,22 @@
     done, parts = [None] * CHUNKS, [None] * CHUNKS
     for c in chunks:
         total, far_total, gap, far_gap = levels[c]
-        part = add_last(True, c, far, far_total, far_gap, got[c])
-        parts[c] = swap(part, 1)
+        if c == 0:
+            part = add_last(True, c, far, far_total, far_gap, got[c])
+            parts[c] = swap(part, 1)
+        else:
+            parts[c], late = [], got[c]
+            for duo in range(PAIRS // 2):
+                part = add_last(True, c, far, far_total, far_gap, late, duos=(duo,))
+                parts[c].append(swap(part, 1))
+                late, _ = after(late, part)
         late, _ = after(got[c], part)
         done[c] = add_last(False, c, queries, weights, total, gap, late)
         if c == 0:
             got[1], done[0] = after(got[1], done[0])
     out = finish(True, [*done, rest[0], parts[0]])
     parts[1], out = after(parts[1], out)
-    return finish(False, [rest[1], parts[1]], out)
+    return finish(False, [rest[1], *parts[1]], out)
 
 
 def solution(mesh):

time: 37 us -> 37.2 us (level)
  starting transfers between devices: 17.5 us -> 16.9 us
  waiting for transfers between devices: 5.28 us -> 5.76 us
    ppermute x13 -> x14, starting transfers between devices: 17.5 us -> 16.9 us  [swap(): lax.ppermute(array, 'ctx', [(i, i ^ mask) for i in range(senders or devic...]
    ppermute x13 -> x14, waiting for transfers between devices: 5.28 us -> 5.76 us  [swap(): lax.ppermute(array, 'ctx', [(i, i ^ mask) for i in range(senders or devic...]
    pallas_call x28 -> x29, Pallas kernels: 13.3 us -> 13.4 us  [call(): pl.pallas_call(kernel, out_shape=outs, in_specs=[ANY if place in far else...]
  transfers between devices with their start and end apart: 13 -> 14, of which waited for: 5 -> 5; matrix products, arithmetic and copies ran while one was open for 0% -> 0% of each run, Pallas kernels for 30% -> 30%
where the time goes in v6:
time: 37.2 us; the launch traced here: 36.5 us
  starting transfers between devices  16.9 us (45%)
  Pallas kernels  13.4 us (36%)
  waiting for transfers between devices  5.76 us (15%)
  between operations  0.43 us (1%)
    ppermute x14, starting transfers between devices, swap(): lax.ppermute(array, 'ctx', [(i, i ^ mask) for i in range(senders or devic...  16.9 us
    pallas_call x29, Pallas kernels, call(): pl.pallas_call(kernel, out_shape=outs, in_specs=[ANY if place in far else...  13.4 us
    ppermute x14, waiting for transfers between devices, swap(): lax.ppermute(array, 'ctx', [(i, i ^ mask) for i in range(senders or devic...  5.76 us
  transfers between devices with their start and end apart: 14, of which 5 were waited for; matrix products, arithmetic and copies ran while one was open for 0% of the time, Pallas kernels for 30%

profile of v6, /device:TPU:1, one launch (start us, length us, event | category | flops | bytes accessed | tf_op | source)
XLA Modules:
  0.0 36.5 jit_solution(16138092052633519789)
XLA Ops:
  0.0 1.6 %fetch.1 = (bf16[528,128]{1,0:T(8,128)(2,1)S(1)}, f32[256,128]{1,0:T(8,128)S(1)}, f32[16,128]{1,0:T(8,128)S(1)}, f32[32,256]{1,0:T(8,128)S(1)}, bf16[256,128]{1,...) custom-call(f32[32,256]{1,0:T(8,128)} %refs_0_.1, ...), custom_call_target="tpu_custom_call" | custom-call | flops 3355443200 | bytes 1024 | tf_op jit(solution)/shard_map/fetch/pallas_call | solution.py:86
  1.6 3.3 %collective-permute-start = (bf16[528,128]{1,0:T(8,128)(2,1)S(1)}, bf16[528,128]{1,0:T(8,128)(2,1)S(1)}, u32[]{:S(2)}, u32[]{:S(2)}) collective-permute-start(bf16[528,128]{1,0:T(8,128)(2,1)S(1)} %get-tuple-element.132), channel_id=1, source_target_pairs={{0,1},{1,0},{2,3},{3,2},{4,5},{5,4},{6,7},{7,6},{8,9},{9,8},{10,11... | collective-permute-start | bytes 405512 | tf_op jit(solution)/shard_map/ppermute | solution.py:368
  5.0 0.5 %ends.3 = bf16[528,128]{1,0:T(8,128)(2,1)S(1)} custom-call(bf16[2,256,512]{2,1,0:T(8,128)(2,1)S(1)} %get-tuple-element.197.x_ref, bf16[256,128]{1,0:T(8,128)(2,1)S(1)} %get-tuple-element.128.key_ref, f32[256,128]{1,0:T(8,128)S(1)} %get-tuple-element.129.factor_ref, f32[16,128]{1,0:T(8,128)S(1)} %get-tuple-element.130.sum_ref), custom_call_target="tpu_custom_call" | custom-call | flops 3355443200 | bytes 1024 | tf_op jit(solution)/shard_map/ends/pallas_call | solution.py:86
  5.6 0.5 %ends.4.refs_0_.refs_4_ = bf16[528,128]{1,0:T(8,128)(2,1)S(1)} custom-call(bf16[2,256,512]{2,1,0:T(8,128)(2,1)S(1)} %get-tuple-element.170.x_ref, bf16[256,128]{1,0:T(8,128)(2,1)S(1)} %get-tuple-element.128.key_ref, f32[256,128]{1,0:T(8,128)S(1)} %get-tuple-element.129.factor_ref, f32[16,128]{1,0:T(8,128)S(1)} %get-tuple-element.130.sum_ref), custom_call_target="tpu_custom_call" | custom-call | flops 3355443200 | bytes 1024 | tf_op jit(solution)/shard_map/ends/pallas_call | solution.py:86
  6.3 0.4 %tables.1 = (f32[256,256]{1,0:T(8,128)S(1)}, f32[256,128]{1,0:T(8,128)S(1)}, f32[32,256]{1,0:T(8,128)S(1)}, f32[256,128]{1,0:T(8,128)S(1)}, bf16[256,384]{1,0:T(8,128)(2,1)S(1)}) custom-call(f32[32,256]{1,0:T(8,128)S(1)} %get-tuple-element.136.decay_ref, f32[6,32,256]{2,1,0:T(8,128)S(1)} %get-tuple-element.139.mix_ref, ...), custom_call_target="tpu_custom_call" | custom-call | flops 3355443200 | bytes 1024 | tf_op jit(solution)/shard_map/tables/pallas_call | solution.py:86
  6.9 0.5 %ends.5.refs_0_.refs_4_ = bf16[528,128]{1,0:T(8,128)(2,1)S(1)} custom-call(bf16[2,256,512]{2,1,0:T(8,128)(2,1)S(1)} %get-tuple-element.197.x_ref, bf16[256,128]{1,0:T(8,128)(2,1)S(1)} %get-tuple-element.128.key_ref, f32[256,128]{1,0:T(8,128)S(1)} %get-tuple-element.129.factor_ref, f32[16,128]{1,0:T(8,128)S(1)} %get-tuple-element.130.sum_ref), custom_call_target="tpu_custom_call" | custom-call | flops 3355443200 | bytes 1024 | tf_op jit(solution)/shard_map/ends/pallas_call | solution.py:86
  7.5 1.4 %collective-permute-start.5 = (bf16[528,128]{1,0:T(8,128)(2,1)S(1)}, bf16[528,128]{1,0:T(8,128)(2,1)S(1)}, u32[]{:S(2)}, u32[]{:S(2)}) collective-permute-start(bf16[528,128]{1,0:T(8,128)(2,1)S(1)} %get-tuple-element.147), channel_id=1, source_target_pairs={{0,2},{1,3},{2,0},{3,1},{4,6},{5,7},{6,4},{7,5},{8,10},{9,11},{10,... | collective-permute-start | bytes 405512 | tf_op jit(solution)/shard_map/ppermute | solution.py:368
  8.9 1.1 %collective-permute-start.3 = (bf16[256,384]{1,0:T(8,128)(2,1)S(1)}, bf16[256,384]{1,0:T(8,128)(2,1)S(1)}, u32[]{:S(2)}, u32[]{:S(2)}) collective-permute-start(bf16[256,384]{1,0:T(8,128)(2,1)S(1)} %get-tuple-element.148), channel_id=1, source_target_pairs={{0,1},{1,0},{2,3},{3,2},{4,5},{5,4},{6,7},{7,6},{8,9},{9,8},{10,11... | collective-permute-start | bytes 589832 | tf_op jit(solution)/shard_map/ppermute | solution.py:368
  10.0 0.6 %local.5.refs_3_ = f32[256,512]{1,0:T(8,128)S(1)} custom-call(f32[256,256]{1,0:T(8,128)S(1)} %get-tuple-element.149.scores_ref, f32[256,128]{1,0:T(8,128)S(1)} %get-tuple-element.150.column_ref, f32[32,256]{1,0:T(8,128)S(1)} %get-tuple-element.151.row_ref, bf16[2,256,512]{2,1,0:T(8,128)(2,1)S(1)} %get-tuple-element.197.x_ref), custom_call_target="tpu_custom_call" | custom-call | flops 13421772800 | bytes 1024 | tf_op jit(solution)/shard_map/local/pallas_call | solution.py:86
  10.6 0.6 %local.4.refs_3_ = f32[256,512]{1,0:T(8,128)S(1)} custom-call(f32[256,256]{1,0:T(8,128)S(1)} %get-tuple-element.149.scores_ref, f32[256,128]{1,0:T(8,128)S(1)} %get-tuple-element.150.column_ref, f32[32,256]{1,0:T(8,128)S(1)} %get-tuple-element.151.row_ref, bf16[2,256,512]{2,1,0:T(8,128)(2,1)S(1)} %get-tuple-element.170.x_ref), custom_call_target="tpu_custom_call" | custom-call | flops 13421772800 | bytes 1024 | tf_op jit(solution)/shard_map/local/pallas_call | solution.py:86
  11.4 0.8 %collective-permute-start.4 = (bf16[528,128]{1,0:T(8,128)(2,1)S(1)}, bf16[528,128]{1,0:T(8,128)(2,1)S(1)}, u32[]{:S(2)}, u32[]{:S(2)}) collective-permute-start(bf16[528,128]{1,0:T(8,128)(2,1)S(1)} %get-tuple-element.155), channel_id=1, source_target_pairs={{0,6},{1,7},{2,4},{3,5},{4,2},{5,3},{6,0},{7,1},{8,14},{9,15},{10,... | collective-permute-start | bytes 405512 | tf_op jit(solution)/shard_map/ppermute | solution.py:368
  12.2 1.6 %collective-permute-done.5.refs_2_.refs_6_ = bf16[528,128]{1,0:T(8,128)(2,1)S(1)} collective-permute-done((bf16[528,128]{1,0:T(8,128)(2,1)S(1)}, bf16[528,128]{1,0:T(8,128)(2,1)S(1)}, u32[]{:S(2)}, u32[]{:S(2)}) %collective-permute-start.5) | collective-permute-done | bytes 135200 | tf_op jit(solution)/shard_map/ppermute | solution.py:368
  14.0 0.8 %collective-permute-start.7 = (bf16[528,128]{1,0:T(8,128)(2,1)S(1)}, bf16[528,128]{1,0:T(8,128)(2,1)S(1)}, u32[]{:S(2)}, u32[]{:S(2)}) collective-permute-start(bf16[528,128]{1,0:T(8,128)(2,1)S(1)} %get-tuple-element.163), channel_id=1, source_target_pairs={{0,6},{1,7},{2,4},{3,5},{4,2},{5,3},{6,0},{7,1},{8,14},{9,15},{10,... | collective-permute-start | bytes 405512 | tf_op jit(solution)/shard_map/ppermute | solution.py:368
  14.8 0.6 %local.6.refs_2_ = f32[256,512]{1,0:T(8,128)S(1)} custom-call(f32[256,256]{1,0:T(8,128)S(1)} %get-tuple-element.149.scores_ref, f32[256,128]{1,0:T(8,128)S(1)} %get-tuple-element.150.column_ref, f32[32,256]{1,0:T(8,128)S(1)} %get-tuple-element.151.row_ref, bf16[2,256,512]{2,1,0:T(8,128)(2,1)S(1)} %get-tuple-element.170.x_ref), custom_call_target="tpu_custom_call" | custom-call | flops 13421772800 | bytes 1024 | tf_op jit(solution)/shard_map/local/pallas_call | solution.py:86
  15.4 0.8 %levels.5 = (f32[256,512]{1,0:T(8,128)S(1)}, f32[256,512]{1,0:T(8,128)S(1)}, f32[8,128]{1,0:T(8,128)S(1)}, f32[8,128]{1,0:T(8,128)S(1)}) custom-call(bf16[256,128]{1,0:T(8,128)(2,1)S(1)} %get-tuple-element.140.query_ref.refs_0_, f32[256,128]{1,0:T(8,128)S(1)} %get-tuple-element.156.refs_1_, bf16[256,384]{1,0:T(8,128)(2,1)S(1)} %collective-permute-done.3.refs_2_.refs_0_, ...), custom_call_target="tpu_custom_call" | custom-call | flops 13421772800 | bytes 1024 | tf_op jit(solution)/shard_map/levels/pallas_call | solution.py:86
  16.3 0.3 collective-permute-done.4.refs_2_.refs_7_
  16.7 1.1 %collective-permute-start.6 = (bf16[528,128]{1,0:T(8,128)(2,1)S(1)}, bf16[528,128]{1,0:T(8,128)(2,1)S(1)}, u32[]{:S(2)}, u32[]{:S(2)}) collective-permute-start(bf16[528,128]{1,0:T(8,128)(2,1)S(1)} %get-tuple-element.172), channel_id=1, source_target_pairs={{0,8},{1,9},{2,10},{3,11},{4,12},{5,13},{6,14},{7,15},{8,0},{9,1},... | collective-permute-start | bytes 405512 | tf_op jit(solution)/shard_map/ppermute | solution.py:368
  17.8 3.1 %collective-permute-done.7.refs_2_.refs_7_ = bf16[528,128]{1,0:T(8,128)(2,1)S(1)} collective-permute-done((bf16[528,128]{1,0:T(8,128)(2,1)S(1)}, bf16[528,128]{1,0:T(8,128)(2,1)S(1)}, u32[]{:S(2)}, u32[]{:S(2)}) %collective-permute-start.7) | collective-permute-done | bytes 135200 | tf_op jit(solution)/shard_map/ppermute | solution.py:368
  21.1 0.6 %local.7.refs_0_ = f32[256,512]{1,0:T(8,128)S(1)} custom-call(f32[256,256]{1,0:T(8,128)S(1)} %get-tuple-element.149.scores_ref, f32[256,128]{1,0:T(8,128)S(1)} %get-tuple-element.150.column_ref, f32[32,256]{1,0:T(8,128)S(1)} %get-tuple-element.151.row_ref, bf16[2,256,512]{2,1,0:T(8,128)(2,1)S(1)} %get-tuple-element.197.x_ref), custom_call_target="tpu_custom_call" | custom-call | flops 13421772800 | bytes 1024 | tf_op jit(solution)/shard_map/local/pallas_call | solution.py:86
  21.7 0.9 %levels.7 = (f32[256,512]{1,0:T(8,128)S(1)}, f32[256,512]{1,0:T(8,128)S(1)}, f32[8,128]{1,0:T(8,128)S(1)}, f32[8,128]{1,0:T(8,128)S(1)}) custom-call(bf16[256,128]{1,0:T(8,128)(2,1)S(1)} %get-tuple-element.140.query_ref.refs_0_, f32[256,128]{1,0:T(8,128)S(1)} %get-tuple-element.156.refs_1_, bf16[256,384]{1,0:T(8,128)(2,1)S(1)} %collective-permute-done.3.refs_2_.refs_0_, ...), custom_call_target="tpu_custom_call" | custom-call | flops 13421772800 | bytes 1024 | tf_op jit(solution)/shard_map/levels/pallas_call | solution.py:86
  22.6 0.5 %levels.6 = (f32[256,512]{1,0:T(8,128)S(1)}, f32[256,512]{1,0:T(8,128)S(1)}, f32[8,128]{1,0:T(8,128)S(1)}, f32[8,128]{1,0:T(8,128)S(1)}) custom-call(bf16[256,128]{1,0:T(8,128)(2,1)S(1)} %get-tuple-element.140.query_ref.refs_0_, f32[256,128]{1,0:T(8,128)S(1)} %get-tuple-element.156.refs_1_, bf16[256,384]{1,0:T(8,128)(2,1)S(1)} %collective-permute-done.3.refs_2_.refs_0_, ...), custom_call_target="tpu_custom_call" | custom-call | flops 6710886400 | bytes 1024 | tf_op jit(solution)/shard_map/levels/pallas_call | solution.py:86
  23.2 2.5 %collective-permute-start.8 = (bf16[528,128]{1,0:T(8,128)(2,1)S(1)}, bf16[528,128]{1,0:T(8,128)(2,1)S(1)}, u32[]{:S(2)}, u32[]{:S(2)}) collective-permute-start(bf16[528,128]{1,0:T(8,128)(2,1)S(1)} %merge.14), channel_id=1, source_target_pairs={{0,24},{1,25},{2,26},{3,27},{4,28},{5,29},{6,30},{7,31},{8,16},{9,... | collective-permute-start | bytes 405512 | tf_op jit(solution)/shard_map/ppermute | solution.py:368
  25.7 0.6 %collective-permute-done.9.refs_2_.refs_8_ = bf16[528,128]{1,0:T(8,128)(2,1)S(1)} collective-permute-done((bf16[528,128]{1,0:T(8,128)(2,1)S(1)}, bf16[528,128]{1,0:T(8,128)(2,1)S(1)}, u32[]{:S(2)}, u32[]{:S(2)}) %collective-permute-start.9) | collective-permute-done | bytes 135200 | tf_op jit(solution)/shard_map/ppermute | solution.py:368
  26.4 2.2 %collective-permute-start.10 = (bf16[528,128]{1,0:T(8,128)(2,1)S(1)}, bf16[528,128]{1,0:T(8,128)(2,1)S(1)}, u32[]{:S(2)}, u32[]{:S(2)}) collective-permute-start(bf16[528,128]{1,0:T(8,128)(2,1)S(1)} %merge.15), channel_id=1, source_target_pairs={{0,24},{1,25},{2,26},{3,27},{4,28},{5,29},{6,30},{7,31},{8,16},{9,... | collective-permute-start | bytes 405512 | tf_op jit(solution)/shard_map/ppermute | solution.py:368
  28.5 0.9 %levels.9 = (f32[256,512]{1,0:T(8,128)S(1)}, f32[256,512]{1,0:T(8,128)S(1)}, f32[8,128]{1,0:T(8,128)S(1)}, f32[8,128]{1,0:T(8,128)S(1)}) custom-call(bf16[256,128]{1,0:T(8,128)(2,1)S(1)} %get-tuple-element.140.query_ref.refs_0_, f32[256,128]{1,0:T(8,128)S(1)} %get-tuple-element.156.refs_1_, bf16[256,384]{1,0:T(8,128)(2,1)S(1)} %collective-permute-done.3.refs_2_.refs_0_, ...), custom_call_target="tpu_custom_call" | custom-call | flops 13421772800 | bytes 1024 | tf_op jit(solution)/shard_map/levels/pallas_call | solution.py:86
  29.4 0.5 %levels.8 = (f32[256,512]{1,0:T(8,128)S(1)}, f32[256,512]{1,0:T(8,128)S(1)}, f32[8,128]{1,0:T(8,128)S(1)}, f32[8,128]{1,0:T(8,128)S(1)}) custom-call(bf16[256,128]{1,0:T(8,128)(2,1)S(1)} %get-tuple-element.140.query_ref.refs_0_, f32[256,128]{1,0:T(8,128)S(1)} %get-tuple-element.156.refs_1_, bf16[256,384]{1,0:T(8,128)(2,1)S(1)} %collective-permute-done.3.refs_2_.refs_0_, ...), custom_call_target="tpu_custom_call" | custom-call | flops 6710886400 | bytes 1024 | tf_op jit(solution)/shard_map/levels/pallas_call | solution.py:86
  29.9 0.3 last.5
  30.2 2.9 %collective-permute-start.13 = (bf16[256,512]{1,0:T(8,128)(2,1)S(1)}, bf16[256,512]{1,0:T(8,128)(2,1)S(1)}, u32[]{:S(2)}, u32[]{:S(2)}) collective-permute-start(bf16[256,512]{1,0:T(8,128)(2,1)S(1)} %last.5), channel_id=1, source_target_pairs={{0,1},{1,0},{2,3},{3,2},{4,5},{5,4},{6,7},{7,6},{8,9},{9,8},{10,11... | collective-permute-start | bytes 786440 | tf_op jit(solution)/shard_map/ppermute | solution.py:368
  33.8 0.4 %collective-permute-start.12 = (bf16[256,256]{1,0:T(8,128)(2,1)S(1)}, bf16[256,256]{1,0:T(8,128)(2,1)S(1)}, u32[]{:S(2)}, u32[]{:S(2)}) collective-permute-start(bf16[256,256]{1,0:T(8,128)(2,1)S(1)} %last.8), channel_id=1, source_target_pairs={{0,1},{1,0},{2,3},{3,2},{4,5},{5,4},{6,7},{7,6},{8,9},{9,8},{10,11... | collective-permute-start | bytes 393224 | tf_op jit(solution)/shard_map/ppermute | solution.py:368
  34.4 0.3 last.9.refs_1_
  34.7 0.9 %finish.2.refs_3_ = bf16[256,2048]{1,0:T(8,128)(2,1)} custom-call(bf16[256,512]{1,0:T(8,128)(2,1)S(1)} %last.6.refs_0_, bf16[256,512]{1,0:T(8,128)(2,1)S(1)} %last.9.refs_1_, f32[256,512]{1,0:T(8,128)S(1)} %local.6.refs_2_, bf16[256,512]{1,0:T(8,128)(2,1)S(1)} %collective-permute-done.13.refs_3_), custom_call_target="tpu_custom_call" | custom-call | flops 13107200 | bytes 1024 | tf_op jit(solution)/shard_map/finish/pallas_call | solution.py:86
  35.6 0.8 %finish.3 = bf16[256,2048]{1,0:T(8,128)(2,1)} custom-call(f32[256,512]{1,0:T(8,128)S(1)} %local.7.refs_0_, bf16[256,256]{1,0:T(8,128)(2,1)S(1)} %collective-permute-done.11.refs_1_, bf16[256,256]{1,0:T(8,128)(2,1)S(1)} %collective-permute-done.12.refs_2_, bf16[256,2048]{1,0:T(8,128)(2,1)} %finish.2.refs_3_), custom_call_target="tpu_custom_call", output_to_operand_aliasing={{}: (3, {})} | custom-call | flops 13107200 | bytes 1024 | tf_op jit(solution)/shard_map/finish/pallas_call | solution.py:86
  (25 shorter events, 2.2 us)
Async XLA Ops:
  1.6 4.4 %collective-permute-start = (bf16[528,128]{1,0:T(8,128)(2,1)S(1)}, bf16[528,128]{1,0:T(8,128)(2,1)S(1)}, u32[]{:S(2)}, u32[]{:S(2)}) collective-permute-start(bf16[528,128]{1,0:T(8,128)(2,1)S(1)} %get-tuple-element.132), channel_id=1, source_target_pairs={{0,1},{1,0},{2,3},{3,2},{4,5},{5,4},{6,7},{7,6},{8,9},{9,8},{10,11... | collective-permute-start | bytes 405512 | tf_op jit(solution)/shard_map/ppermute | solution.py:368
  5.5 1.4 %collective-permute-start.2 = (bf16[528,128]{1,0:T(8,128)(2,1)S(1)}, bf16[528,128]{1,0:T(8,128)(2,1)S(1)}, u32[]{:S(2)}, u32[]{:S(2)}) collective-permute-start(bf16[528,128]{1,0:T(8,128)(2,1)S(1)} %ends.3), channel_id=1, source_target_pairs={{0,1},{1,0},{2,3},{3,2},{4,5},{5,4},{6,7},{7,6},{8,9},{9,8},{10,11... | collective-permute-start | bytes 405512 | tf_op jit(solution)/shard_map/ppermute | solution.py:368
  6.2 5.0 %collective-permute-start.1 = (bf16[528,128]{1,0:T(8,128)(2,1)S(1)}, bf16[528,128]{1,0:T(8,128)(2,1)S(1)}, u32[]{:S(2)}, u32[]{:S(2)}) collective-permute-start(bf16[528,128]{1,0:T(8,128)(2,1)S(1)} %get-tuple-element.135), channel_id=1, source_target_pairs={{0,2},{1,3},{2,0},{3,1},{4,6},{5,7},{6,4},{7,5},{8,10},{9,11},{10,... | collective-permute-start | bytes 405512 | tf_op jit(solution)/shard_map/ppermute | solution.py:368
  7.5 6.3 %collective-permute-start.5 = (bf16[528,128]{1,0:T(8,128)(2,1)S(1)}, bf16[528,128]{1,0:T(8,128)(2,1)S(1)}, u32[]{:S(2)}, u32[]{:S(2)}) collective-permute-start(bf16[528,128]{1,0:T(8,128)(2,1)S(1)} %get-tuple-element.147), channel_id=1, source_target_pairs={{0,2},{1,3},{2,0},{3,1},{4,6},{5,7},{6,4},{7,5},{8,10},{9,11},{10,... | collective-permute-start | bytes 405512 | tf_op jit(solution)/shard_map/ppermute | solution.py:368
  8.9 2.3 %collective-permute-start.3 = (bf16[256,384]{1,0:T(8,128)(2,1)S(1)}, bf16[256,384]{1,0:T(8,128)(2,1)S(1)}, u32[]{:S(2)}, u32[]{:S(2)}) collective-permute-start(bf16[256,384]{1,0:T(8,128)(2,1)S(1)} %get-tuple-element.148), channel_id=1, source_target_pairs={{0,1},{1,0},{2,3},{3,2},{4,5},{5,4},{6,7},{7,6},{8,9},{9,8},{10,11... | collective-permute-start | bytes 589832 | tf_op jit(solution)/shard_map/ppermute | solution.py:368
  11.4 5.2 %collective-permute-start.4 = (bf16[528,128]{1,0:T(8,128)(2,1)S(1)}, bf16[528,128]{1,0:T(8,128)(2,1)S(1)}, u32[]{:S(2)}, u32[]{:S(2)}) collective-permute-start(bf16[528,128]{1,0:T(8,128)(2,1)S(1)} %get-tuple-element.155), channel_id=1, source_target_pairs={{0,6},{1,7},{2,4},{3,5},{4,2},{5,3},{6,0},{7,1},{8,14},{9,15},{10,... | collective-permute-start | bytes 405512 | tf_op jit(solution)/shard_map/ppermute | solution.py:368
  14.0 6.9 %collective-permute-start.7 = (bf16[528,128]{1,0:T(8,128)(2,1)S(1)}, bf16[528,128]{1,0:T(8,128)(2,1)S(1)}, u32[]{:S(2)}, u32[]{:S(2)}) collective-permute-start(bf16[528,128]{1,0:T(8,128)(2,1)S(1)} %get-tuple-element.163), channel_id=1, source_target_pairs={{0,6},{1,7},{2,4},{3,5},{4,2},{5,3},{6,0},{7,1},{8,14},{9,15},{10,... | collective-permute-start | bytes 405512 | tf_op jit(solution)/shard_map/ppermute | solution.py:368
  16.7 6.4 %collective-permute-start.6 = (bf16[528,128]{1,0:T(8,128)(2,1)S(1)}, bf16[528,128]{1,0:T(8,128)(2,1)S(1)}, u32[]{:S(2)}, u32[]{:S(2)}) collective-permute-start(bf16[528,128]{1,0:T(8,128)(2,1)S(1)} %get-tuple-element.172), channel_id=1, source_target_pairs={{0,8},{1,9},{2,10},{3,11},{4,12},{5,13},{6,14},{7,15},{8,0},{9,1},... | collective-permute-start | bytes 405512 | tf_op jit(solution)/shard_map/ppermute | solution.py:368
  21.0 5.2 %collective-permute-start.9 = (bf16[528,128]{1,0:T(8,128)(2,1)S(1)}, bf16[528,128]{1,0:T(8,128)(2,1)S(1)}, u32[]{:S(2)}, u32[]{:S(2)}) collective-permute-start(bf16[528,128]{1,0:T(8,128)(2,1)S(1)} %get-tuple-element.182), channel_id=1, source_target_pairs={{0,8},{1,9},{2,10},{3,11},{4,12},{5,13},{6,14},{7,15},{8,0},{9,1},... | collective-permute-start | bytes 405512 | tf_op jit(solution)/shard_map/ppermute | solution.py:368
  23.2 6.7 %collective-permute-start.8 = (bf16[528,128]{1,0:T(8,128)(2,1)S(1)}, bf16[528,128]{1,0:T(8,128)(2,1)S(1)}, u32[]{:S(2)}, u32[]{:S(2)}) collective-permute-start(bf16[528,128]{1,0:T(8,128)(2,1)S(1)} %merge.14), channel_id=1, source_target_pairs={{0,24},{1,25},{2,26},{3,27},{4,28},{5,29},{6,30},{7,31},{8,16},{9,... | collective-permute-start | bytes 405512 | tf_op jit(solution)/shard_map/ppermute | solution.py:368
  26.4 7.0 %collective-permute-start.10 = (bf16[528,128]{1,0:T(8,128)(2,1)S(1)}, bf16[528,128]{1,0:T(8,128)(2,1)S(1)}, u32[]{:S(2)}, u32[]{:S(2)}) collective-permute-start(bf16[528,128]{1,0:T(8,128)(2,1)S(1)} %merge.15), channel_id=1, source_target_pairs={{0,24},{1,25},{2,26},{3,27},{4,28},{5,29},{6,30},{7,31},{8,16},{9,... | collective-permute-start | bytes 405512 | tf_op jit(solution)/shard_map/ppermute | solution.py:368
  30.2 4.4 %collective-permute-start.13 = (bf16[256,512]{1,0:T(8,128)(2,1)S(1)}, bf16[256,512]{1,0:T(8,128)(2,1)S(1)}, u32[]{:S(2)}, u32[]{:S(2)}) collective-permute-start(bf16[256,512]{1,0:T(8,128)(2,1)S(1)} %last.5), channel_id=1, source_target_pairs={{0,1},{1,0},{2,3},{3,2},{4,5},{5,4},{6,7},{7,6},{8,9},{9,8},{10,11... | collective-permute-start | bytes 786440 | tf_op jit(solution)/shard_map/ppermute | solution.py:368
  33.8 1.8 %collective-permute-start.12 = (bf16[256,256]{1,0:T(8,128)(2,1)S(1)}, bf16[256,256]{1,0:T(8,128)(2,1)S(1)}, u32[]{:S(2)}, u32[]{:S(2)}) collective-permute-start(bf16[256,256]{1,0:T(8,128)(2,1)S(1)} %last.8), channel_id=1, source_target_pairs={{0,1},{1,0},{2,3},{3,2},{4,5},{5,4},{6,7},{7,6},{8,9},{9,8},{10,11... | collective-permute-start | bytes 393224 | tf_op jit(solution)/shard_map/ppermute | solution.py:368
  34.2 1.4 %collective-permute-start.11 = (bf16[256,256]{1,0:T(8,128)(2,1)S(1)}, bf16[256,256]{1,0:T(8,128)(2,1)S(1)}, u32[]{:S(2)}, u32[]{:S(2)}) collective-permute-start(bf16[256,256]{1,0:T(8,128)(2,1)S(1)} %last.7), channel_id=1, source_target_pairs={{0,1},{1,0},{2,3},{3,2},{4,5},{5,4},{6,7},{7,6},{8,9},{9,8},{10,11... | collective-permute-start | bytes 393224 | tf_op jit(solution)/shard_map/ppermute | solution.py:368

commit v7 on v5

--- a/solution.py
+++ b/solution.py
@@ -132,7 +132,7 @@
     copies[0].wait()
     decay = pad_heads(targets[0][...])
     factor = jnp.exp(exact_dot(later, decay, ((1,), (1,))))
-    sums = exact_dot(jnp.ones((16, TOK), BF16), decay, ((1,), (1,)), 3)
+    sums = exact_dot(jnp.ones((16, TOK), BF16), decay, ((1,), (1,)))
     factor_ref[...] = factor
     sum_ref[...] = sums
     copies[1].wait()

time: 37 us -> 37 us (level)
  no operation moved by 1% of the time
where the time goes in v7:
time: 37 us; the launch traced here: 36.5 us
  starting transfers between devices  17.5 us (47%)
  Pallas kernels  13.3 us (36%)
  waiting for transfers between devices  5.25 us (14%)
  between operations  0.41 us (1%)
    ppermute x13, starting transfers between devices, swap(): lax.ppermute(array, 'ctx', [(i, i ^ mask) for i in range(senders or devic...  17.5 us
    pallas_call x28, Pallas kernels, call(): pl.pallas_call(kernel, out_shape=outs, in_specs=[ANY if place in far else...  13.3 us
    ppermute x13, waiting for transfers between devices, swap(): lax.ppermute(array, 'ctx', [(i, i ^ mask) for i in range(senders or devic...  5.25 us
  transfers between devices with their start and end apart: 13, of which 5 were waited for; matrix products, arithmetic and copies ran while one was open for 0% of the time, Pallas kernels for 30%

profile of v7, /device:TPU:1, one launch (start us, length us, event | category | flops | bytes accessed | tf_op | source)
XLA Modules:
  0.0 36.5 jit_solution(7505588605962541669)
XLA Ops:
  0.0 1.6 %fetch.1 = (bf16[528,128]{1,0:T(8,128)(2,1)S(1)}, f32[256,128]{1,0:T(8,128)S(1)}, f32[16,128]{1,0:T(8,128)S(1)}, f32[32,256]{1,0:T(8,128)S(1)}, bf16[256,128]{1,...) custom-call(f32[32,256]{1,0:T(8,128)} %refs_0_.1, ...), custom_call_target="tpu_custom_call" | custom-call | flops 3355443200 | bytes 1024 | tf_op jit(solution)/shard_map/fetch/pallas_call | solution.py:86
  1.6 3.3 %collective-permute-start = (bf16[528,128]{1,0:T(8,128)(2,1)S(1)}, bf16[528,128]{1,0:T(8,128)(2,1)S(1)}, u32[]{:S(2)}, u32[]{:S(2)}) collective-permute-start(bf16[528,128]{1,0:T(8,128)(2,1)S(1)} %get-tuple-element.126), channel_id=1, source_target_pairs={{0,1},{1,0},{2,3},{3,2},{4,5},{5,4},{6,7},{7,6},{8,9},{9,8},{10,11... | collective-permute-start | bytes 405512 | tf_op jit(solution)/shard_map/ppermute | solution.py:367
  5.0 0.5 %ends.3 = bf16[528,128]{1,0:T(8,128)(2,1)S(1)} custom-call(bf16[2,256,512]{2,1,0:T(8,128)(2,1)S(1)} %get-tuple-element.187.x_ref, bf16[256,128]{1,0:T(8,128)(2,1)S(1)} %get-tuple-element.122.key_ref, f32[256,128]{1,0:T(8,128)S(1)} %get-tuple-element.123.factor_ref, f32[16,128]{1,0:T(8,128)S(1)} %get-tuple-element.124.sum_ref), custom_call_target="tpu_custom_call" | custom-call | flops 3355443200 | bytes 1024 | tf_op jit(solution)/shard_map/ends/pallas_call | solution.py:86
  5.6 0.5 %ends.4.refs_0_.refs_4_ = bf16[528,128]{1,0:T(8,128)(2,1)S(1)} custom-call(bf16[2,256,512]{2,1,0:T(8,128)(2,1)S(1)} %get-tuple-element.160.x_ref, bf16[256,128]{1,0:T(8,128)(2,1)S(1)} %get-tuple-element.122.key_ref, f32[256,128]{1,0:T(8,128)S(1)} %get-tuple-element.123.factor_ref, f32[16,128]{1,0:T(8,128)S(1)} %get-tuple-element.124.sum_ref), custom_call_target="tpu_custom_call" | custom-call | flops 3355443200 | bytes 1024 | tf_op jit(solution)/shard_map/ends/pallas_call | solution.py:86
  6.3 0.5 %ends.5.refs_0_.refs_4_ = bf16[528,128]{1,0:T(8,128)(2,1)S(1)} custom-call(bf16[2,256,512]{2,1,0:T(8,128)(2,1)S(1)} %get-tuple-element.187.x_ref, bf16[256,128]{1,0:T(8,128)(2,1)S(1)} %get-tuple-element.122.key_ref, f32[256,128]{1,0:T(8,128)S(1)} %get-tuple-element.123.factor_ref, f32[16,128]{1,0:T(8,128)S(1)} %get-tuple-element.124.sum_ref), custom_call_target="tpu_custom_call" | custom-call | flops 3355443200 | bytes 1024 | tf_op jit(solution)/shard_map/ends/pallas_call | solution.py:86
  7.0 1.5 %collective-permute-start.5 = (bf16[528,128]{1,0:T(8,128)(2,1)S(1)}, bf16[528,128]{1,0:T(8,128)(2,1)S(1)}, u32[]{:S(2)}, u32[]{:S(2)}) collective-permute-start(bf16[528,128]{1,0:T(8,128)(2,1)S(1)} %get-tuple-element.135), channel_id=1, source_target_pairs={{0,2},{1,3},{2,0},{3,1},{4,6},{5,7},{6,4},{7,5},{8,10},{9,11},{10,... | collective-permute-start | bytes 405512 | tf_op jit(solution)/shard_map/ppermute | solution.py:367
  8.5 0.4 %tables.1 = (f32[256,256]{1,0:T(8,128)S(1)}, f32[256,128]{1,0:T(8,128)S(1)}, f32[32,256]{1,0:T(8,128)S(1)}, f32[256,128]{1,0:T(8,128)S(1)}, bf16[256,384]{1,0:T(8,128)(2,1)S(1)}) custom-call(f32[32,256]{1,0:T(8,128)S(1)} %get-tuple-element.130.decay_ref, f32[6,32,256]{2,1,0:T(8,128)S(1)} %get-tuple-element.136.mix_ref, ...), custom_call_target="tpu_custom_call" | custom-call | flops 3355443200 | bytes 1024 | tf_op jit(solution)/shard_map/tables/pallas_call | solution.py:86
  8.9 1.1 %collective-permute-start.3 = (bf16[256,384]{1,0:T(8,128)(2,1)S(1)}, bf16[256,384]{1,0:T(8,128)(2,1)S(1)}, u32[]{:S(2)}, u32[]{:S(2)}) collective-permute-start(bf16[256,384]{1,0:T(8,128)(2,1)S(1)} %get-tuple-element.138), channel_id=1, source_target_pairs={{0,1},{1,0},{2,3},{3,2},{4,5},{5,4},{6,7},{7,6},{8,9},{9,8},{10,11... | collective-permute-start | bytes 589832 | tf_op jit(solution)/shard_map/ppermute | solution.py:367
  10.1 0.6 %local.5.refs_3_ = f32[256,512]{1,0:T(8,128)S(1)} custom-call(f32[256,256]{1,0:T(8,128)S(1)} %get-tuple-element.139.scores_ref, f32[256,128]{1,0:T(8,128)S(1)} %get-tuple-element.140.column_ref, f32[32,256]{1,0:T(8,128)S(1)} %get-tuple-element.141.row_ref, bf16[2,256,512]{2,1,0:T(8,128)(2,1)S(1)} %get-tuple-element.187.x_ref), custom_call_target="tpu_custom_call" | custom-call | flops 13421772800 | bytes 1024 | tf_op jit(solution)/shard_map/local/pallas_call | solution.py:86
  10.7 0.6 %local.4.refs_3_ = f32[256,512]{1,0:T(8,128)S(1)} custom-call(f32[256,256]{1,0:T(8,128)S(1)} %get-tuple-element.139.scores_ref, f32[256,128]{1,0:T(8,128)S(1)} %get-tuple-element.140.column_ref, f32[32,256]{1,0:T(8,128)S(1)} %get-tuple-element.141.row_ref, bf16[2,256,512]{2,1,0:T(8,128)(2,1)S(1)} %get-tuple-element.160.x_ref), custom_call_target="tpu_custom_call" | custom-call | flops 13421772800 | bytes 1024 | tf_op jit(solution)/shard_map/local/pallas_call | solution.py:86
  11.5 0.8 %collective-permute-start.4 = (bf16[528,128]{1,0:T(8,128)(2,1)S(1)}, bf16[528,128]{1,0:T(8,128)(2,1)S(1)}, u32[]{:S(2)}, u32[]{:S(2)}) collective-permute-start(bf16[528,128]{1,0:T(8,128)(2,1)S(1)} %get-tuple-element.145), channel_id=1, source_target_pairs={{0,6},{1,7},{2,4},{3,5},{4,2},{5,3},{6,0},{7,1},{8,14},{9,15},{10,... | collective-permute-start | bytes 405512 | tf_op jit(solution)/shard_map/ppermute | solution.py:367
  12.3 1.6 %collective-permute-done.5.refs_2_.refs_6_ = bf16[528,128]{1,0:T(8,128)(2,1)S(1)} collective-permute-done((bf16[528,128]{1,0:T(8,128)(2,1)S(1)}, bf16[528,128]{1,0:T(8,128)(2,1)S(1)}, u32[]{:S(2)}, u32[]{:S(2)}) %collective-permute-start.5) | collective-permute-done | bytes 135200 | tf_op jit(solution)/shard_map/ppermute | solution.py:367
  14.0 0.8 %collective-permute-start.7 = (bf16[528,128]{1,0:T(8,128)(2,1)S(1)}, bf16[528,128]{1,0:T(8,128)(2,1)S(1)}, u32[]{:S(2)}, u32[]{:S(2)}) collective-permute-start(bf16[528,128]{1,0:T(8,128)(2,1)S(1)} %get-tuple-element.153), channel_id=1, source_target_pairs={{0,6},{1,7},{2,4},{3,5},{4,2},{5,3},{6,0},{7,1},{8,14},{9,15},{10,... | collective-permute-start | bytes 405512 | tf_op jit(solution)/shard_map/ppermute | solution.py:367
  14.8 0.6 %local.6.refs_2_ = f32[256,512]{1,0:T(8,128)S(1)} custom-call(f32[256,256]{1,0:T(8,128)S(1)} %get-tuple-element.139.scores_ref, f32[256,128]{1,0:T(8,128)S(1)} %get-tuple-element.140.column_ref, f32[32,256]{1,0:T(8,128)S(1)} %get-tuple-element.141.row_ref, bf16[2,256,512]{2,1,0:T(8,128)(2,1)S(1)} %get-tuple-element.160.x_ref), custom_call_target="tpu_custom_call" | custom-call | flops 13421772800 | bytes 1024 | tf_op jit(solution)/shard_map/local/pallas_call | solution.py:86
  15.4 0.8 %levels.5 = (f32[256,512]{1,0:T(8,128)S(1)}, f32[256,512]{1,0:T(8,128)S(1)}, f32[8,128]{1,0:T(8,128)S(1)}, f32[8,128]{1,0:T(8,128)S(1)}) custom-call(bf16[256,128]{1,0:T(8,128)(2,1)S(1)} %get-tuple-element.137.query_ref.refs_0_, f32[256,128]{1,0:T(8,128)S(1)} %get-tuple-element.146.refs_1_, bf16[256,384]{1,0:T(8,128)(2,1)S(1)} %collective-permute-done.3.refs_2_.refs_0_, ...), custom_call_target="tpu_custom_call" | custom-call | flops 13421772800 | bytes 1024 | tf_op jit(solution)/shard_map/levels/pallas_call | solution.py:86
  16.3 0.4 collective-permute-done.4.refs_2_.refs_7_
  16.7 1.0 %collective-permute-start.6 = (bf16[528,128]{1,0:T(8,128)(2,1)S(1)}, bf16[528,128]{1,0:T(8,128)(2,1)S(1)}, u32[]{:S(2)}, u32[]{:S(2)}) collective-permute-start(bf16[528,128]{1,0:T(8,128)(2,1)S(1)} %get-tuple-element.162), channel_id=1, source_target_pairs={{0,8},{1,9},{2,10},{3,11},{4,12},{5,13},{6,14},{7,15},{8,0},{9,1},... | collective-permute-start | bytes 405512 | tf_op jit(solution)/shard_map/ppermute | solution.py:367
  17.8 3.1 %collective-permute-done.7.refs_2_.refs_7_ = bf16[528,128]{1,0:T(8,128)(2,1)S(1)} collective-permute-done((bf16[528,128]{1,0:T(8,128)(2,1)S(1)}, bf16[528,128]{1,0:T(8,128)(2,1)S(1)}, u32[]{:S(2)}, u32[]{:S(2)}) %collective-permute-start.7) | collective-permute-done | bytes 135200 | tf_op jit(solution)/shard_map/ppermute | solution.py:367
  21.1 0.6 %local.7.refs_0_ = f32[256,512]{1,0:T(8,128)S(1)} custom-call(f32[256,256]{1,0:T(8,128)S(1)} %get-tuple-element.139.scores_ref, f32[256,128]{1,0:T(8,128)S(1)} %get-tuple-element.140.column_ref, f32[32,256]{1,0:T(8,128)S(1)} %get-tuple-element.141.row_ref, bf16[2,256,512]{2,1,0:T(8,128)(2,1)S(1)} %get-tuple-element.187.x_ref), custom_call_target="tpu_custom_call" | custom-call | flops 13421772800 | bytes 1024 | tf_op jit(solution)/shard_map/local/pallas_call | solution.py:86
  21.7 0.9 %levels.7 = (f32[256,512]{1,0:T(8,128)S(1)}, f32[256,512]{1,0:T(8,128)S(1)}, f32[8,128]{1,0:T(8,128)S(1)}, f32[8,128]{1,0:T(8,128)S(1)}) custom-call(bf16[256,128]{1,0:T(8,128)(2,1)S(1)} %get-tuple-element.137.query_ref.refs_0_, f32[256,128]{1,0:T(8,128)S(1)} %get-tuple-element.146.refs_1_, bf16[256,384]{1,0:T(8,128)(2,1)S(1)} %collective-permute-done.3.refs_2_.refs_0_, ...), custom_call_target="tpu_custom_call" | custom-call | flops 13421772800 | bytes 1024 | tf_op jit(solution)/shard_map/levels/pallas_call | solution.py:86
  22.6 0.5 %levels.6 = (f32[256,512]{1,0:T(8,128)S(1)}, f32[256,512]{1,0:T(8,128)S(1)}, f32[8,128]{1,0:T(8,128)S(1)}, f32[8,128]{1,0:T(8,128)S(1)}) custom-call(bf16[256,128]{1,0:T(8,128)(2,1)S(1)} %get-tuple-element.137.query_ref.refs_0_, f32[256,128]{1,0:T(8,128)S(1)} %get-tuple-element.146.refs_1_, bf16[256,384]{1,0:T(8,128)(2,1)S(1)} %collective-permute-done.3.refs_2_.refs_0_, ...), custom_call_target="tpu_custom_call" | custom-call | flops 6710886400 | bytes 1024 | tf_op jit(solution)/shard_map/levels/pallas_call | solution.py:86
  23.2 2.9 %collective-permute-start.8 = (bf16[528,128]{1,0:T(8,128)(2,1)S(1)}, bf16[528,128]{1,0:T(8,128)(2,1)S(1)}, u32[]{:S(2)}, u32[]{:S(2)}) collective-permute-start(bf16[528,128]{1,0:T(8,128)(2,1)S(1)} %merge.14), channel_id=1, source_target_pairs={{0,24},{1,25},{2,26},{3,27},{4,28},{5,29},{6,30},{7,31},{8,16},{9,... | collective-permute-start | bytes 405512 | tf_op jit(solution)/shard_map/ppermute | solution.py:367
  26.4 2.3 %collective-permute-start.10 = (bf16[528,128]{1,0:T(8,128)(2,1)S(1)}, bf16[528,128]{1,0:T(8,128)(2,1)S(1)}, u32[]{:S(2)}, u32[]{:S(2)}) collective-permute-start(bf16[528,128]{1,0:T(8,128)(2,1)S(1)} %merge.15), channel_id=1, source_target_pairs={{0,24},{1,25},{2,26},{3,27},{4,28},{5,29},{6,30},{7,31},{8,16},{9,... | collective-permute-start | bytes 405512 | tf_op jit(solution)/shard_map/ppermute | solution.py:367
  28.7 0.9 %levels.9 = (f32[256,512]{1,0:T(8,128)S(1)}, f32[256,512]{1,0:T(8,128)S(1)}, f32[8,128]{1,0:T(8,128)S(1)}, f32[8,128]{1,0:T(8,128)S(1)}) custom-call(bf16[256,128]{1,0:T(8,128)(2,1)S(1)} %get-tuple-element.137.query_ref.refs_0_, f32[256,128]{1,0:T(8,128)S(1)} %get-tuple-element.146.refs_1_, bf16[256,384]{1,0:T(8,128)(2,1)S(1)} %collective-permute-done.3.refs_2_.refs_0_, ...), custom_call_target="tpu_custom_call" | custom-call | flops 13421772800 | bytes 1024 | tf_op jit(solution)/shard_map/levels/pallas_call | solution.py:86
  29.5 0.5 %levels.8 = (f32[256,512]{1,0:T(8,128)S(1)}, f32[256,512]{1,0:T(8,128)S(1)}, f32[8,128]{1,0:T(8,128)S(1)}, f32[8,128]{1,0:T(8,128)S(1)}) custom-call(bf16[256,128]{1,0:T(8,128)(2,1)S(1)} %get-tuple-element.137.query_ref.refs_0_, f32[256,128]{1,0:T(8,128)S(1)} %get-tuple-element.146.refs_1_, bf16[256,384]{1,0:T(8,128)(2,1)S(1)} %collective-permute-done.3.refs_2_.refs_0_, ...), custom_call_target="tpu_custom_call" | custom-call | flops 6710886400 | bytes 1024 | tf_op jit(solution)/shard_map/levels/pallas_call | solution.py:86
  30.1 0.3 last.4
  30.3 3.0 %collective-permute-start.12 = (bf16[256,512]{1,0:T(8,128)(2,1)S(1)}, bf16[256,512]{1,0:T(8,128)(2,1)S(1)}, u32[]{:S(2)}, u32[]{:S(2)}) collective-permute-start(bf16[256,512]{1,0:T(8,128)(2,1)S(1)} %last.4), channel_id=1, source_target_pairs={{0,1},{1,0},{2,3},{3,2},{4,5},{5,4},{6,7},{7,6},{8,9},{9,8},{10,11... | collective-permute-start | bytes 786440 | tf_op jit(solution)/shard_map/ppermute | solution.py:367
  33.6 0.3 last.6
  33.9 0.4 %collective-permute-start.11 = (bf16[256,512]{1,0:T(8,128)(2,1)S(1)}, bf16[256,512]{1,0:T(8,128)(2,1)S(1)}, u32[]{:S(2)}, u32[]{:S(2)}) collective-permute-start(bf16[256,512]{1,0:T(8,128)(2,1)S(1)} %last.6), channel_id=1, source_target_pairs={{0,1},{1,0},{2,3},{3,2},{4,5},{5,4},{6,7},{7,6},{8,9},{9,8},{10,11... | collective-permute-start | bytes 786440 | tf_op jit(solution)/shard_map/ppermute | solution.py:367
  34.3 0.3 last.7.refs_1_
  34.6 0.9 %finish.2.refs_2_ = bf16[256,2048]{1,0:T(8,128)(2,1)} custom-call(bf16[256,512]{1,0:T(8,128)(2,1)S(1)} %last.5.refs_0_, bf16[256,512]{1,0:T(8,128)(2,1)S(1)} %last.7.refs_1_, f32[256,512]{1,0:T(8,128)S(1)} %local.6.refs_2_, bf16[256,512]{1,0:T(8,128)(2,1)S(1)} %collective-permute-done.12.refs_3_), custom_call_target="tpu_custom_call" | custom-call | flops 13107200 | bytes 1024 | tf_op jit(solution)/shard_map/finish/pallas_call | solution.py:86
  35.5 0.8 %finish.3 = bf16[256,2048]{1,0:T(8,128)(2,1)} custom-call(f32[256,512]{1,0:T(8,128)S(1)} %local.7.refs_0_, bf16[256,512]{1,0:T(8,128)(2,1)S(1)} %collective-permute-done.11.refs_1_, bf16[256,2048]{1,0:T(8,128)(2,1)} %finish.2.refs_2_), custom_call_target="tpu_custom_call", output_to_operand_aliasing={{}: (2, {})} | custom-call | flops 13107200 | bytes 1024 | tf_op jit(solution)/shard_map/finish/pallas_call | solution.py:86
  (22 shorter events, 1.7 us)
Async XLA Ops:
  1.6 4.4 %collective-permute-start = (bf16[528,128]{1,0:T(8,128)(2,1)S(1)}, bf16[528,128]{1,0:T(8,128)(2,1)S(1)}, u32[]{:S(2)}, u32[]{:S(2)}) collective-permute-start(bf16[528,128]{1,0:T(8,128)(2,1)S(1)} %get-tuple-element.126), channel_id=1, source_target_pairs={{0,1},{1,0},{2,3},{3,2},{4,5},{5,4},{6,7},{7,6},{8,9},{9,8},{10,11... | collective-permute-start | bytes 405512 | tf_op jit(solution)/shard_map/ppermute | solution.py:367
  5.5 1.4 %collective-permute-start.2 = (bf16[528,128]{1,0:T(8,128)(2,1)S(1)}, bf16[528,128]{1,0:T(8,128)(2,1)S(1)}, u32[]{:S(2)}, u32[]{:S(2)}) collective-permute-start(bf16[528,128]{1,0:T(8,128)(2,1)S(1)} %ends.3), channel_id=1, source_target_pairs={{0,1},{1,0},{2,3},{3,2},{4,5},{5,4},{6,7},{7,6},{8,9},{9,8},{10,11... | collective-permute-start | bytes 405512 | tf_op jit(solution)/shard_map/ppermute | solution.py:367
  6.2 5.1 %collective-permute-start.1 = (bf16[528,128]{1,0:T(8,128)(2,1)S(1)}, bf16[528,128]{1,0:T(8,128)(2,1)S(1)}, u32[]{:S(2)}, u32[]{:S(2)}) collective-permute-start(bf16[528,128]{1,0:T(8,128)(2,1)S(1)} %get-tuple-element.129), channel_id=1, source_target_pairs={{0,2},{1,3},{2,0},{3,1},{4,6},{5,7},{6,4},{7,5},{8,10},{9,11},{10,... | collective-permute-start | bytes 405512 | tf_op jit(solution)/shard_map/ppermute | solution.py:367
  7.0 6.8 %collective-permute-start.5 = (bf16[528,128]{1,0:T(8,128)(2,1)S(1)}, bf16[528,128]{1,0:T(8,128)(2,1)S(1)}, u32[]{:S(2)}, u32[]{:S(2)}) collective-permute-start(bf16[528,128]{1,0:T(8,128)(2,1)S(1)} %get-tuple-element.135), channel_id=1, source_target_pairs={{0,2},{1,3},{2,0},{3,1},{4,6},{5,7},{6,4},{7,5},{8,10},{9,11},{10,... | collective-permute-start | bytes 405512 | tf_op jit(solution)/shard_map/ppermute | solution.py:367
  8.9 2.4 %collective-permute-start.3 = (bf16[256,384]{1,0:T(8,128)(2,1)S(1)}, bf16[256,384]{1,0:T(8,128)(2,1)S(1)}, u32[]{:S(2)}, u32[]{:S(2)}) collective-permute-start(bf16[256,384]{1,0:T(8,128)(2,1)S(1)} %get-tuple-element.138), channel_id=1, source_target_pairs={{0,1},{1,0},{2,3},{3,2},{4,5},{5,4},{6,7},{7,6},{8,9},{9,8},{10,11... | collective-permute-start | bytes 589832 | tf_op jit(solution)/shard_map/ppermute | solution.py:367
  11.5 5.2 %collective-permute-start.4 = (bf16[528,128]{1,0:T(8,128)(2,1)S(1)}, bf16[528,128]{1,0:T(8,128)(2,1)S(1)}, u32[]{:S(2)}, u32[]{:S(2)}) collective-permute-start(bf16[528,128]{1,0:T(8,128)(2,1)S(1)} %get-tuple-element.145), channel_id=1, source_target_pairs={{0,6},{1,7},{2,4},{3,5},{4,2},{5,3},{6,0},{7,1},{8,14},{9,15},{10,... | collective-permute-start | bytes 405512 | tf_op jit(solution)/shard_map/ppermute | solution.py:367
  14.0 6.9 %collective-permute-start.7 = (bf16[528,128]{1,0:T(8,128)(2,1)S(1)}, bf16[528,128]{1,0:T(8,128)(2,1)S(1)}, u32[]{:S(2)}, u32[]{:S(2)}) collective-permute-start(bf16[528,128]{1,0:T(8,128)(2,1)S(1)} %get-tuple-element.153), channel_id=1, source_target_pairs={{0,6},{1,7},{2,4},{3,5},{4,2},{5,3},{6,0},{7,1},{8,14},{9,15},{10,... | collective-permute-start | bytes 405512 | tf_op jit(solution)/shard_map/ppermute | solution.py:367
  16.7 6.4 %collective-permute-start.6 = (bf16[528,128]{1,0:T(8,128)(2,1)S(1)}, bf16[528,128]{1,0:T(8,128)(2,1)S(1)}, u32[]{:S(2)}, u32[]{:S(2)}) collective-permute-start(bf16[528,128]{1,0:T(8,128)(2,1)S(1)} %get-tuple-element.162), channel_id=1, source_target_pairs={{0,8},{1,9},{2,10},{3,11},{4,12},{5,13},{6,14},{7,15},{8,0},{9,1},... | collective-permute-start | bytes 405512 | tf_op jit(solution)/shard_map/ppermute | solution.py:367
  21.0 5.2 %collective-permute-start.9 = (bf16[528,128]{1,0:T(8,128)(2,1)S(1)}, bf16[528,128]{1,0:T(8,128)(2,1)S(1)}, u32[]{:S(2)}, u32[]{:S(2)}) collective-permute-start(bf16[528,128]{1,0:T(8,128)(2,1)S(1)} %get-tuple-element.172), channel_id=1, source_target_pairs={{0,8},{1,9},{2,10},{3,11},{4,12},{5,13},{6,14},{7,15},{8,0},{9,1},... | collective-permute-start | bytes 405512 | tf_op jit(solution)/shard_map/ppermute | solution.py:367
  23.2 6.8 %collective-permute-start.8 = (bf16[528,128]{1,0:T(8,128)(2,1)S(1)}, bf16[528,128]{1,0:T(8,128)(2,1)S(1)}, u32[]{:S(2)}, u32[]{:S(2)}) collective-permute-start(bf16[528,128]{1,0:T(8,128)(2,1)S(1)} %merge.14), channel_id=1, source_target_pairs={{0,24},{1,25},{2,26},{3,27},{4,28},{5,29},{6,30},{7,31},{8,16},{9,... | collective-permute-start | bytes 405512 | tf_op jit(solution)/shard_map/ppermute | solution.py:367
  26.4 7.3 %collective-permute-start.10 = (bf16[528,128]{1,0:T(8,128)(2,1)S(1)}, bf16[528,128]{1,0:T(8,128)(2,1)S(1)}, u32[]{:S(2)}, u32[]{:S(2)}) collective-permute-start(bf16[528,128]{1,0:T(8,128)(2,1)S(1)} %merge.15), channel_id=1, source_target_pairs={{0,24},{1,25},{2,26},{3,27},{4,28},{5,29},{6,30},{7,31},{8,16},{9,... | collective-permute-start | bytes 405512 | tf_op jit(solution)/shard_map/ppermute | solution.py:367
  30.3 4.2 %collective-permute-start.12 = (bf16[256,512]{1,0:T(8,128)(2,1)S(1)}, bf16[256,512]{1,0:T(8,128)(2,1)S(1)}, u32[]{:S(2)}, u32[]{:S(2)}) collective-permute-start(bf16[256,512]{1,0:T(8,128)(2,1)S(1)} %last.4), channel_id=1, source_target_pairs={{0,1},{1,0},{2,3},{3,2},{4,5},{5,4},{6,7},{7,6},{8,9},{9,8},{10,11... | collective-permute-start | bytes 786440 | tf_op jit(solution)/shard_map/ppermute | solution.py:367
  33.9 1.6 %collective-permute-start.11 = (bf16[256,512]{1,0:T(8,128)(2,1)S(1)}, bf16[256,512]{1,0:T(8,128)(2,1)S(1)}, u32[]{:S(2)}, u32[]{:S(2)}) collective-permute-start(bf16[256,512]{1,0:T(8,128)(2,1)S(1)} %last.6), channel_id=1, source_target_pairs={{0,1},{1,0},{2,3},{3,2},{4,5},{5,4},{6,7},{7,6},{8,9},{9,8},{10,11... | collective-permute-start | bytes 786440 | tf_op jit(solution)/shard_map/ppermute | solution.py:367
